TPU v7x, 256 devices: a whole 4x4x8 slice. The times are simulated.
256 devices in a mesh: group: 8 (over z), seq: 2 (over core), req: 16 (over y, x).
Axes of the slice: x: 4, y: 4, z: 8, core: 2. Of those that a mesh axis runs over, the one named last changes fastest.
Arguments:
- queries: bfloat16 [2, 128, 4, 128, 192], P(None, ('group', 'req')), may hold values from -8 to 8
- w_absorb_k: bfloat16 [2, 128, 128, 512], P(None, 'req', None, 'seq'), may hold values from -0.5 to 0.5
- w_absorb_v: bfloat16 [2, 128, 512, 128], P(None, 'req', 'seq'), may hold values from -1.1953125 to 1.1953125
- prefill_pages: bfloat16 [16, 16, 2, 16, 64, 576], P(('group', 'seq'), 'req'), may hold values from -8 to 8
- send_to: int32 [16, 16, 16], P(('group', 'seq'), 'req'), may hold values from 0 to 15, each once within a row
- slot_of: int32 [16, 16, 16], P(('group', 'seq'), 'req'), may hold values from 0 to 15, each once within a row
- lengths: int32 [128], P(('group', 'req')), may hold values from 1 to 2048, 131072 in all
- new_latents: bfloat16 [2, 128, 4, 576], P(None, ('group', 'req')), may hold values from -6 to 6
Outputs:
- attn_out: bfloat16 [2, 128, 4, 128, 128], P(None, 'group', None, 'req')
Inputs may be any that keep to these rules, and one draw needn't show every extreme that they name: For each prefill device and request column (r), send_to is a permutation of the 16 holders of that column (numbered group-major): each prefill device holds exactly one page for each holder. For each holder and request column (r), slot_of is a permutation: the page from prefill device p fills page slot slot_of[p] of the holder's block.
All inputs are finite; a program needn't handle non-finite values. No bound on the sum of `lengths` on one device may be relied on, other than what follows from the above.
Results may differ from a plain program's by a relative error of at most 0.0075.
Values may be sent and summed in bfloat16 or wider, within the bound.
No kernel may reach another device: no remote copies, remote signals or barrier semaphores. Data moves between devices by JAX's collectives and lax.ppermute only.
A program may use at most 192 MiB of HBM per device.

v0:
```python
import math

import jax
import jax.numpy as jnp
from jax import lax
from jax.sharding import PartitionSpec as P

KV_RANK = 512
ROPE = 64
NOPE = 128


empty_score = -1e30


def combined_all(value, axis, join):
    pieces = jax.tree.map(lambda part: lax.all_gather(part, axis), value)
    head = jax.tree.map(lambda part: part[0], pieces)
    tail = jax.tree.map(lambda part: part[1:], pieces)
    total, _ = lax.scan(lambda total, section: (join(total, section), None), head, tail)
    return total


def combine_parts(first, second):
    peak = jnp.maximum(first[0], second[0])
    first_factor = jnp.exp(first[0] - peak)
    second_factor = jnp.exp(second[0] - peak)
    total = first[1] * first_factor + second[1] * second_factor
    summed = first[2] * first_factor[..., None] + second[2] * second_factor[..., None]
    return (peak, total, summed)


def block_part(flat_query, cache_keys, new_keys, holder, length, heads):
    scale = 1.0 / math.sqrt(NOPE + ROPE)
    row_count = flat_query.shape[0]
    step_count = new_keys.shape[0]
    contract = (((1,), (1,)), ((), ()))
    scores = (
        lax.dot_general(flat_query, cache_keys, contract, preferred_element_type=jnp.float32)
        * scale
    )
    new_scores = (
        lax.dot_general(flat_query, new_keys, contract, preferred_element_type=jnp.float32) * scale
    )
    positions = holder * cache_keys.shape[0] + jnp.arange(cache_keys.shape[0], dtype=jnp.int32)
    cache_live = (positions < length)[None, :]
    row_step = jnp.arange(row_count, dtype=jnp.int32) // heads
    new_live = (jnp.arange(step_count, dtype=jnp.int32)[None, :] <= row_step[:, None]) & (
        holder == 0
    )
    cache_peak = jnp.max(jnp.where(cache_live, scores, empty_score), axis=1)
    new_peak = jnp.max(jnp.where(new_live, new_scores, empty_score), axis=1)
    peak = jnp.maximum(cache_peak, new_peak)
    weights = jnp.where(cache_live, jnp.exp(scores - peak[:, None]), 0.0).astype(jnp.bfloat16)
    new_weights = jnp.where(new_live, jnp.exp(new_scores - peak[:, None]), 0.0).astype(jnp.bfloat16)
    total = jnp.sum(weights, axis=1, dtype=jnp.float32) + jnp.sum(
        new_weights, axis=1, dtype=jnp.float32
    )
    summed = jnp.dot(weights, cache_keys[:, :KV_RANK], preferred_element_type=jnp.float32)
    summed = summed + jnp.dot(
        new_weights, new_keys[:, :KV_RANK], preferred_element_type=jnp.float32
    )
    return (peak, total, summed)


def shards(queries, w_absorb_k, w_absorb_v, prefill_pages, send_to, slot_of, lengths, new_latents):
    layers = queries.shape[0]
    steps = queries.shape[2]
    heads = queries.shape[3]
    holder = lax.axis_index("seq")
    length = lengths[0]
    seq_count = lax.axis_size("seq")
    page_group = prefill_pages[0, 0]
    outgoing = jnp.take(page_group, jnp.argsort(send_to[0, 0]), axis=1)
    incoming = lax.all_to_all(outgoing, ("group", "seq"), split_axis=1, concat_axis=1, tiled=True)
    placed = jnp.take(incoming, jnp.argsort(slot_of[0, 0]), axis=1)
    caches = placed.reshape(layers, page_group.shape[1] * page_group.shape[2], page_group.shape[3])
    query_heads = lax.all_to_all(queries, "req", split_axis=3, concat_axis=1, tiled=True)
    latent_part = jnp.einsum(
        "lrthd,lhdc->lrthc", query_heads[..., :NOPE], w_absorb_k, preferred_element_type=jnp.float32
    ).astype(jnp.bfloat16)
    latent_cols = lax.all_gather(latent_part, "seq", axis=4, tiled=True)
    latent_query = lax.all_to_all(latent_cols, "req", split_axis=1, concat_axis=3, tiled=True)
    full_query = jnp.concatenate([latent_query[:, 0], queries[:, 0, :, :, NOPE:]], axis=-1)
    row_count = steps * heads
    peak_list = []
    total_list = []
    summed_list = []
    for layer_index in range(layers):
        flat_query = full_query[layer_index].reshape(row_count, full_query.shape[-1])
        cache_keys = caches[layer_index]
        new_keys = new_latents[layer_index, 0]
        block_result = block_part(flat_query, cache_keys, new_keys, holder, length, heads)
        peak_list.append(block_result[0].reshape(steps, heads))
        total_list.append(block_result[1].reshape(steps, heads))
        summed_list.append(block_result[2].reshape(steps, heads, KV_RANK))
    peaks = jnp.stack(peak_list)
    totals = jnp.stack(total_list)
    sums = jnp.stack(summed_list)
    merged = combined_all((peaks, totals, sums), "seq", combine_parts)
    latent_full = merged[2] / merged[1][..., None]
    column_width = KV_RANK // seq_count
    latent_out = lax.dynamic_slice_in_dim(
        latent_full, holder * column_width, column_width, 3
    ).astype(jnp.bfloat16)
    latent_heads = lax.all_to_all(
        latent_out[:, None], "req", split_axis=3, concat_axis=1, tiled=True
    )
    head_part = jnp.einsum(
        "lrthc,lhcv->lrthv", latent_heads, w_absorb_v, preferred_element_type=jnp.float32
    )
    return lax.psum(head_part, "seq").astype(jnp.bfloat16)


def solution(mesh):
    in_specs = (
        P(None, ("group", "req"), None, None, None),
        P(None, "req", None, "seq"),
        P(None, "req", "seq", None),
        P(("group", "seq"), "req", None, None, None, None),
        P(("group", "seq"), "req", None),
        P(("group", "seq"), "req", None),
        P(("group", "req")),
        P(None, ("group", "req"), None, None),
    )
    out_specs = P(None, "group", None, "req", None)
    return jax.shard_map(shards, mesh=mesh, in_specs=in_specs, out_specs=out_specs, check_vma=False)
```

profile of v0, /device:TPU:1, one launch (start us, length us, event | category | flops | bytes accessed | tf_op | source)
XLA Modules:
  0.0 202.5 jit_solution(1582897406503274032)
XLA Ops:
  6.5 1.6 copy.17
  8.1 18.0 %all_to_all.56 = bf16[2,1,4,128,192]{4,2,0,1,3:T(4,128)(2,1)S(1)} all-to-all(bf16[2,1,4,128,192]{4,2,0,1,3:T(4,128)(2,1)S(1)} %copy.17), channel_id=1, replica_groups=mesh['group'=8,'seq'=2,'req'=16] {'req'}, dimensions={3} | all-to-all | bytes 786432 | tf_op jit(solution)/shard_map/all_to_all | solution.py:78
  26.5 1.1 fusion
  27.6 15.6 %all-gather.6.cloned.1.call-done = bf16[2,16,4,8,512]{4,1,2,3,0:T(8,128)(2,1)} async-done(((bf16[2,16,4,8,256]{4,1,2,3,0:T(8,128)(2,1)}), bf16[2,16,4,8,512]{4,1,2,3,0:T(8,128)(2,1)}) %all-gather.6.cloned.1.call-update) | async-done | bytes 1048592 | tf_op jit(solution)/shard_map/all_gather | solution.py:82
  43.2 3.0 %copy.20 = bf16[2,16,4,8,512]{4,2,3,0,1:T(4,128)(2,1)} copy(bf16[2,16,4,8,512]{4,1,2,3,0:T(8,128)(2,1)} %all-gather.6.cloned.1.call-done) | data formatting | bytes 2097152 | tf_op jit(solution)/shard_map/all_gather | solution.py:82
  46.2 6.3 %all-to-all-start.1 = ((bf16[2,16,4,8,512]{4,2,3,0,1:T(4,128)(2,1)}), bf16[2,16,4,8,512]{4,2,3,0,1:T(4,128)(2,1)}, u32[]{:S(2)}, u32[]{:S(2)}) async-start(bf16[2,16,4,8,512]{4,2,3,0,1:T(4,128)(2,1)} %copy.20), calls=%async_computation.1 | async-start | bytes 2097152 | tf_op jit(solution)/shard_map/all_to_all | solution.py:83
  52.5 1.2 sort.31
  53.8 2.4 %gather_fusion = bf16[16,2,64,576]{3,2,1,0:T(8,128)(2,1)} fusion(bf16[2,16,64,576]{3,2,1,0:T(8,128)(2,1)S(1)} %bitcast.73, s32[1024]{0:T(1024)S(1)} %pad_clamp_fusion.1), kind=kCustom, calls=%fused_computation.clone | custom fusion | bytes 4718656 | tf_op jit(solution)/shard_map/jit(_take)/gather | solution.py:74
  56.2 3.6 %select_bitcast_fusion.1 = bf16[2,16,64,576]{3,2,0,1:T(8,128)(2,1)} fusion(bf16[16,2,64,576]{3,2,1,0:T(8,128)(2,1)} %gather_fusion, pred[16]{0:T(512)(128)(4,1)S(1)} %compare_and_fusion.1), kind=kLoop, calls=%fused_computation.3 | loop fusion | flops 1179648 | bytes 4718608 | tf_op jit(solution)/shard_map/jit(_take)/select_n | solution.py:74
  59.8 9.3 %all-to-all-done.1 = bf16[2,16,4,8,512]{4,2,3,0,1:T(4,128)(2,1)} async-done(((bf16[2,16,4,8,512]{4,2,3,0,1:T(4,128)(2,1)}), bf16[2,16,4,8,512]{4,2,3,0,1:T(4,128)(2,1)}, u32[]{:S(2)}, u32[]{:S(2)}) %all-to-all-start.1) | async-done | bytes 1048608 | tf_op jit(solution)/shard_map/all_to_all | solution.py:83
  69.1 8.9 %all-to-all-start.2 = ((bf16[2,16,64,576]{3,2,0,1:T(8,128)(2,1)}), bf16[2,16,64,576]{3,2,0,1:T(8,128)(2,1)}, u32[]{:S(2)}, u32[]{:S(2)}) async-start(bf16[2,16,64,576]{3,2,0,1:T(8,128)(2,1)} %select_bitcast_fusion.1), calls=%async_computation.2 | async-start | bytes 5242880 | tf_op jit(solution)/shard_map/all_to_all | solution.py:75
  78.9 1.3 sort.32
  80.7 0.6 pad_clamp_fusion
  81.9 0.6 slice_bitcast_fusion.1
  82.5 1.4 copy.40
  84.0 0.8 copy-done.2
  85.2 52.7 %all-to-all-done.2 = bf16[2,16,64,576]{3,2,0,1:T(8,128)(2,1)} async-done(((bf16[2,16,64,576]{3,2,0,1:T(8,128)(2,1)}), bf16[2,16,64,576]{3,2,0,1:T(8,128)(2,1)}, u32[]{:S(2)}, u32[]{:S(2)}) %all-to-all-start.2) | async-done | bytes 2359328 | tf_op jit(solution)/shard_map/all_to_all | solution.py:75
  137.9 4.3 %gather_fusion.1 = bf16[16,2,64,576]{3,2,1,0:T(8,128)(2,1)} fusion(bf16[2,16,64,576]{3,2,0,1:T(8,128)(2,1)} %all-to-all-done.2, s32[1024]{0:T(1024)} %pad_clamp_fusion), kind=kCustom, calls=%fused_computation.1.clone | custom fusion | bytes 4718656 | tf_op jit(solution)/shard_map/jit(_take)/gather | solution.py:76
  142.2 2.1 %select_bitcast_fusion = bf16[2,16,64,576]{3,2,0,1:T(8,128)(2,1)S(1)} fusion(bf16[16,2,64,576]{3,2,1,0:T(8,128)(2,1)} %gather_fusion.1, pred[16]{0:T(512)(128)(4,1)S(1)} %copy-done.10), kind=kLoop, calls=%fused_computation.2 | loop fusion | flops 1179648 | bytes 4718608 | tf_op jit(solution)/shard_map/jit(_take)/select_n | solution.py:76
  144.5 1.0 fusion.30
  145.6 1.3 select_reduce_fusion.1
  147.2 0.8 fusion.5
  148.2 0.8 fusion.3
  150.1 1.6 pad_maximum_fusion
  151.7 2.4 %all-gather.1 = f32[4,4,128]{2,1,0:T(4,128)S(1)} all-gather(f32[2,4,128]{2,1,0:T(4,128)S(1)} %pad_maximum_fusion.2), channel_id=3, replica_groups=mesh['group'=8,'seq'=2,'req'=16] {'seq'}, dimensions={0}, use_global_device_ids=true | all-gather | bytes 12288 | tf_op jit(solution)/shard_map/all_gather | solution.py:17
  154.1 3.2 %convert_reduce_fusion.1 = (f32[512]{0:T(512)S(1)}, f32[512]{0:T(512)S(1)}) fusion(f32[512]{0:T(512)S(1)} %max.48, f32[512,1024]{1,0:T(8,128)} %copy-done.4, pred[1024]{0:T(1024)(128)(4,1)S(1)} %copy-done.9, f32[512]{0:T(512)S(1)} %max.49, f32[512,1024]{1,0:T(8,128)} %copy-done.1), kind=kLoop, calls=%fused_computation.6 | loop fusion | flops 6290432 | bytes 4203520 | tf_op jit(solution)/shard_map/reduce_sum | solution.py:56
  157.4 2.0 all-gather.2
  159.4 7.7 %all-gather.8.cloned.1.call-done = f32[4,4,128,512]{3,2,1,0:T(8,128)} async-done(((f32[2,4,128,512]{3,2,1,0:T(8,128)}), f32[4,4,128,512]{3,2,1,0:T(8,128)}) %all-gather.8.cloned.1.call-update) | async-done | bytes 4194320 | tf_op jit(solution)/shard_map/all_gather | solution.py:17
  167.1 2.9 %fusion.28 = (f32[2,4,128,512]{3,2,1,0:T(8,128)S(1)}, f32[2,4,128,512]{3,2,1,0:T(8,128)S(1)}) fusion(f32[4,4,128,512]{3,2,1,0:T(8,128)} %all-gather.8.cloned.1.call-done), kind=kLoop, calls=%fused_computation.76 | loop fusion | bytes 8388608 | tf_op jit(solution)/shard_map/slice | solution.py:18
  171.0 16.9 %all_to_all.57 = bf16[2,1,4,128,256]{4,2,0,1,3:T(4,128)(2,1)S(1)} all-to-all(bf16[2,1,4,128,256]{4,2,0,1,3:T(4,128)(2,1)S(1)} %copy.23), channel_id=1, replica_groups=mesh['group'=8,'seq'=2,'req'=16] {'req'}, dimensions={3} | all-to-all | bytes 1048576 | tf_op jit(solution)/shard_map/all_to_all | solution.py:106
  188.4 6.3 %all-reduce.1 = bf16[2,16,4,8,128]{4,1,2,3,0:T(8,128)(2,1)S(1)} all-reduce(f32[2,16,4,8,128]{4,1,2,3,0:T(8,128)S(1)} %convolution_bitcast_fusion), channel_id=1, replica_groups=mesh['group'=8,'seq'=2,'req'=16] {'seq'}, use_global_device_ids=true, to_apply=%region_10.12 | all-reduce | flops 131072 | bytes 786432 | tf_op jit(solution)/shard_map/psum | solution.py:112
  194.7 0.9 copy.26
  (61 shorter events, 5.4 us)
Async XLA Ops:
  6.5 47.3 %copy-start = (bf16[1,1,2,16,64,576]{5,4,3,2,1,0:T(8,128)(2,1)S(1)}, bf16[1,1,2,16,64,576]{5,4,3,2,1,0:T(8,128)(2,1)}, u32[]{:S(2)}) copy-start(bf16[1,1,2,16,64,576]{5,4,3,2,1,0:T(8,128)(2,1)} %param.13) | copy-start | bytes 7077892
  6.5 36.6 %all-gather.6.cloned.1.call-start = ((), (), s32[]{:S(2)}) async-start(), calls=%async_computation.4 | async-start | bytes 1572864 | tf_op jit(solution)/shard_map/all_gather | solution.py:82
  8.1 18.3 %copy-start.11 = (bf16[2,8,128,256]{3,2,1,0:T(8,128)(2,1)S(1)}, bf16[2,8,128,256]{3,2,1,0:T(8,128)(2,1)}, u32[]{:S(2)}) copy-start(bf16[2,8,128,256]{3,2,1,0:T(8,128)(2,1)} %param.11) | copy-start | bytes 3145732
  27.6 25.0 %copy-start.12 = (s32[1,1,16]{2,1,0:T(1,128)S(1)}, s32[1,1,16]{2,1,0:T(1,128)}, u32[]{:S(2)}) copy-start(s32[1,1,16]{2,1,0:T(1,128)} %param.14) | copy-start | bytes 196
  46.2 22.9 %all-to-all-start.1 = ((bf16[2,16,4,8,512]{4,2,3,0,1:T(4,128)(2,1)}), bf16[2,16,4,8,512]{4,2,3,0,1:T(4,128)(2,1)}, u32[]{:S(2)}, u32[]{:S(2)}) async-start(bf16[2,16,4,8,512]{4,2,3,0,1:T(4,128)(2,1)} %copy.20), calls=%async_computation.1 | async-start | bytes 2097152 | tf_op jit(solution)/shard_map/all_to_all | solution.py:83
  59.8 18.9 %slice-start = ((bf16[2,1,4,128,192]{3,4,2,1,0:T(8,128)(2,1)}), bf16[2,1,4,128,64]{3,4,2,1,0:T(8,128)(2,1)S(1)}, s32[]{:S(2)}) async-start(bf16[2,1,4,128,192]{3,4,2,1,0:T(8,128)(2,1)} %param.10), calls=%async_computation.6 | async-start | bytes 262144 | tf_op jit(solution)/shard_map/slice | solution.py:84
  59.8 19.1 %copy-start.13 = (s32[1,1,16]{2,1,0:T(1,128)S(1)}, s32[1,1,16]{2,1,0:T(1,128)}, u32[]{:S(2)}) copy-start(s32[1,1,16]{2,1,0:T(1,128)} %param.15) | copy-start | bytes 196
  59.8 22.0 %copy-start.6 = (bf16[2,1,4,576]{3,2,1,0:T(4,128)(2,1)S(1)}, bf16[2,1,4,576]{3,2,1,0:T(4,128)(2,1)}, u32[]{:S(2)}) copy-start(bf16[2,1,4,576]{3,2,1,0:T(4,128)(2,1)} %param.17) | copy-start | bytes 27652
  69.1 68.8 %all-to-all-start.2 = ((bf16[2,16,64,576]{3,2,0,1:T(8,128)(2,1)}), bf16[2,16,64,576]{3,2,0,1:T(8,128)(2,1)}, u32[]{:S(2)}, u32[]{:S(2)}) async-start(bf16[2,16,64,576]{3,2,0,1:T(8,128)(2,1)} %select_bitcast_fusion.1), calls=%async_computation.2 | async-start | bytes 5242880 | tf_op jit(solution)/shard_map/all_to_all | solution.py:75
  78.0 89.1 %all-gather.8.cloned.1.call-start = ((), (), s32[]{:S(2)}) async-start(), calls=%async_computation.5 | async-start | bytes 6291456 | tf_op jit(solution)/shard_map/all_gather | solution.py:17
  84.0 0.9 copy-start.2
  85.2 57.0 %copy-start.10 = (pred[16]{0:T(512)(128)(4,1)S(1)}, pred[16]{0:T(512)(128)(4,1)}, u32[]{:S(2)}) copy-start(pred[16]{0:T(512)(128)(4,1)} %compare_and_fusion) | copy-start | bytes 52
  144.5 1.1 copy-start.3
  144.5 1.1 copy-start.9
  145.6 2.7 %copy-start.1 = (f32[512,1024]{1,0:T(8,128)}, f32[512,1024]{1,0:T(8,128)S(1)}, u32[]{:S(2)}) copy-start(f32[512,1024]{1,0:T(8,128)S(1)} %fusion.30) | copy-start | bytes 6291460
  146.9 1.3 copy-start.4
  148.2 0.8 copy-start.8
  149.0 0.7 copy-start.7
  170.1 17.8 %copy-start.5 = (bf16[2,8,256,128]{3,2,1,0:T(8,128)(2,1)S(1)}, bf16[2,8,256,128]{3,2,1,0:T(8,128)(2,1)}, u32[]{:S(2)}) copy-start(bf16[2,8,256,128]{3,2,1,0:T(8,128)(2,1)} %param.12) | copy-start | bytes 3145732
Sparse Core Ops, SparseCore 0:
  27.7 15.4 all-gather.5
  151.9 15.2 all-gather.7
where the time goes:
time: 203 us; the launch traced here: 202 us
  waiting for transfers between devices  85.3 us (42%)
  blocking collectives  45.6 us (22%)
  local copies, waits for them, and re-layouts  19.7 us (10%)
  other arithmetic  15.4 us (8%)
  starting transfers between devices  15.3 us (8%)
  between operations  14.4 us (7%)
  matrix products  6.77 us (3%)
    all_to_all x1, waiting for transfers between devices, shards(): lax.all_to_all(outgoing, ('group', 'seq'), split_axis=1, concat_axis=1, t...  52.7 us
    all_to_all x1, blocking collectives, shards(): lax.all_to_all(queries, 'req', split_axis=3, concat_axis=1, tiled=True)  18 us
    all_to_all x1, blocking collectives, shards(): lax.all_to_all(latent_out[:, None], 'req', split_axis=3, concat_axis=1, t...  16.9 us
    all_gather x1, waiting for transfers between devices, shards(): latent_cols = lax.all_gather(latent_part, 'seq', axis=4, tiled=True)  15.6 us
    all_to_all x1, waiting for transfers between devices, shards(): lax.all_to_all(latent_cols, 'req', split_axis=1, concat_axis=3, tiled=True)  9.25 us
    all_to_all x1, starting transfers between devices, shards(): lax.all_to_all(outgoing, ('group', 'seq'), split_axis=1, concat_axis=1, t...  8.93 us
    all_gather x1, waiting for transfers between devices, combined_all(): pieces = jax.tree.map(lambda part: lax.all_gather(part, axis), value)  7.73 us
    psum x1, blocking collectives, shards(): return lax.psum(head_part, 'seq').astype(jnp.bfloat16)  6.32 us
  transfers between devices with their start and end apart: 4, of which 4 were waited for; matrix products, arithmetic and copies ran while one was open for 8% of the time, Pallas kernels for 0%

commit v1 on v0

v1 whole, which is shorter than its diff:
```python
import math

import jax
import jax.numpy as jnp
from jax import lax
from jax.experimental import pallas as pl
from jax.experimental.pallas import tpu as pltpu
from jax.sharding import PartitionSpec as P

KV_RANK = 512
ROPE = 64
NOPE = 128
HEADS_PER = 8
STEPS = 4
PAGE = 64
SIDE = 4
SRC = 16
PAIR_ROWS = 2 * PAGE + 16
DEAD = -1e30
SCALE = 1.0 / math.sqrt(NOPE + ROPE)


def send_kernel(page_of, pages, out, held, packed, in_sem, lat_sem, rope_sem):
    def fetch(dest, half):
        chip, layer = dest // 2, dest % 2
        index = dest * 2 + half
        return pltpu.make_async_copy(
            pages.at[layer, page_of[chip * 2 + half]], held.at[index], in_sem.at[index]
        )

    def latents(dest, half):
        index = dest * 2 + half
        return pltpu.make_async_copy(
            held.at[index, :, pl.ds(0, KV_RANK)],
            out.at[dest, pl.ds(half * PAGE, PAGE)],
            lat_sem.at[index],
        )

    def ropes(dest):
        return pltpu.make_async_copy(
            packed.at[dest], out.at[dest, pl.ds(2 * PAGE, 16)], rope_sem.at[dest]
        )

    for dest in range(SRC):
        for half in range(2):
            fetch(dest, half).start()
    for dest in range(SRC):
        for half in range(2):
            fetch(dest, half).wait()
            latents(dest, half).start()
        groups = [
            held[dest * 2 + half, 16 * k : 16 * k + 16, KV_RANK:]
            for half in range(2)
            for k in range(PAGE // 16)
        ]
        packed[dest] = jnp.concatenate(groups, axis=1)
        ropes(dest).start()
    for dest in range(SRC):
        for half in range(2):
            latents(dest, half).wait()
        ropes(dest).wait()


def gather_pages(page_of, pages):
    return pl.pallas_call(
        send_kernel,
        out_shape=jax.ShapeDtypeStruct((SRC, PAIR_ROWS, KV_RANK), jnp.bfloat16),
        in_specs=[
            pl.BlockSpec(memory_space=pltpu.SMEM),
            pl.BlockSpec(memory_space=pl.ANY),
        ],
        out_specs=pl.BlockSpec(memory_space=pl.ANY),
        scratch_shapes=[
            pltpu.VMEM((2 * SRC, PAGE, KV_RANK + ROPE), jnp.bfloat16),
            pltpu.VMEM((SRC, 16, KV_RANK), jnp.bfloat16),
            pltpu.SemaphoreType.DMA((2 * SRC,)),
            pltpu.SemaphoreType.DMA((2 * SRC,)),
            pltpu.SemaphoreType.DMA((SRC,)),
        ],
        compiler_params=pltpu.CompilerParams(vmem_limit_bytes=24 << 20),
        cost_estimate=pl.CostEstimate(flops=0, bytes_accessed=5 << 20, transcendentals=0),
    )(page_of, pages)


def attend_kernel(order, q_lat, q_rope, pages, bias, new_lat, new_rope, out, ropes, scores):
    contract = (((1,), (1,)), ((), ()))

    def dot(a, b):
        return lax.dot_general(a, b, contract, preferred_element_type=jnp.float32)

    rows = q_lat.shape[0]
    for p in range(SRC):
        for k in range(8):
            ropes[p * 128 + 16 * k : p * 128 + 16 * k + 16, :] = pages[
                p, 2 * PAGE : PAIR_ROWS, ROPE * k : ROPE * k + ROPE
            ]
    ql, qr = q_lat[...], q_rope[...]
    step = lax.rem(lax.broadcasted_iota(jnp.int32, (rows, 16), 0) // HEADS_PER, STEPS)
    key = lax.broadcasted_iota(jnp.int32, (rows, 16), 1)
    fresh = (dot(ql, new_lat[...]) + dot(qr, new_rope[...])) * SCALE
    fresh = jnp.where(key <= step, fresh, DEAD)
    peak = jnp.max(fresh, axis=1, keepdims=True)
    chunk = 256
    for n in range(SRC // 2):
        part = slice(n * chunk, (n + 1) * chunk)
        lat = pages[2 * n : 2 * n + 2, : 2 * PAGE, :].reshape(chunk, KV_RANK)
        s = (dot(ql, lat) + dot(qr, ropes[part, :])) * SCALE
        s = jnp.where(bias[:, part] > 0.0, s, DEAD)
        scores[:, part] = s
        peak = jnp.maximum(peak, jnp.max(s, axis=1, keepdims=True))
    weight = jnp.exp(fresh - peak).astype(jnp.bfloat16)
    total = jnp.sum(weight.astype(jnp.float32), axis=1, keepdims=True)
    summed = jnp.dot(weight, new_lat[...], preferred_element_type=jnp.float32)
    for n in range(SRC // 2):
        part = slice(n * chunk, (n + 1) * chunk)
        lat = pages[2 * n : 2 * n + 2, : 2 * PAGE, :].reshape(chunk, KV_RANK)
        weight = jnp.exp(scores[:, part] - peak).astype(jnp.bfloat16)
        total = total + jnp.sum(weight.astype(jnp.float32), axis=1, keepdims=True)
        summed = summed + jnp.dot(weight, lat, preferred_element_type=jnp.float32)
    result = (summed / total).astype(jnp.bfloat16)
    block = HEADS_PER * STEPS
    for j in range(SRC):
        out[order[j]] = result[j * block : (j + 1) * block]


def attend(order, q_lat, q_rope, pages, bias, new_lat, new_rope):
    block = HEADS_PER * STEPS
    vmem = pl.BlockSpec(memory_space=pltpu.VMEM)
    rows = q_lat.shape[0]
    return pl.pallas_call(
        attend_kernel,
        out_shape=jax.ShapeDtypeStruct((SRC, block, KV_RANK), jnp.bfloat16),
        in_specs=[pl.BlockSpec(memory_space=pltpu.SMEM)] + [vmem] * 6,
        out_specs=vmem,
        scratch_shapes=[
            pltpu.VMEM((SRC * 2 * PAGE, ROPE), jnp.bfloat16),
            pltpu.VMEM((rows, SRC * 2 * PAGE), jnp.float32),
        ],
        compiler_params=pltpu.CompilerParams(vmem_limit_bytes=40 << 20),
        cost_estimate=pl.CostEstimate(
            flops=2 * rows * 2048 * 1088, bytes_accessed=4 << 20, transcendentals=rows * 2048
        ),
    )(order, q_lat, q_rope, pages, bias, new_lat, new_rope)


def shifted(value, dy, dx):
    pairs = [
        (y * SIDE + x, ((y + dy) % SIDE) * SIDE + (x + dx) % SIDE)
        for y in range(SIDE)
        for x in range(SIDE)
    ]
    return lax.ppermute(value, "req", pairs)


def exchange(value):
    columns = [value[:, 0]] + [shifted(value[:, d], 0, d) for d in range(1, SIDE)]
    rows = jnp.stack(columns, axis=1)
    return jnp.stack([rows[0]] + [shifted(rows[d], d, 0) for d in range(1, SIDE)])


def swapped(value):
    return lax.ppermute(value, "seq", [(0, 1), (1, 0)])


def pick(value, index):
    return lax.dynamic_index_in_dim(value, index, 0, keepdims=False)


def shards(queries, w_absorb_k, w_absorb_v, prefill_pages, send_to, slot_of, lengths, new_latents):
    layer = lax.axis_index("seq")
    place = lax.axis_index("req")
    py, px = place // SIDE, place % SIDE
    length = lengths[0]
    numbers = jnp.arange(SRC, dtype=jnp.int32)

    page_of = jnp.sum(
        jnp.where(send_to[0, 0][None, :] == numbers[:, None], numbers[None, :], 0), axis=1
    )
    sent = gather_pages(page_of, prefill_pages[0, 0])
    pages = lax.all_to_all(sent, ("group", "seq"), split_axis=0, concat_axis=0, tiled=True)

    forward = ((py + numbers // SIDE) % SIDE) * SIDE + (px + numbers % SIDE) % SIDE
    backward = ((py - numbers // SIDE) % SIDE) * SIDE + (px - numbers % SIDE) % SIDE

    own_k, other_k = pick(w_absorb_k, layer), swapped(pick(w_absorb_k, 1 - layer))
    weight_k = jnp.where(
        layer == 0,
        jnp.concatenate([own_k, other_k], axis=2),
        jnp.concatenate([other_k, own_k], axis=2),
    )
    own_v, other_v = pick(w_absorb_v, layer), swapped(pick(w_absorb_v, 1 - layer))
    weight_v = jnp.where(
        layer == 0,
        jnp.concatenate([own_v, other_v], axis=1),
        jnp.concatenate([other_v, own_v], axis=1),
    )

    own = pick(queries, layer)[0].reshape(STEPS, SRC, HEADS_PER, NOPE + ROPE).transpose(1, 0, 2, 3)
    own = jnp.take(own, forward, axis=0, mode="clip")
    grid = (SIDE, SIDE, STEPS, HEADS_PER)
    heads = exchange(own[..., :NOPE].reshape(grid + (NOPE,)))
    latent = jnp.einsum(
        "yxthd,hdc->yxthc", heads, weight_k, preferred_element_type=jnp.float32
    ).astype(jnp.bfloat16)
    turned = (-jnp.arange(SIDE)) % SIDE
    back = exchange(latent[turned][:, turned])[turned][:, turned]
    rows = SRC * STEPS * HEADS_PER
    q_lat = back.reshape(rows, KV_RANK)
    q_rope = own[..., NOPE:].reshape(rows, ROPE)

    other_slot = swapped(slot_of[0, 0])
    slots = jnp.where(
        layer == 0, jnp.stack([slot_of[0, 0], other_slot]), jnp.stack([other_slot, slot_of[0, 0]])
    )
    starts = jnp.arange(2, dtype=jnp.int32)[None, :] * 1024 + slots.T * PAGE
    live = starts[:, :, None] + jnp.arange(PAGE, dtype=jnp.int32) < length
    bias = live.reshape(1, SRC * 2 * PAGE).astype(jnp.float32)
    fresh = jnp.pad(pick(new_latents, layer)[0], ((0, 16 - STEPS), (0, 0)))
    latent_out = attend(
        forward, q_lat, q_rope, pages, bias, fresh[:, :KV_RANK], fresh[:, KV_RANK:]
    )

    latent_heads = lax.all_to_all(latent_out, "req", split_axis=0, concat_axis=0, tiled=True)
    head_out = jnp.einsum(
        "rthc,hcv->rthv",
        latent_heads.reshape(SRC, STEPS, HEADS_PER, KV_RANK),
        weight_v,
        preferred_element_type=jnp.float32,
    ).astype(jnp.bfloat16)
    return lax.all_gather(head_out, "seq", axis=0)


def solution(mesh):
    in_specs = (
        P(None, ("group", "req"), None, None, None),
        P(None, "req", None, "seq"),
        P(None, "req", "seq", None),
        P(("group", "seq"), "req", None, None, None, None),
        P(("group", "seq"), "req", None),
        P(("group", "seq"), "req", None),
        P(("group", "req")),
        P(None, ("group", "req"), None, None),
    )
    out_specs = P(None, "group", None, "req", None)
    return jax.shard_map(shards, mesh=mesh, in_specs=in_specs, out_specs=out_specs, check_vma=False)
```

time: 203 us -> 103 us (0.51)
  waiting for transfers between devices: 85.3 us -> 22.5 us
  blocking collectives: 45.6 us -> 3.61 us
  starting transfers between devices: 15.3 us -> 35.7 us
  between operations: 14.4 us -> 0.97 us
  Pallas kernels: 0 us -> 11.5 us
  other arithmetic: 15.4 us -> 4.08 us
  matrix products: 6.77 us -> 4.33 us
    all_to_all x2, waiting for transfers between devices: 62 us -> 13.8 us  [the longest x1 10.5 us: shards(): lax.all_to_all(latent_out, 'req', split_axis=0, concat_axis=0, tiled=True)]
    all_to_all x2 -> x0, blocking collectives: 34.9 us -> none  [the longest x1 18 us: shards(): lax.all_to_all(queries, 'req', split_axis=3, concat_axis=1, tiled=True)]
    all_gather x2 -> x0, waiting for transfers between devices: 23.3 us -> none  [the longest x1 15.6 us: shards(): latent_cols = lax.all_gather(latent_part, 'seq', axis=4, tiled=True)]
    ppermute x0 -> x15, starting transfers between devices: none -> 18.9 us  [the longest x12 16.5 us: shifted(): return lax.ppermute(value, 'req', pairs)]
    pallas_call x0 -> x2, Pallas kernels: none -> 11.5 us  [the longest x1 6.59 us: gather_pages(): pl.pallas_call(send_kernel, out_shape=jax.ShapeDtypeStruct((SRC, PAIR_ROW...]
    ppermute x0 -> x15, waiting for transfers between devices: none -> 8.66 us  [the longest x12 8.66 us: shifted(): return lax.ppermute(value, 'req', pairs)]
    psum x1 -> x0, blocking collectives: 6.32 us -> none  [shards(): return lax.psum(head_part, 'seq').astype(jnp.bfloat16)]
    select_n x5 -> x1, other arithmetic: 5.69 us -> 0.01 us  [shards(): back = exchange(latent[turned][:, turned])[turned][:, turned]]
  transfers between devices with their start and end apart: 4 -> 17, of which waited for: 4 -> 6; matrix products, arithmetic and copies ran while one was open for 8% -> 21% of each run, Pallas kernels for 0% -> 5%
where the time goes in v1:
time: 103 us
  starting transfers between devices  35.7 us (35%)
  waiting for transfers between devices  22.5 us (22%)
  local copies, waits for them, and re-layouts  19.9 us (19%)
  Pallas kernels  11.5 us (11%)
  matrix products  4.33 us (4%)
  other arithmetic  4.08 us (4%)
  blocking collectives  3.61 us (4%)
    ppermute x12, starting transfers between devices, shifted(): return lax.ppermute(value, 'req', pairs)  16.5 us
    all_to_all x1, waiting for transfers between devices, shards(): lax.all_to_all(latent_out, 'req', split_axis=0, concat_axis=0, tiled=True)  10.5 us
    all_to_all x1, starting transfers between devices, shards(): lax.all_to_all(sent, ('group', 'seq'), split_axis=0, concat_axis=0, tiled...  9.99 us
    gather x5, local copies, waits for them, and re-layouts, shards(): back = exchange(latent[turned][:, turned])[turned][:, turned]  9.53 us
    ppermute x12, waiting for transfers between devices, shifted(): return lax.ppermute(value, 'req', pairs)  8.66 us
    all_to_all x1, starting transfers between devices, shards(): lax.all_to_all(latent_out, 'req', split_axis=0, concat_axis=0, tiled=True)  6.77 us
    pallas_call x1, Pallas kernels, gather_pages(): pl.pallas_call(send_kernel, out_shape=jax.ShapeDtypeStruct((SRC, PAIR_ROW...  6.59 us
    pallas_call x1, Pallas kernels, attend(): pl.pallas_call(attend_kernel, out_shape=jax.ShapeDtypeStruct((SRC, block,...  4.92 us
  transfers between devices with their start and end apart: 17, of which 6 were waited for; matrix products, arithmetic and copies ran while one was open for 21% of the time, Pallas kernels for 5%

profile of v1, /device:TPU:1, one launch (start us, length us, event | category | flops | bytes accessed | tf_op | source)
XLA Modules:
  0.0 102.5 jit_solution(12621591331026358777)
XLA Ops:
  0.8 1.7 %copy-done.1 = bf16[1,1,2,16,64,576]{5,4,3,2,1,0:T(8,128)(2,1)S(1)} copy-done((bf16[1,1,2,16,64,576]{5,4,3,2,1,0:T(8,128)(2,1)S(1)}, bf16[1,1,2,16,64,576]{5,4,3,2,1,0:T(8,128)(2,1)}, u32[]{:S(2)}) %copy-start.1) | copy-done | bytes 2359320
  2.6 6.6 %shard_map.82 = bf16[16,144,512]{2,1,0:T(8,128)(2,1)} custom-call(s32[16]{0:T(128)S(1)} %select_reduce_fusion.page_of, bf16[2,16,64,576]{3,2,1,0:T(8,128)(2,1)S(1)} %bitcast.100), custom_call_target="tpu_custom_call" | custom-call | bytes 5242880 | tf_op jit(solution)/shard_map/pallas_call | solution.py:65
  9.2 10.0 %all-to-all-start = ((bf16[16,144,512]{2,1,0:T(8,128)(2,1)}), bf16[16,144,512]{2,1,0:T(8,128)(2,1)S(1)}, u32[]{:S(2)}, u32[]{:S(2)}) async-start(bf16[16,144,512]{2,1,0:T(8,128)(2,1)} %shard_map.82), calls=%async_computation | async-start | bytes 4718592 | tf_op jit(solution)/shard_map/all_to_all | solution.py:180
  20.1 1.3 %collective-permute-start.2 = (bf16[4,4,8,128]{3,1,2,0:T(4,128)(2,1)S(1)}, bf16[4,4,8,128]{3,1,2,0:T(4,128)(2,1)S(1)}, u32[]{:S(2)}, u32[]{:S(2)}) collective-permute-start(bf16[4,4,8,128]{3,1,2,0:T(4,128)(2,1)S(1)} %bitcast.113), channel_id=1, source_target_pairs={{0,1},{1,2},{2,3},{3,0},{4,5},{5,6},{6,7},{7,4},{8,9},{9,10},{10,1... | collective-permute-start | bytes 98312 | tf_op jit(solution)/shard_map/ppermute | solution.py:152
  21.4 2.5 %collective-permute-start.3 = (bf16[4,4,8,128]{3,1,2,0:T(4,128)(2,1)S(1)}, bf16[4,4,8,128]{3,1,2,0:T(4,128)(2,1)S(1)}, u32[]{:S(2)}, u32[]{:S(2)}) collective-permute-start(bf16[4,4,8,128]{3,1,2,0:T(4,128)(2,1)S(1)} %bitcast.114), channel_id=1, source_target_pairs={{0,2},{1,3},{2,0},{3,1},{4,6},{5,7},{6,4},{7,5},{8,10},{9,11},{10,... | collective-permute-start | bytes 98312 | tf_op jit(solution)/shard_map/ppermute | solution.py:152
  24.0 1.2 %collective-permute-start.4 = (bf16[4,4,8,128]{3,1,2,0:T(4,128)(2,1)S(1)}, bf16[4,4,8,128]{3,1,2,0:T(4,128)(2,1)S(1)}, u32[]{:S(2)}, u32[]{:S(2)}) collective-permute-start(bf16[4,4,8,128]{3,1,2,0:T(4,128)(2,1)S(1)} %bitcast.115), channel_id=1, source_target_pairs={{0,3},{1,0},{2,1},{3,2},{4,7},{5,4},{6,5},{7,6},{8,11},{9,8},{10,9... | collective-permute-start | bytes 98312 | tf_op jit(solution)/shard_map/ppermute | solution.py:152
  25.2 2.4 %dynamic-slice_bitcast_fusion.1 = (bf16[8,128,256]{2,1,0:T(8,128)(2,1)}, bf16[8,128,256]{2,1,0:T(8,128)(2,1)}) fusion(bf16[2,8,128,256]{3,2,1,0:T(8,128)(2,1)} %param.9, s32[]{:T(128)S(6)} %select_n.147, s32[]{:T(128)S(6)} %select_n.148), kind=kLoop, calls=%fused_computation.29 | loop fusion | bytes 2097160 | tf_op jit(solution)/shard_map/jit(dynamic_index_in_dim)/squeeze | solution.py:166
  27.5 1.0 collective-permute-start.1
  28.7 1.1 %dynamic-slice_bitcast_fusion.3 = (bf16[8,256,128]{2,1,0:T(8,128)(2,1)}, bf16[8,256,128]{2,1,0:T(8,128)(2,1)}) fusion(bf16[2,8,256,128]{3,2,1,0:T(8,128)(2,1)S(1)} %copy-done.2, s32[]{:T(128)S(6)} %select_n.147, s32[]{:T(128)S(6)} %select_n.148), kind=kLoop, calls=%fused_computation.31 | loop fusion | bytes 2097160 | tf_op jit(solution)/shard_map/jit(dynamic_index_in_dim)/squeeze | solution.py:166
  30.0 1.4 %collective-permute-start.5 = (bf16[4,4,8,128]{3,1,0,2:T(4,128)(2,1)S(1)}, bf16[4,4,8,128]{3,1,0,2:T(4,128)(2,1)S(1)}, u32[]{:S(2)}, u32[]{:S(2)}) collective-permute-start(bf16[4,4,8,128]{3,1,0,2:T(4,128)(2,1)S(1)} %get-tuple-element.20), channel_id=1, source_target_pairs={{0,4},{1,5},{2,6},{3,7},{4,8},{5,9},{6,10},{7,11},{8,12},{9,13},{1... | collective-permute-start | bytes 98312 | tf_op jit(solution)/shard_map/ppermute | solution.py:152
  31.3 2.6 %collective-permute-start.6 = (bf16[4,4,8,128]{3,1,0,2:T(4,128)(2,1)S(1)}, bf16[4,4,8,128]{3,1,0,2:T(4,128)(2,1)S(1)}, u32[]{:S(2)}, u32[]{:S(2)}) collective-permute-start(bf16[4,4,8,128]{3,1,0,2:T(4,128)(2,1)S(1)} %get-tuple-element.19), channel_id=1, source_target_pairs={{0,8},{1,9},{2,10},{3,11},{4,12},{5,13},{6,14},{7,15},{8,0},{9,1},... | collective-permute-start | bytes 98312 | tf_op jit(solution)/shard_map/ppermute | solution.py:152
  34.0 1.1 %collective-permute-start.7 = (bf16[4,4,8,128]{3,1,0,2:T(4,128)(2,1)S(1)}, bf16[4,4,8,128]{3,1,0,2:T(4,128)(2,1)S(1)}, u32[]{:S(2)}, u32[]{:S(2)}) collective-permute-start(bf16[4,4,8,128]{3,1,0,2:T(4,128)(2,1)S(1)} %get-tuple-element.18), channel_id=1, source_target_pairs={{0,12},{1,13},{2,14},{3,15},{4,0},{5,1},{6,2},{7,3},{8,4},{9,5},{1... | collective-permute-start | bytes 98312 | tf_op jit(solution)/shard_map/ppermute | solution.py:152
  35.7 1.4 %collective-permute-start = (bf16[8,256,128]{2,1,0:T(8,128)(2,1)}, bf16[8,256,128]{2,1,0:T(8,128)(2,1)}, u32[]{:S(2)}, u32[]{:S(2)}) collective-permute-start(bf16[8,256,128]{2,1,0:T(8,128)(2,1)} %get-tuple-element.8), channel_id=1, source_target_pairs={{0,16},{16,0},{1,17},{17,1},{2,18},{18,2},{3,19},{19,3},{4,20},{20... | collective-permute-start | bytes 1572872 | tf_op jit(solution)/shard_map/ppermute | solution.py:162
  37.7 2.0 %fusion = bf16[4,4,4,8,512]{4,2,1,0,3:T(4,128)(2,1)S(1)} fusion(bf16[8,128,256]{2,1,0:T(8,128)(2,1)} %collective-permute-done.1, bf16[8,128,256]{2,1,0:T(8,128)(2,1)} %get-tuple-element.5, pred[]{:T(512)S(6)} %eq.28, bf16[1,4,4,8,128]{4,2,1,0,3:T(4,128)(2,1)} %bitcast.124, bf16[1,4,4,8,128]{4,2,1,0,3:T(4,128)(2,1)S(1)} %bitcast.123, ...), kind=kOutput, calls=%fused_computation.6 | convolution fusion | flops 72613888 | bytes 1703937 | tf_op jit(solution)/shard_map/yxthd,hdc->yxthc/dot_general | solution.py:202
  39.8 1.8 %gather_fusion.1 = bf16[4,4,4,8,512]{4,2,1,3,0:T(4,128)(2,1)} fusion(bf16[4,4,4,8,512]{4,2,1,0,3:T(4,128)(2,1)S(1)} %fusion, s32[1024]{0:T(1024)S(1)} %pad_clamp_fusion), kind=kCustom, calls=%fused_computation.1 | custom fusion | bytes 1048592 | tf_op jit(solution)/shard_map/gather | solution.py:206
  41.5 2.1 %gather_fusion.2 = bf16[4,4,4,8,512]{4,2,3,1,0:T(4,128)(2,1)S(1)} fusion(bf16[4,4,4,8,512]{4,2,1,3,0:T(4,128)(2,1)} %gather_fusion.1, s32[1024]{0:T(1024)S(1)} %pad_clamp_fusion), kind=kCustom, calls=%fused_computation.2 | custom fusion | bytes 1048592 | tf_op jit(solution)/shard_map/gather | solution.py:206
  44.9 1.6 %collective-permute-start.9 = (bf16[4,4,8,512]{3,1,2,0:T(4,128)(2,1)}, bf16[4,4,8,512]{3,1,2,0:T(4,128)(2,1)S(1)}, u32[]{:S(2)}, u32[]{:S(2)}) collective-permute-start(bf16[4,4,8,512]{3,1,2,0:T(4,128)(2,1)} %get-tuple-element.14), channel_id=1, source_target_pairs={{0,2},{1,3},{2,0},{3,1},{4,6},{5,7},{6,4},{7,5},{8,10},{9,11},{10,... | collective-permute-start | bytes 393224 | tf_op jit(solution)/shard_map/ppermute | solution.py:152
  47.4 4.4 %collective-permute-done.8 = bf16[4,4,8,512]{3,1,2,0:T(4,128)(2,1)S(1)} collective-permute-done((bf16[4,4,8,512]{3,1,2,0:T(4,128)(2,1)}, bf16[4,4,8,512]{3,1,2,0:T(4,128)(2,1)S(1)}, u32[]{:S(2)}, u32[]{:S(2)}) %collective-permute-start.8) | collective-permute-done | bytes 131104 | tf_op jit(solution)/shard_map/ppermute | solution.py:152
  52.4 1.4 %pad_maximum_fusion = bf16[4,4,4,8,512]{4,2,3,0,1:T(4,128)(2,1)S(1)} fusion(bf16[4,1,4,8,512]{4,2,3,0,1:T(4,128)(2,1)S(1)} %bitcast.111, bf16[4,1,4,8,512]{4,2,3,0,1:T(4,128)(2,1)S(1)} %bitcast.109, bf16[4,1,4,8,512]{4,2,3,0,1:T(4,128)(2,1)S(1)} %bitcast.108, bf16[4,1,4,8,512]{4,2,3,0,1:T(4,128)(2,1)} %get-tuple-element.13), kind=kLoop, calls=%fused_computation.25 | loop fusion | flops 786432 | bytes 1048576 | tf_op jit(solution)/shard_map/stack | solution.py:157
  55.6 2.4 %collective-permute-start.12 = (bf16[4,4,8,512]{3,1,2,0:T(4,128)(2,1)S(1)}, bf16[4,4,8,512]{3,1,2,0:T(4,128)(2,1)S(1)}, u32[]{:S(2)}, u32[]{:S(2)}) collective-permute-start(bf16[4,4,8,512]{3,1,2,0:T(4,128)(2,1)S(1)} %get-tuple-element.12), channel_id=1, source_target_pairs={{0,8},{1,9},{2,10},{3,11},{4,12},{5,13},{6,14},{7,15},{8,0},{9,1},... | collective-permute-start | bytes 393224 | tf_op jit(solution)/shard_map/ppermute | solution.py:152
  58.5 1.7 %collective-permute-done.11 = bf16[4,4,8,512]{3,1,2,0:T(4,128)(2,1)S(1)} collective-permute-done((bf16[4,4,8,512]{3,1,2,0:T(4,128)(2,1)}, bf16[4,4,8,512]{3,1,2,0:T(4,128)(2,1)S(1)}, u32[]{:S(2)}, u32[]{:S(2)}) %collective-permute-start.11) | collective-permute-done | bytes 131104 | tf_op jit(solution)/shard_map/ppermute | solution.py:152
  60.2 2.0 %collective-permute-done.12 = bf16[4,4,8,512]{3,1,2,0:T(4,128)(2,1)S(1)} collective-permute-done((bf16[4,4,8,512]{3,1,2,0:T(4,128)(2,1)S(1)}, bf16[4,4,8,512]{3,1,2,0:T(4,128)(2,1)S(1)}, u32[]{:S(2)}, u32[]{:S(2)}) %collective-permute-start.12) | collective-permute-done | bytes 131104 | tf_op jit(solution)/shard_map/ppermute | solution.py:152
  62.9 1.6 %pad_maximum_fusion.1 = bf16[4,4,4,8,512]{4,2,3,1,0:T(4,128)(2,1)S(1)} fusion(bf16[1,4,4,8,512]{4,2,3,1,0:T(4,128)(2,1)} %bitcast.41, bf16[1,4,4,8,512]{4,2,3,1,0:T(4,128)(2,1)} %bitcast.112, bf16[1,4,4,8,512]{4,2,3,1,0:T(4,128)(2,1)} %bitcast.110, bf16[1,4,4,8,512]{4,2,3,1,0:T(4,128)(2,1)} %get-tuple-element.9), kind=kLoop, calls=%fused_computation.26 | loop fusion | flops 786432 | bytes 1048576 | tf_op jit(solution)/shard_map/stack | solution.py:158
  64.5 1.8 %gather_fusion.3 = bf16[4,4,4,8,512]{4,2,3,1,0:T(4,128)(2,1)} fusion(bf16[4,4,4,8,512]{4,2,3,1,0:T(4,128)(2,1)S(1)} %pad_maximum_fusion.1, s32[1024]{0:T(1024)S(1)} %pad_clamp_fusion), kind=kCustom, calls=%fused_computation.3 | custom fusion | bytes 1048592 | tf_op jit(solution)/shard_map/gather | solution.py:206
  66.2 2.8 %gather_fusion.4 = bf16[4,4,4,8,512]{4,2,3,1,0:T(4,128)(2,1)} fusion(bf16[4,4,4,8,512]{4,2,3,1,0:T(4,128)(2,1)} %gather_fusion.3, s32[1024]{0:T(1024)S(1)} %pad_clamp_fusion), kind=kCustom, calls=%fused_computation.4 | custom fusion | bytes 1048592 | tf_op jit(solution)/shard_map/gather | solution.py:206
  69.0 1.1 %copy.50 = bf16[4,4,4,8,512]{4,3,2,1,0:T(8,128)(2,1)S(1)} copy(bf16[4,4,4,8,512]{4,2,3,0,1:T(4,128)(2,1)} %bitcast.104) | data formatting | bytes 1048576 | tf_op jit(solution)/shard_map/gather | solution.py:206
  70.2 3.3 %all-to-all-done.pages = bf16[16,144,512]{2,1,0:T(8,128)(2,1)S(1)} async-done(((bf16[16,144,512]{2,1,0:T(8,128)(2,1)}), bf16[16,144,512]{2,1,0:T(8,128)(2,1)S(1)}, u32[]{:S(2)}, u32[]{:S(2)}) %all-to-all-start) | async-done | bytes 2359328 | tf_op jit(solution)/shard_map/all_to_all | solution.py:180
  73.5 4.9 %shard_map.83 = bf16[16,32,512]{2,1,0:T(8,128)(2,1)} custom-call(s32[16]{0:T(128)S(1)} %fusion.30.order, bf16[512,512]{1,0:T(8,128)(2,1)S(1)} %bitcast.101, bf16[512,64]{1,0:T(8,128)(2,1)S(1)} %bitcast.102, bf16[16,144,512]{2,1,0:T(8,128)(2,1)S(1)} %all-to-all-done.pages, f32[1,2048]{1,0:T(1,128)S(1)} %reshape.234.bias, ...), custom_call_target="tpu_custom_call" | custom-call | flops 2281701376 | bytes 4194304 | tf_op jit(solution)/shard_map/pallas_call | solution.py:130
  78.4 6.8 %all-to-all-start.1 = ((bf16[16,32,512]{2,1,0:T(8,128)(2,1)}), bf16[16,32,512]{2,1,0:T(8,128)(2,1)S(1)}, u32[]{:S(2)}, u32[]{:S(2)}) async-start(bf16[16,32,512]{2,1,0:T(8,128)(2,1)} %shard_map.83), calls=%async_computation.1 | async-start | bytes 1048576 | tf_op jit(solution)/shard_map/all_to_all | solution.py:223
  85.2 10.5 %all-to-all-done.1 = bf16[16,32,512]{2,1,0:T(8,128)(2,1)S(1)} async-done(((bf16[16,32,512]{2,1,0:T(8,128)(2,1)}), bf16[16,32,512]{2,1,0:T(8,128)(2,1)S(1)}, u32[]{:S(2)}, u32[]{:S(2)}) %all-to-all-start.1) | async-done | bytes 524320 | tf_op jit(solution)/shard_map/all_to_all | solution.py:223
  95.7 2.3 %fusion.1 = bf16[16,4,8,128]{3,0,1,2:T(8,128)(2,1)S(1)} fusion(bf16[8,256,128]{2,1,0:T(8,128)(2,1)} %collective-permute-done, bf16[8,256,128]{2,1,0:T(8,128)(2,1)} %get-tuple-element.7, pred[]{:T(512)S(6)} %eq.28, bf16[16,4,8,512]{3,2,1,0:T(8,128)(2,1)S(1)} %bitcast.106), kind=kOutput, calls=%fused_computation.8 | convolution fusion | flops 71892992 | bytes 1703937 | tf_op jit(solution)/shard_map/rthc,hcv->rthv/dot_general | solution.py:224
  98.1 3.6 %all-gather = bf16[32,4,8,128]{3,0,1,2:T(8,128)(2,1)S(1)} all-gather(bf16[16,4,8,128]{3,0,1,2:T(8,128)(2,1)S(1)} %fusion.1), channel_id=2, replica_groups=mesh['group'=8,'seq'=2,'req'=16] {'seq'}, dimensions={0}, use_global_device_ids=true | all-gather | bytes 393216 | tf_op jit(solution)/shard_map/all_gather | solution.py:230
  (62 shorter events, 9.3 us)
Async XLA Ops:
  0.0 19.2 %copy-start = (bf16[2,1,4,128,192]{3,4,2,1,0:T(8,128)(2,1)S(1)}, bf16[2,1,4,128,192]{3,4,2,1,0:T(8,128)(2,1)}, u32[]{:S(2)}) copy-start(bf16[2,1,4,128,192]{3,4,2,1,0:T(8,128)(2,1)} %param.8) | copy-start | bytes 1179652
  0.8 1.7 %copy-start.1 = (bf16[1,1,2,16,64,576]{5,4,3,2,1,0:T(8,128)(2,1)S(1)}, bf16[1,1,2,16,64,576]{5,4,3,2,1,0:T(8,128)(2,1)}, u32[]{:S(2)}) copy-start(bf16[1,1,2,16,64,576]{5,4,3,2,1,0:T(8,128)(2,1)} %param.11) | copy-start | bytes 7077892
  9.2 64.3 %all-to-all-start = ((bf16[16,144,512]{2,1,0:T(8,128)(2,1)}), bf16[16,144,512]{2,1,0:T(8,128)(2,1)S(1)}, u32[]{:S(2)}, u32[]{:S(2)}) async-start(bf16[16,144,512]{2,1,0:T(8,128)(2,1)} %shard_map.82), calls=%async_computation | async-start | bytes 4718592 | tf_op jit(solution)/shard_map/all_to_all | solution.py:180
  19.2 9.3 %copy-start.6 = (s32[1,1,16]{2,1,0:T(1,128)S(1)}, s32[1,1,16]{2,1,0:T(1,128)}, u32[]{:S(2)}) copy-start(s32[1,1,16]{2,1,0:T(1,128)} %param.13) | copy-start | bytes 196
  19.2 9.4 %copy-start.5 = (bf16[2,1,4,576]{3,2,1,0:T(4,128)(2,1)S(1)}, bf16[2,1,4,576]{3,2,1,0:T(4,128)(2,1)}, u32[]{:S(2)}) copy-start(bf16[2,1,4,576]{3,2,1,0:T(4,128)(2,1)} %param.15) | copy-start | bytes 27652
  20.1 9.7 %collective-permute-start.2 = (bf16[4,4,8,128]{3,1,2,0:T(4,128)(2,1)S(1)}, bf16[4,4,8,128]{3,1,2,0:T(4,128)(2,1)S(1)}, u32[]{:S(2)}, u32[]{:S(2)}) collective-permute-start(bf16[4,4,8,128]{3,1,2,0:T(4,128)(2,1)S(1)} %bitcast.113), channel_id=1, source_target_pairs={{0,1},{1,2},{2,3},{3,0},{4,5},{5,6},{6,7},{7,4},{8,9},{9,10},{10,1... | collective-permute-start | bytes 98312 | tf_op jit(solution)/shard_map/ppermute | solution.py:152
  21.4 8.4 %collective-permute-start.3 = (bf16[4,4,8,128]{3,1,2,0:T(4,128)(2,1)S(1)}, bf16[4,4,8,128]{3,1,2,0:T(4,128)(2,1)S(1)}, u32[]{:S(2)}, u32[]{:S(2)}) collective-permute-start(bf16[4,4,8,128]{3,1,2,0:T(4,128)(2,1)S(1)} %bitcast.114), channel_id=1, source_target_pairs={{0,2},{1,3},{2,0},{3,1},{4,6},{5,7},{6,4},{7,5},{8,10},{9,11},{10,... | collective-permute-start | bytes 98312 | tf_op jit(solution)/shard_map/ppermute | solution.py:152
  24.0 5.8 %collective-permute-start.4 = (bf16[4,4,8,128]{3,1,2,0:T(4,128)(2,1)S(1)}, bf16[4,4,8,128]{3,1,2,0:T(4,128)(2,1)S(1)}, u32[]{:S(2)}, u32[]{:S(2)}) collective-permute-start(bf16[4,4,8,128]{3,1,2,0:T(4,128)(2,1)S(1)} %bitcast.115), channel_id=1, source_target_pairs={{0,3},{1,0},{2,1},{3,2},{4,7},{5,4},{6,5},{7,6},{8,11},{9,8},{10,9... | collective-permute-start | bytes 98312 | tf_op jit(solution)/shard_map/ppermute | solution.py:152
  25.2 3.5 %copy-start.2 = (bf16[2,8,256,128]{3,2,1,0:T(8,128)(2,1)S(1)}, bf16[2,8,256,128]{3,2,1,0:T(8,128)(2,1)}, u32[]{:S(2)}) copy-start(bf16[2,8,256,128]{3,2,1,0:T(8,128)(2,1)} %param.10) | copy-start | bytes 3145732
  27.5 9.6 %collective-permute-start.1 = (bf16[8,128,256]{2,1,0:T(8,128)(2,1)}, bf16[8,128,256]{2,1,0:T(8,128)(2,1)}, u32[]{:S(2)}, u32[]{:S(2)}) collective-permute-start(bf16[8,128,256]{2,1,0:T(8,128)(2,1)} %get-tuple-element.6), channel_id=1, source_target_pairs={{0,16},{16,0},{1,17},{17,1},{2,18},{18,2},{3,19},{19,3},{4,20},{20... | collective-permute-start | bytes 1572872 | tf_op jit(solution)/shard_map/ppermute | solution.py:162
  28.5 18.7 %collective-permute-start.14 = (s32[16]{0:T(128)S(1)}, s32[16]{0:T(128)S(1)}, u32[]{:S(2)}, u32[]{:S(2)}) collective-permute-start(s32[16]{0:T(128)S(1)} %bitcast.119), channel_id=1, source_target_pairs={{0,16},{16,0},{1,17},{17,1},{2,18},{18,2},{3,19},{19,3},{4,20},{20... | collective-permute-start | bytes 200 | tf_op jit(solution)/shard_map/ppermute | solution.py:162
  30.0 5.7 %collective-permute-start.5 = (bf16[4,4,8,128]{3,1,0,2:T(4,128)(2,1)S(1)}, bf16[4,4,8,128]{3,1,0,2:T(4,128)(2,1)S(1)}, u32[]{:S(2)}, u32[]{:S(2)}) collective-permute-start(bf16[4,4,8,128]{3,1,0,2:T(4,128)(2,1)S(1)} %get-tuple-element.20), channel_id=1, source_target_pairs={{0,4},{1,5},{2,6},{3,7},{4,8},{5,9},{6,10},{7,11},{8,12},{9,13},{1... | collective-permute-start | bytes 98312 | tf_op jit(solution)/shard_map/ppermute | solution.py:152
  31.3 5.8 %collective-permute-start.6 = (bf16[4,4,8,128]{3,1,0,2:T(4,128)(2,1)S(1)}, bf16[4,4,8,128]{3,1,0,2:T(4,128)(2,1)S(1)}, u32[]{:S(2)}, u32[]{:S(2)}) collective-permute-start(bf16[4,4,8,128]{3,1,0,2:T(4,128)(2,1)S(1)} %get-tuple-element.19), channel_id=1, source_target_pairs={{0,8},{1,9},{2,10},{3,11},{4,12},{5,13},{6,14},{7,15},{8,0},{9,1},... | collective-permute-start | bytes 98312 | tf_op jit(solution)/shard_map/ppermute | solution.py:152
  34.0 3.2 %collective-permute-start.7 = (bf16[4,4,8,128]{3,1,0,2:T(4,128)(2,1)S(1)}, bf16[4,4,8,128]{3,1,0,2:T(4,128)(2,1)S(1)}, u32[]{:S(2)}, u32[]{:S(2)}) collective-permute-start(bf16[4,4,8,128]{3,1,0,2:T(4,128)(2,1)S(1)} %get-tuple-element.18), channel_id=1, source_target_pairs={{0,12},{1,13},{2,14},{3,15},{4,0},{5,1},{6,2},{7,3},{8,4},{9,5},{1... | collective-permute-start | bytes 98312 | tf_op jit(solution)/shard_map/ppermute | solution.py:152
  35.7 49.5 %collective-permute-start = (bf16[8,256,128]{2,1,0:T(8,128)(2,1)}, bf16[8,256,128]{2,1,0:T(8,128)(2,1)}, u32[]{:S(2)}, u32[]{:S(2)}) collective-permute-start(bf16[8,256,128]{2,1,0:T(8,128)(2,1)} %get-tuple-element.8), channel_id=1, source_target_pairs={{0,16},{16,0},{1,17},{17,1},{2,18},{18,2},{3,19},{19,3},{4,20},{20... | collective-permute-start | bytes 1572872 | tf_op jit(solution)/shard_map/ppermute | solution.py:162
  37.1 0.6 copy-start.7
  44.6 7.3 %collective-permute-start.8 = (bf16[4,4,8,512]{3,1,2,0:T(4,128)(2,1)}, bf16[4,4,8,512]{3,1,2,0:T(4,128)(2,1)S(1)}, u32[]{:S(2)}, u32[]{:S(2)}) collective-permute-start(bf16[4,4,8,512]{3,1,2,0:T(4,128)(2,1)} %get-tuple-element.15), channel_id=1, source_target_pairs={{0,1},{1,2},{2,3},{3,0},{4,5},{5,6},{6,7},{7,4},{8,9},{9,10},{10,1... | collective-permute-start | bytes 393224 | tf_op jit(solution)/shard_map/ppermute | solution.py:152
  44.9 7.0 %collective-permute-start.9 = (bf16[4,4,8,512]{3,1,2,0:T(4,128)(2,1)}, bf16[4,4,8,512]{3,1,2,0:T(4,128)(2,1)S(1)}, u32[]{:S(2)}, u32[]{:S(2)}) collective-permute-start(bf16[4,4,8,512]{3,1,2,0:T(4,128)(2,1)} %get-tuple-element.14), channel_id=1, source_target_pairs={{0,2},{1,3},{2,0},{3,1},{4,6},{5,7},{6,4},{7,5},{8,10},{9,11},{10,... | collective-permute-start | bytes 393224 | tf_op jit(solution)/shard_map/ppermute | solution.py:152
  46.5 5.9 %collective-permute-start.10 = (bf16[4,4,8,512]{3,1,2,0:T(4,128)(2,1)}, bf16[4,4,8,512]{3,1,2,0:T(4,128)(2,1)S(1)}, u32[]{:S(2)}, u32[]{:S(2)}) collective-permute-start(bf16[4,4,8,512]{3,1,2,0:T(4,128)(2,1)} %get-tuple-element.16), channel_id=1, source_target_pairs={{0,3},{1,0},{2,1},{3,2},{4,7},{5,4},{6,5},{7,6},{8,11},{9,8},{10,9... | collective-permute-start | bytes 393224 | tf_op jit(solution)/shard_map/ppermute | solution.py:152
  54.7 5.5 %collective-permute-start.11 = (bf16[4,4,8,512]{3,1,2,0:T(4,128)(2,1)}, bf16[4,4,8,512]{3,1,2,0:T(4,128)(2,1)S(1)}, u32[]{:S(2)}, u32[]{:S(2)}) collective-permute-start(bf16[4,4,8,512]{3,1,2,0:T(4,128)(2,1)} %get-tuple-element.10), channel_id=1, source_target_pairs={{0,4},{1,5},{2,6},{3,7},{4,8},{5,9},{6,10},{7,11},{8,12},{9,13},{1... | collective-permute-start | bytes 393224 | tf_op jit(solution)/shard_map/ppermute | solution.py:152
  55.6 6.6 %collective-permute-start.12 = (bf16[4,4,8,512]{3,1,2,0:T(4,128)(2,1)S(1)}, bf16[4,4,8,512]{3,1,2,0:T(4,128)(2,1)S(1)}, u32[]{:S(2)}, u32[]{:S(2)}) collective-permute-start(bf16[4,4,8,512]{3,1,2,0:T(4,128)(2,1)S(1)} %get-tuple-element.12), channel_id=1, source_target_pairs={{0,8},{1,9},{2,10},{3,11},{4,12},{5,13},{6,14},{7,15},{8,0},{9,1},... | collective-permute-start | bytes 393224 | tf_op jit(solution)/shard_map/ppermute | solution.py:152
  58.0 4.3 %collective-permute-start.13 = (bf16[4,4,8,512]{3,1,2,0:T(4,128)(2,1)S(1)}, bf16[4,4,8,512]{3,1,2,0:T(4,128)(2,1)}, u32[]{:S(2)}, u32[]{:S(2)}) collective-permute-start(bf16[4,4,8,512]{3,1,2,0:T(4,128)(2,1)S(1)} %get-tuple-element.11), channel_id=1, source_target_pairs={{0,12},{1,13},{2,14},{3,15},{4,0},{5,1},{6,2},{7,3},{8,4},{9,5},{1... | collective-permute-start | bytes 393224 | tf_op jit(solution)/shard_map/ppermute | solution.py:152
  60.2 2.0 %copy-start.3 = (bf16[4,4,8,512]{3,1,2,0:T(4,128)(2,1)}, bf16[4,4,8,512]{3,1,2,0:T(4,128)(2,1)S(1)}, u32[]{:S(2)}) copy-start(bf16[4,4,8,512]{3,1,2,0:T(4,128)(2,1)S(1)} %collective-permute-done.11) | copy-start | bytes 393220
  62.2 0.7 copy-start.4
  78.4 17.3 %all-to-all-start.1 = ((bf16[16,32,512]{2,1,0:T(8,128)(2,1)}), bf16[16,32,512]{2,1,0:T(8,128)(2,1)S(1)}, u32[]{:S(2)}, u32[]{:S(2)}) async-start(bf16[16,32,512]{2,1,0:T(8,128)(2,1)} %shard_map.83), calls=%async_computation.1 | async-start | bytes 1048576 | tf_op jit(solution)/shard_map/all_to_all | solution.py:223

commit v2 on v0

v2 whole, which is shorter than its diff:
```python
import functools
import math

import jax
import jax.numpy as jnp
from jax import lax
from jax.experimental import pallas as pl
from jax.experimental.pallas import tpu as pltpu
from jax.sharding import PartitionSpec as P

KV_RANK = 512
ROPE = 64
NOPE = 128
VDIM = 128
HEADS_PER = 8
STEPS = 4
PAGE = 64
PEERS = 16
BLOCK_KEYS = 1024
PAIR = 2 * PAGE
PAIR_ROWS = PAIR + 16
BLOCK = HEADS_PER * STEPS
ROWS = PEERS * BLOCK
HALF = KV_RANK // 2
DEAD = -1e30
SCALE = 1.0 / math.sqrt(NOPE + ROPE)
TO_LOG2 = SCALE * math.log2(math.e)
SIDE = 4
VMEM = pl.BlockSpec(memory_space=pltpu.VMEM)
SMEM = pl.BlockSpec(memory_space=pltpu.SMEM)
ANY = pl.BlockSpec(memory_space=pl.ANY)


def send_kernel(send_to, pages, out, target_of, page_of, held, packed, target_sem, in_sem, lat_sem, rope_sem):
    targets = pltpu.make_async_copy(send_to, target_of, target_sem)
    targets.start()

    def fetch(layer):
        return pltpu.make_async_copy(pages.at[layer], held.at[layer], in_sem.at[layer])

    def latents(dest, half):
        index = dest * 2 + half
        return pltpu.make_async_copy(
            held.at[dest % 2, page_of[dest - dest % 2 + half], :, pl.ds(0, KV_RANK)],
            out.at[dest, pl.ds(half * PAGE, PAGE)],
            lat_sem.at[index],
        )

    def ropes(dest):
        return pltpu.make_async_copy(
            packed.at[dest], out.at[dest, pl.ds(PAIR, 16)], rope_sem.at[dest]
        )

    for layer in range(2):
        fetch(layer).start()
    targets.wait()
    for page in range(PEERS):
        page_of[target_of[page]] = page
    for layer in range(2):
        fetch(layer).wait()
        for dest in range(layer, PEERS, 2):
            for half in range(2):
                latents(dest, half).start()
        for dest in range(layer, PEERS, 2):
            groups = [
                held[layer, page_of[dest - layer + half], 16 * k : 16 * k + 16, KV_RANK:]
                for half in range(2)
                for k in range(PAGE // 16)
            ]
            packed[dest] = jnp.concatenate(groups, axis=1)
            ropes(dest).start()
    for dest in range(PEERS):
        for half in range(2):
            latents(dest, half).wait()
        ropes(dest).wait()


def gather_pages(send_to, pages):
    return pl.pallas_call(
        send_kernel,
        out_shape=jax.ShapeDtypeStruct((PEERS, PAIR_ROWS, KV_RANK), jnp.bfloat16),
        in_specs=[ANY, ANY],
        out_specs=ANY,
        scratch_shapes=[
            pltpu.SMEM((PEERS,), jnp.int32),
            pltpu.SMEM((PEERS,), jnp.int32),
            pltpu.VMEM(pages.shape, jnp.bfloat16),
            pltpu.VMEM((PEERS, 16, KV_RANK), jnp.bfloat16),
            pltpu.SemaphoreType.DMA,
            pltpu.SemaphoreType.DMA((2,)),
            pltpu.SemaphoreType.DMA((2 * PEERS,)),
            pltpu.SemaphoreType.DMA((PEERS,)),
        ],
        compiler_params=pltpu.CompilerParams(vmem_limit_bytes=60 << 20),
        cost_estimate=pl.CostEstimate(flops=0, bytes_accessed=5 << 20, transcendentals=0),
    )(send_to, pages)


def around(place, step, sign):
    y = lax.rem(place // SIDE + SIDE + sign * (step // SIDE), SIDE)
    x = lax.rem(lax.rem(place, SIDE) + SIDE + sign * (step % SIDE), SIDE)
    return y * SIDE + x


def queries_kernel(where, queries, nope, rope, rows):
    rows[...] = queries[0, 0].astype(jnp.float32)
    for j in range(PEERS):
        ahead = pl.multiple_of(around(where[2], j, 1) * HEADS_PER, HEADS_PER)
        behind = pl.multiple_of(around(where[2], j, -1) * HEADS_PER, HEADS_PER)
        nope[j] = jnp.concatenate(
            [rows[t, pl.ds(ahead, HEADS_PER), :NOPE] for t in range(STEPS)], axis=0
        ).astype(jnp.bfloat16)
        rope[j * BLOCK : (j + 1) * BLOCK, :] = jnp.concatenate(
            [rows[t, pl.ds(behind, HEADS_PER), NOPE:] for t in range(STEPS)], axis=0
        ).astype(jnp.bfloat16)


def split_queries(where, queries):
    return pl.pallas_call(
        queries_kernel,
        out_shape=(
            jax.ShapeDtypeStruct((PEERS, BLOCK, NOPE), jnp.bfloat16),
            jax.ShapeDtypeStruct((ROWS, ROPE), jnp.bfloat16),
        ),
        grid_spec=pltpu.PrefetchScalarGridSpec(
            num_scalar_prefetch=1,
            grid=(1,),
            in_specs=[
                pl.BlockSpec((1,) + queries.shape[1:], lambda i, where: (where[1], 0, 0, 0, 0))
            ],
            out_specs=(
                pl.BlockSpec((PEERS, BLOCK, NOPE), lambda i, where: (0, 0, 0)),
                pl.BlockSpec((ROWS, ROPE), lambda i, where: (0, 0)),
            ),
            scratch_shapes=[pltpu.VMEM(queries.shape[2:], jnp.float32)],
        ),
        compiler_params=pltpu.CompilerParams(vmem_limit_bytes=8 << 20),
        cost_estimate=pl.CostEstimate(flops=0, bytes_accessed=600000, transcendentals=0),
    )(where, queries)


def absorb_kernel(where, heads, own, got, out):
    rows = heads[...]
    head = lax.rem(lax.broadcasted_iota(jnp.int32, rows.shape, 0), HEADS_PER)
    spread = jnp.concatenate(
        [jnp.where(head == h, rows, jnp.zeros_like(rows)) for h in range(HEADS_PER)], axis=1
    )
    for weight, half in ((own, where[1]), (got, 1 - where[1])):
        part = weight[0].reshape(HEADS_PER * NOPE, HALF)
        result = jnp.dot(spread, part, preferred_element_type=jnp.float32)
        result = result.astype(jnp.bfloat16)
        columns = pl.ds(pl.multiple_of(half * HALF, HALF), HALF)
        for j in range(PEERS):
            turned = (-(j // SIDE) % SIDE) * SIDE + -j % SIDE
            out[turned * BLOCK : (turned + 1) * BLOCK, columns] = result[j * BLOCK : (j + 1) * BLOCK]


def pick_values_kernel(where, own, got, out):
    layer = where[1]
    for weight, half in ((own, layer), (got, 1 - layer)):
        rows = pl.ds(pl.multiple_of(half * HALF, HALF), HALF)
        for h in range(HEADS_PER):
            out[h // 2, rows, h % 2 * VDIM : (h % 2 + 1) * VDIM] = weight[layer, h]


def pick_values(where, own, got):
    return pl.pallas_call(
        pick_values_kernel,
        out_shape=jax.ShapeDtypeStruct((HEADS_PER // 2, KV_RANK, 2 * VDIM), jnp.bfloat16),
        in_specs=[SMEM, VMEM, VMEM],
        out_specs=VMEM,
        compiler_params=pltpu.CompilerParams(vmem_limit_bytes=16 << 20),
        cost_estimate=pl.CostEstimate(flops=0, bytes_accessed=3 << 20, transcendentals=0),
    )(where, own, got)


def value_kernel(latent, weight, out):
    rows = latent[...]
    head = lax.rem(lax.broadcasted_iota(jnp.int32, (ROWS, VDIM), 0), HEADS_PER)
    result = jnp.zeros((ROWS, VDIM), jnp.float32)
    for p in range(HEADS_PER // 2):
        both = jnp.dot(rows, weight[p], preferred_element_type=jnp.float32)
        result = jnp.where(head == 2 * p, both[:, :VDIM], result)
        result = jnp.where(head == 2 * p + 1, both[:, VDIM:], result)
    out[...] = result.astype(jnp.bfloat16)


def project_values(latent, weight):
    return pl.pallas_call(
        value_kernel,
        out_shape=jax.ShapeDtypeStruct((ROWS, VDIM), jnp.bfloat16),
        in_specs=[VMEM, VMEM],
        out_specs=VMEM,
        compiler_params=pltpu.CompilerParams(vmem_limit_bytes=16 << 20),
        cost_estimate=pl.CostEstimate(
            flops=2 * ROWS * 1024 * KV_RANK, bytes_accessed=2 << 20, transcendentals=0
        ),
    )(latent, weight)


def project(kernel, width, where, rows, own, got):
    shape = (1,) + own.shape[1:]
    weight_spec = pl.BlockSpec(shape, lambda i, where: (where[1], 0, 0, 0))
    return pl.pallas_call(
        kernel,
        out_shape=jax.ShapeDtypeStruct((ROWS, width), jnp.bfloat16),
        grid_spec=pltpu.PrefetchScalarGridSpec(
            num_scalar_prefetch=1,
            grid=(1,),
            in_specs=[pl.BlockSpec(rows.shape, lambda i, where: (0, 0)), weight_spec, weight_spec],
            out_specs=pl.BlockSpec((ROWS, width), lambda i, where: (0, 0)),
        ),
        compiler_params=pltpu.CompilerParams(vmem_limit_bytes=24 << 20),
        cost_estimate=pl.CostEstimate(
            flops=2 * ROWS * 1024 * KV_RANK, bytes_accessed=2 << 20, transcendentals=0
        ),
    )(where, rows, own, got)


def dot_rows(a, b):
    return lax.dot_general(a, b, (((1,), (1,)), ((), ())), preferred_element_type=jnp.float32)


def attend_kernel(where, length, own_slot, other_slot, query, fresh, pages, out, ropes, scores, result, out_sem):
    layer = where[1]

    def store(j):
        return pltpu.make_async_copy(
            result.at[pl.ds(j * BLOCK, BLOCK)], out.at[around(where[2], j, -1)], out_sem.at[j]
        )

    lane = lax.broadcasted_iota(jnp.int32, (1, PAIR), 1)

    def live_of(source):
        mine, theirs = own_slot[source] * PAGE, other_slot[source] * PAGE
        first = jnp.where(layer == 0, mine, theirs)
        second = jnp.where(layer == 0, theirs, mine) + BLOCK_KEYS
        return lane < jnp.where(lane < PAGE, length[0] - first, length[0] - second + PAGE)

    for p in range(PEERS):
        for k in range(8):
            ropes[p * PAIR + 16 * k : p * PAIR + 16 * k + 16, :] = pages[
                p, PAIR:PAIR_ROWS, ROPE * k : ROPE * k + ROPE
            ]
    ql, qr = query[:, :KV_RANK], query[:, KV_RANK : KV_RANK + ROPE]
    step = lax.rem(lax.broadcasted_iota(jnp.int32, (ROWS, 16), 0) // HEADS_PER, STEPS)
    key = lax.broadcasted_iota(jnp.int32, (ROWS, 16), 1)
    lat, rope = fresh[:, :KV_RANK], fresh[:, KV_RANK:]
    extra = jnp.where(key <= step, dot_rows(ql, lat) + dot_rows(qr, rope), DEAD)
    width = 2 * PAIR
    highest = jnp.full((ROWS, PAIR), DEAD, jnp.float32)
    for n in range(0, PEERS, 2):
        part = slice(n * PAIR, n * PAIR + width)
        lat = pages[n : n + 2, :PAIR, :].reshape(width, KV_RANK)
        s = dot_rows(ql, lat) + dot_rows(qr, ropes[part, :])
        s = jnp.where(jnp.concatenate([live_of(n), live_of(n + 1)], axis=1), s, DEAD)
        scores[:, part] = s
        highest = jnp.maximum(highest, jnp.maximum(s[:, :PAIR], s[:, PAIR:]))
    peak = jnp.maximum(
        jnp.max(extra, axis=1, keepdims=True), jnp.max(highest, axis=1, keepdims=True)
    )
    weight = jnp.exp2((extra - peak) * TO_LOG2).astype(jnp.bfloat16)
    total = jnp.sum(weight.astype(jnp.float32), axis=1, keepdims=True)
    summed = jnp.dot(weight, fresh[:, :KV_RANK], preferred_element_type=jnp.float32)
    added = jnp.zeros((ROWS, PAIR), jnp.float32)
    for n in range(0, PEERS, 2):
        part = slice(n * PAIR, n * PAIR + width)
        lat = pages[n : n + 2, :PAIR, :].reshape(width, KV_RANK)
        weight = jnp.exp2((scores[:, part] - peak) * TO_LOG2).astype(jnp.bfloat16)
        kept = weight.astype(jnp.float32)
        added = added + (kept[:, :PAIR] + kept[:, PAIR:])
        summed = summed + jnp.dot(weight, lat, preferred_element_type=jnp.float32)
    total = total + jnp.sum(added, axis=1, keepdims=True)
    result[...] = (summed * (1.0 / total)).astype(jnp.bfloat16)
    for j in range(PEERS):
        store(j).start()
    for j in range(PEERS):
        store(j).wait()


def attend(*args):
    keys = PEERS * PAIR
    return pl.pallas_call(
        attend_kernel,
        out_shape=jax.ShapeDtypeStruct((PEERS, BLOCK, KV_RANK), jnp.bfloat16),
        in_specs=[SMEM] * 4 + [VMEM] * 3,
        out_specs=ANY,
        scratch_shapes=[
            pltpu.VMEM((keys, ROPE), jnp.bfloat16),
            pltpu.VMEM((ROWS, keys), jnp.float32),
            pltpu.VMEM((ROWS, KV_RANK), jnp.bfloat16),
            pltpu.SemaphoreType.DMA((PEERS,)),
        ],
        compiler_params=pltpu.CompilerParams(vmem_limit_bytes=40 << 20),
        cost_estimate=pl.CostEstimate(
            flops=2 * ROWS * keys * 1088, bytes_accessed=4 << 20, transcendentals=ROWS * keys
        ),
    )(*args)


def shifted(value, dy, dx):
    pairs = [
        (y * SIDE + x, ((y + dy) % SIDE) * SIDE + (x + dx) % SIDE)
        for y in range(SIDE)
        for x in range(SIDE)
    ]
    return lax.ppermute(value, "req", pairs)


def exchange(value):
    value = value.reshape((SIDE,) + (SIDE, BLOCK) + value.shape[1:])
    columns = [value[:, 0]] + [shifted(value[:, d], 0, d) for d in range(1, SIDE)]
    rows = jnp.stack(columns, axis=1)
    back = jnp.stack([rows[0]] + [shifted(rows[d], d, 0) for d in range(1, SIDE)])
    return back.reshape((ROWS,) + back.shape[3:])


def swapped(value):
    return lax.ppermute(value, "seq", [(0, 1), (1, 0)])


def shards(queries, w_absorb_k, w_absorb_v, prefill_pages, send_to, slot_of, lengths, new_latents):
    layer = lax.axis_index("seq")
    where = jnp.stack([lax.axis_index("group"), layer, lax.axis_index("req")]).astype(jnp.int32)

    sent = gather_pages(send_to[0, 0], prefill_pages[0, 0])
    pages = lax.all_to_all(sent, ("group", "seq"), split_axis=0, concat_axis=0, tiled=True)

    own_slot = slot_of[0, 0]
    nope, rope = split_queries(where, queries)
    heads = exchange(nope.reshape(ROWS, NOPE))
    latent = project(absorb_kernel, KV_RANK, where, heads, w_absorb_k, swapped(w_absorb_k))
    q_lat = exchange(latent)
    values = pick_values(where, w_absorb_v, swapped(w_absorb_v))

    fresh = lax.dynamic_index_in_dim(new_latents, layer, 0, keepdims=False)[0]
    fresh = jnp.pad(fresh, ((0, 16 - STEPS), (0, 0)))
    query = jnp.concatenate([q_lat, rope, jnp.zeros_like(rope)], axis=1)
    query, values = lax.optimization_barrier((query, values))
    latent_out = attend(where, lengths, own_slot, swapped(own_slot), query, fresh, pages)
    latent_heads = lax.all_to_all(latent_out, "req", split_axis=0, concat_axis=0, tiled=True)
    head_out = project_values(latent_heads.reshape(ROWS, KV_RANK), values)
    return lax.all_gather(head_out.reshape(PEERS, STEPS, HEADS_PER, VDIM), "seq", axis=0)


def solution(mesh):
    in_specs = (
        P(None, ("group", "req"), None, None, None),
        P(None, "req", None, "seq"),
        P(None, "req", "seq", None),
        P(("group", "seq"), "req", None, None, None, None),
        P(("group", "seq"), "req", None),
        P(("group", "seq"), "req", None),
        P(("group", "req")),
        P(None, ("group", "req"), None, None),
    )
    out_specs = P(None, "group", None, "req", None)
    return jax.shard_map(shards, mesh=mesh, in_specs=in_specs, out_specs=out_specs, check_vma=False)
```

time: 203 us -> 97.9 us (0.48)
  waiting for transfers between devices: 85.3 us -> 21.7 us
  blocking collectives: 45.6 us -> 20.7 us
  starting transfers between devices: 15.3 us -> 33 us
  local copies, waits for them, and re-layouts: 19.7 us -> 4.32 us
  Pallas kernels: 0 us -> 14.4 us
  between operations: 14.4 us -> 0.86 us
  other arithmetic: 15.4 us -> 2.59 us
  matrix products: 6.77 us -> 0 us
    all_to_all x2 -> x1, waiting for transfers between devices: 62 us -> 13.4 us  [shards(): lax.all_to_all(sent, ('group', 'seq'), split_axis=0, concat_axis=0, tiled...]
    all_gather x2 -> x0, waiting for transfers between devices: 23.3 us -> none  [the longest x1 15.6 us: shards(): latent_cols = lax.all_gather(latent_part, 'seq', axis=4, tiled=True)]
    ppermute x0 -> x15, starting transfers between devices: none -> 22.9 us  [the longest x12 16.4 us: shifted(): return lax.ppermute(value, 'req', pairs)]
    all_to_all x2 -> x1, blocking collectives: 34.9 us -> 17.1 us  [shards(): lax.all_to_all(latent_out, 'req', split_axis=0, concat_axis=0, tiled=True)]
    pallas_call x0 -> x6, Pallas kernels: none -> 14.4 us  [the longest x1 5.8 us: attend(): pl.pallas_call(attend_kernel, out_shape=jax.ShapeDtypeStruct((PEERS, BLOC...]
    ppermute x0 -> x15, waiting for transfers between devices: none -> 8.26 us  [the longest x12 8.25 us: shifted(): return lax.ppermute(value, 'req', pairs)]
    dot_general x10 -> x0, matrix products: 6.77 us -> none  [the longest x2 2.3 us: block_part(): lax.dot_general(flat_query, cache_keys, contract, preferred_element_type=...]
    gather x2 -> x0, local copies, waits for them, and re-layouts: 6.65 us -> none  [the longest x1 4.26 us: shards(): placed = jnp.take(incoming, jnp.argsort(slot_of[0, 0]), axis=1)]
  transfers between devices with their start and end apart: 4 -> 16, of which waited for: 4 -> 8; matrix products, arithmetic and copies ran while one was open for 8% -> 4% of each run, Pallas kernels for 0% -> 5%
where the time goes in v2:
time: 97.9 us; the launch traced here: 97.5 us
  starting transfers between devices  33 us (34%)
  waiting for transfers between devices  21.7 us (22%)
  blocking collectives  20.7 us (21%)
  Pallas kernels  14.4 us (15%)
  local copies, waits for them, and re-layouts  4.32 us (4%)
  other arithmetic  2.59 us (3%)
    all_to_all x1, blocking collectives, shards(): lax.all_to_all(latent_out, 'req', split_axis=0, concat_axis=0, tiled=True)  17.1 us
    ppermute x12, starting transfers between devices, shifted(): return lax.ppermute(value, 'req', pairs)  16.4 us
    all_to_all x1, waiting for transfers between devices, shards(): lax.all_to_all(sent, ('group', 'seq'), split_axis=0, concat_axis=0, tiled...  13.4 us
    all_to_all x1, starting transfers between devices, shards(): lax.all_to_all(sent, ('group', 'seq'), split_axis=0, concat_axis=0, tiled...  10.1 us
    ppermute x12, waiting for transfers between devices, shifted(): return lax.ppermute(value, 'req', pairs)  8.25 us
    ppermute x3, starting transfers between devices, swapped(): return lax.ppermute(value, 'seq', [(0, 1), (1, 0)])  6.48 us
    pallas_call x1, Pallas kernels, attend(): pl.pallas_call(attend_kernel, out_shape=jax.ShapeDtypeStruct((PEERS, BLOC...  5.8 us
    all_gather x1, blocking collectives, shards(): lax.all_gather(head_out.reshape(PEERS, STEPS, HEADS_PER, VDIM), 'seq', ax...  3.6 us
  transfers between devices with their start and end apart: 16, of which 8 were waited for; matrix products, arithmetic and copies ran while one was open for 4% of the time, Pallas kernels for 5%

profile of v2, /device:TPU:1, one launch (start us, length us, event | category | flops | bytes accessed | tf_op | source)
XLA Modules:
  0.0 97.5 jit_solution(6618732075838646375)
XLA Ops:
  0.0 3.3 %shard_map.85 = bf16[16,144,512]{2,1,0:T(8,128)(2,1)} custom-call(s32[16]{0:T(128)} %bitcast.78, bf16[2,16,64,576]{3,2,1,0:T(8,128)(2,1)} %bitcast.67), custom_call_target="tpu_custom_call" | custom-call | bytes 5242880 | tf_op jit(solution)/shard_map/pallas_call | solution.py:79
  3.3 10.1 %all-to-all-start = ((bf16[16,144,512]{2,1,0:T(8,128)(2,1)}), bf16[16,144,512]{2,1,0:T(8,128)(2,1)S(1)}, u32[]{:S(2)}, u32[]{:S(2)}) async-start(bf16[16,144,512]{2,1,0:T(8,128)(2,1)} %shard_map.85), calls=%async_computation | async-start | bytes 4718592 | tf_op jit(solution)/shard_map/all_to_all | solution.py:327
  13.9 0.7 shard_map.82
  14.6 2.6 %collective-permute-start.3 = (bf16[4,32,128]{2,1,0:T(8,128)(2,1)S(1)}, bf16[4,32,128]{2,1,0:T(8,128)(2,1)S(1)}, u32[]{:S(2)}, u32[]{:S(2)}) collective-permute-start(bf16[4,32,128]{2,1,0:T(8,128)(2,1)S(1)} %get-tuple-element.28), channel_id=1, source_target_pairs={{0,3},{1,0},{2,1},{3,2},{4,7},{5,4},{6,5},{7,6},{8,11},{9,8},{10,9... | collective-permute-start | bytes 98312 | tf_op jit(solution)/shard_map/ppermute | solution.py:307
  17.1 1.7 %collective-permute-start.2 = (bf16[4,32,128]{2,1,0:T(8,128)(2,1)S(1)}, bf16[4,32,128]{2,1,0:T(8,128)(2,1)S(1)}, u32[]{:S(2)}, u32[]{:S(2)}) collective-permute-start(bf16[4,32,128]{2,1,0:T(8,128)(2,1)S(1)} %get-tuple-element.26), channel_id=1, source_target_pairs={{0,2},{1,3},{2,0},{3,1},{4,6},{5,7},{6,4},{7,5},{8,10},{9,11},{10,... | collective-permute-start | bytes 98312 | tf_op jit(solution)/shard_map/ppermute | solution.py:307
  18.9 1.2 %collective-permute-start.14 = (bf16[2,8,256,128]{3,2,1,0:T(8,128)(2,1)}, bf16[2,8,256,128]{3,2,1,0:T(8,128)(2,1)}, u32[]{:S(2)}, u32[]{:S(2)}) collective-permute-start(bf16[2,8,256,128]{3,2,1,0:T(8,128)(2,1)} %own.3), channel_id=1, source_target_pairs={{0,16},{16,0},{1,17},{17,1},{2,18},{18,2},{3,19},{19,3},{4,20},{20... | collective-permute-start | bytes 3145736 | tf_op jit(solution)/shard_map/ppermute | solution.py:319
  20.0 1.4 %collective-permute-done.1 = bf16[4,32,128]{2,1,0:T(8,128)(2,1)S(1)} collective-permute-done((bf16[4,32,128]{2,1,0:T(8,128)(2,1)S(1)}, bf16[4,32,128]{2,1,0:T(8,128)(2,1)S(1)}, u32[]{:S(2)}, u32[]{:S(2)}) %collective-permute-start.1) | collective-permute-done | bytes 32800 | tf_op jit(solution)/shard_map/ppermute | solution.py:307
  21.5 0.4 collective-permute-done.2
  21.9 1.4 %collective-permute-start.4 = (bf16[4,32,128]{2,1,0:T(8,128)(2,1)S(1)}, bf16[4,32,128]{2,1,0:T(8,128)(2,1)S(1)}, u32[]{:S(2)}, u32[]{:S(2)}) collective-permute-start(bf16[4,32,128]{2,1,0:T(8,128)(2,1)S(1)} %get-tuple-element.24), channel_id=1, source_target_pairs={{0,4},{1,5},{2,6},{3,7},{4,8},{5,9},{6,10},{7,11},{8,12},{9,13},{1... | collective-permute-start | bytes 98312 | tf_op jit(solution)/shard_map/ppermute | solution.py:307
  23.3 2.6 %collective-permute-start.5 = (bf16[4,32,128]{2,1,0:T(8,128)(2,1)S(1)}, bf16[4,32,128]{2,1,0:T(8,128)(2,1)S(1)}, u32[]{:S(2)}, u32[]{:S(2)}) collective-permute-start(bf16[4,32,128]{2,1,0:T(8,128)(2,1)S(1)} %get-tuple-element.23), channel_id=1, source_target_pairs={{0,8},{1,9},{2,10},{3,11},{4,12},{5,13},{6,14},{7,15},{8,0},{9,1},... | collective-permute-start | bytes 98312 | tf_op jit(solution)/shard_map/ppermute | solution.py:307
  25.9 1.1 %collective-permute-start.6 = (bf16[4,32,128]{2,1,0:T(8,128)(2,1)S(1)}, bf16[4,32,128]{2,1,0:T(8,128)(2,1)S(1)}, u32[]{:S(2)}, u32[]{:S(2)}) collective-permute-start(bf16[4,32,128]{2,1,0:T(8,128)(2,1)S(1)} %get-tuple-element.22), channel_id=1, source_target_pairs={{0,12},{1,13},{2,14},{3,15},{4,0},{5,1},{6,2},{7,3},{8,4},{9,5},{1... | collective-permute-start | bytes 98312 | tf_op jit(solution)/shard_map/ppermute | solution.py:307
  27.0 0.9 collective-permute-done.5
  27.9 1.4 %collective-permute-done.6 = bf16[4,32,128]{2,1,0:T(8,128)(2,1)S(1)} collective-permute-done((bf16[4,32,128]{2,1,0:T(8,128)(2,1)S(1)}, bf16[4,32,128]{2,1,0:T(8,128)(2,1)S(1)}, u32[]{:S(2)}, u32[]{:S(2)}) %collective-permute-start.6) | collective-permute-done | bytes 32800 | tf_op jit(solution)/shard_map/ppermute | solution.py:307
  29.3 2.5 %shard_map.83 = bf16[512,512]{1,0:T(8,128)(2,1)S(1)} custom-call(s32[3]{0:T(128)S(1)} %pad_add_fusion.where, bf16[512,128]{1,0:T(8,128)(2,1)S(1)} %bitcast.63, bf16[2,8,128,256]{3,2,1,0:T(8,128)(2,1)} %own.2, bf16[2,8,128,256]{3,2,1,0:T(8,128)(2,1)} %collective-permute-done.7.got), custom_call_target="tpu_custom_call" | custom-call | flops 536870912 | bytes 2097152 | tf_op jit(solution)/shard_map/pallas_call | solution.py:204
  31.9 3.4 %collective-permute-start.9 = (bf16[4,32,512]{2,1,0:T(8,128)(2,1)S(1)}, bf16[4,32,512]{2,1,0:T(8,128)(2,1)S(1)}, u32[]{:S(2)}, u32[]{:S(2)}) collective-permute-start(bf16[4,32,512]{2,1,0:T(8,128)(2,1)S(1)} %get-tuple-element.18), channel_id=1, source_target_pairs={{0,2},{1,3},{2,0},{3,1},{4,6},{5,7},{6,4},{7,5},{8,10},{9,11},{10,... | collective-permute-start | bytes 393224 | tf_op jit(solution)/shard_map/ppermute | solution.py:307
  35.3 1.9 %collective-permute-done.8 = bf16[4,32,512]{2,1,0:T(8,128)(2,1)S(1)} collective-permute-done((bf16[4,32,512]{2,1,0:T(8,128)(2,1)S(1)}, bf16[4,32,512]{2,1,0:T(8,128)(2,1)S(1)}, u32[]{:S(2)}, u32[]{:S(2)}) %collective-permute-start.8) | collective-permute-done | bytes 131104 | tf_op jit(solution)/shard_map/ppermute | solution.py:307
  37.3 2.1 %collective-permute-done.9 = bf16[4,32,512]{2,1,0:T(8,128)(2,1)S(1)} collective-permute-done((bf16[4,32,512]{2,1,0:T(8,128)(2,1)S(1)}, bf16[4,32,512]{2,1,0:T(8,128)(2,1)S(1)}, u32[]{:S(2)}, u32[]{:S(2)}) %collective-permute-start.9) | collective-permute-done | bytes 131104 | tf_op jit(solution)/shard_map/ppermute | solution.py:307
  39.5 0.8 fusion
  40.5 3.3 %collective-permute-start.12 = (bf16[4,32,512]{2,1,0:T(8,128)(2,1)}, bf16[4,32,512]{2,1,0:T(8,128)(2,1)}, u32[]{:S(2)}, u32[]{:S(2)}) collective-permute-start(bf16[4,32,512]{2,1,0:T(8,128)(2,1)} %get-tuple-element.15), channel_id=1, source_target_pairs={{0,8},{1,9},{2,10},{3,11},{4,12},{5,13},{6,14},{7,15},{8,0},{9,1},... | collective-permute-start | bytes 393224 | tf_op jit(solution)/shard_map/ppermute | solution.py:307
  43.9 5.1 %collective-permute-start = (s32[16]{0:T(128)}, s32[16]{0:T(128)}, u32[]{:S(2)}, u32[]{:S(2)}) collective-permute-start(s32[16]{0:T(128)} %bitcast.3.own_slot), channel_id=1, source_target_pairs={{0,16},{16,0},{1,17},{17,1},{2,18},{18,2},{3,19},{19,3},{4,20},{20... | collective-permute-start | bytes 200 | tf_op jit(solution)/shard_map/ppermute | solution.py:319
  49.7 0.6 pad.4.fresh
  50.4 1.5 %shard_map.84.weight = bf16[4,512,256]{2,1,0:T(8,128)(2,1)S(1)} custom-call(s32[3]{0:T(128)S(1)} %pad_add_fusion.where, bf16[2,8,256,128]{3,2,1,0:T(8,128)(2,1)S(1)} %copy-done.1, bf16[2,8,256,128]{3,2,1,0:T(8,128)(2,1)} %collective-permute-done.14.got), custom_call_target="tpu_custom_call" | custom-call | bytes 3145728 | tf_op jit(solution)/shard_map/pallas_call | solution.py:167
  51.9 1.4 %pad_maximum_fusion.1 = bf16[4,4,32,512]{3,2,1,0:T(8,128)(2,1)S(1)} fusion(bf16[1,4,32,512]{3,2,1,0:T(8,128)(2,1)} %bitcast.30, bf16[1,4,32,512]{3,2,1,0:T(8,128)(2,1)} %bitcast.28, bf16[1,4,32,512]{3,2,1,0:T(8,128)(2,1)} %bitcast.26, bf16[1,4,32,512]{3,2,1,0:T(8,128)(2,1)S(1)} %copy-done.6), kind=kLoop, calls=%fused_computation.2 | loop fusion | flops 786432 | bytes 1048576 | tf_op jit(solution)/shard_map/stack | solution.py:314
  53.3 1.0 maximum_maximum_fusion.query
  54.3 13.4 %all-to-all-done.pages = bf16[16,144,512]{2,1,0:T(8,128)(2,1)S(1)} async-done(((bf16[16,144,512]{2,1,0:T(8,128)(2,1)}), bf16[16,144,512]{2,1,0:T(8,128)(2,1)S(1)}, u32[]{:S(2)}, u32[]{:S(2)}) %all-to-all-start) | async-done | bytes 2359328 | tf_op jit(solution)/shard_map/all_to_all | solution.py:327
  67.8 1.1 %copy-done.4 = bf16[512,640]{1,0:T(8,128)(2,1)S(1)} copy-done((bf16[512,640]{1,0:T(8,128)(2,1)S(1)}, bf16[512,640]{1,0:T(8,128)(2,1)}, u32[]{:S(2)}) %copy-start.4) | copy-done | bytes 655384
  68.9 0.7 copy-done.5
  69.6 5.8 %shard_map.86 = bf16[16,32,512]{2,1,0:T(8,128)(2,1)S(1)} custom-call(s32[3]{0:T(128)S(1)} %pad_add_fusion.where, s32[1]{0:T(128)S(6)} %copy.30.length, s32[16]{0:T(128)} %bitcast.3.own_slot, s32[16]{0:T(128)} %collective-permute-done.other_slot, bf16[512,640]{1,0:T(8,128)(2,1)S(1)} %copy-done.4, bf16[16,576]{1,0:T(8,128)(2,1)S(1)} %copy-done.5, ...), custom_call_target="tpu_custom_call" | custom-call | flops 2281701376 | bytes 4194304 | tf_op jit(solution)/shard_map/pallas_call | solution.py:283
  75.4 17.1 %all_to_all.10 = bf16[16,32,512]{2,1,0:T(8,128)(2,1)S(1)} all-to-all(bf16[16,32,512]{2,1,0:T(8,128)(2,1)S(1)} %shard_map.86), channel_id=1, replica_groups=mesh['group'=8,'seq'=2,'req'=16] {'req'}, dimensions={0} | all-to-all | bytes 1048576 | tf_op jit(solution)/shard_map/all_to_all | solution.py:341
  92.5 0.7 shard_map.87
  93.2 3.6 %all_gather.3 = bf16[2,16,4,8,128]{4,3,2,1,0:T(8,128)(2,1)S(1)} all-gather(bf16[1,16,4,8,128]{4,3,2,1,0:T(8,128)(2,1)S(1)} %bitcast.65), channel_id=1, replica_groups=mesh['group'=8,'seq'=2,'req'=16] {'seq'}, dimensions={0}, use_global_device_ids=true | all-gather | bytes 393216 | tf_op jit(solution)/shard_map/all_gather | solution.py:343
  96.8 0.7 copy.31
  (40 shorter events, 1.2 us)
Async XLA Ops:
  0.0 49.7 %copy-start = (bf16[2,1,4,576]{3,2,1,0:T(4,128)(2,1)S(1)}, bf16[2,1,4,576]{3,2,1,0:T(4,128)(2,1)}, u32[]{:S(2)}) copy-start(bf16[2,1,4,576]{3,2,1,0:T(4,128)(2,1)} %param.15) | copy-start | bytes 27652
  3.3 10.3 %copy-start.7 = (bf16[2,1,4,128,192]{3,4,2,1,0:T(8,128)(2,1)S(1)}, bf16[2,1,4,128,192]{3,4,2,1,0:T(8,128)(2,1)}, u32[]{:S(2)}) copy-start(bf16[2,1,4,128,192]{3,4,2,1,0:T(8,128)(2,1)} %param.8) | copy-start | bytes 1179652
  3.3 64.5 %all-to-all-start = ((bf16[16,144,512]{2,1,0:T(8,128)(2,1)}), bf16[16,144,512]{2,1,0:T(8,128)(2,1)S(1)}, u32[]{:S(2)}, u32[]{:S(2)}) async-start(bf16[16,144,512]{2,1,0:T(8,128)(2,1)} %shard_map.85), calls=%async_computation | async-start | bytes 4718592 | tf_op jit(solution)/shard_map/all_to_all | solution.py:327
  13.4 15.9 %collective-permute-start.7 = (bf16[2,8,128,256]{3,2,1,0:T(8,128)(2,1)}, bf16[2,8,128,256]{3,2,1,0:T(8,128)(2,1)}, u32[]{:S(2)}, u32[]{:S(2)}) collective-permute-start(bf16[2,8,128,256]{3,2,1,0:T(8,128)(2,1)} %own.2), channel_id=1, source_target_pairs={{0,16},{16,0},{1,17},{17,1},{2,18},{18,2},{3,19},{19,3},{4,20},{20... | collective-permute-start | bytes 3145736 | tf_op jit(solution)/shard_map/ppermute | solution.py:319
  14.6 5.5 %collective-permute-start.3 = (bf16[4,32,128]{2,1,0:T(8,128)(2,1)S(1)}, bf16[4,32,128]{2,1,0:T(8,128)(2,1)S(1)}, u32[]{:S(2)}, u32[]{:S(2)}) collective-permute-start(bf16[4,32,128]{2,1,0:T(8,128)(2,1)S(1)} %get-tuple-element.28), channel_id=1, source_target_pairs={{0,3},{1,0},{2,1},{3,2},{4,7},{5,4},{6,5},{7,6},{8,11},{9,8},{10,9... | collective-permute-start | bytes 98312 | tf_op jit(solution)/shard_map/ppermute | solution.py:307
  17.1 4.3 %collective-permute-start.1 = (bf16[4,32,128]{2,1,0:T(8,128)(2,1)S(1)}, bf16[4,32,128]{2,1,0:T(8,128)(2,1)S(1)}, u32[]{:S(2)}, u32[]{:S(2)}) collective-permute-start(bf16[4,32,128]{2,1,0:T(8,128)(2,1)S(1)} %get-tuple-element.27), channel_id=1, source_target_pairs={{0,1},{1,2},{2,3},{3,0},{4,5},{5,6},{6,7},{7,4},{8,9},{9,10},{10,1... | collective-permute-start | bytes 98312 | tf_op jit(solution)/shard_map/ppermute | solution.py:307
  17.1 4.7 %collective-permute-start.2 = (bf16[4,32,128]{2,1,0:T(8,128)(2,1)S(1)}, bf16[4,32,128]{2,1,0:T(8,128)(2,1)S(1)}, u32[]{:S(2)}, u32[]{:S(2)}) collective-permute-start(bf16[4,32,128]{2,1,0:T(8,128)(2,1)S(1)} %get-tuple-element.26), channel_id=1, source_target_pairs={{0,2},{1,3},{2,0},{3,1},{4,6},{5,7},{6,4},{7,5},{8,10},{9,11},{10,... | collective-permute-start | bytes 98312 | tf_op jit(solution)/shard_map/ppermute | solution.py:307
  18.9 31.5 %collective-permute-start.14 = (bf16[2,8,256,128]{3,2,1,0:T(8,128)(2,1)}, bf16[2,8,256,128]{3,2,1,0:T(8,128)(2,1)}, u32[]{:S(2)}, u32[]{:S(2)}) collective-permute-start(bf16[2,8,256,128]{3,2,1,0:T(8,128)(2,1)} %own.3), channel_id=1, source_target_pairs={{0,16},{16,0},{1,17},{17,1},{2,18},{18,2},{3,19},{19,3},{4,20},{20... | collective-permute-start | bytes 3145736 | tf_op jit(solution)/shard_map/ppermute | solution.py:319
  21.9 5.1 %collective-permute-start.4 = (bf16[4,32,128]{2,1,0:T(8,128)(2,1)S(1)}, bf16[4,32,128]{2,1,0:T(8,128)(2,1)S(1)}, u32[]{:S(2)}, u32[]{:S(2)}) collective-permute-start(bf16[4,32,128]{2,1,0:T(8,128)(2,1)S(1)} %get-tuple-element.24), channel_id=1, source_target_pairs={{0,4},{1,5},{2,6},{3,7},{4,8},{5,9},{6,10},{7,11},{8,12},{9,13},{1... | collective-permute-start | bytes 98312 | tf_op jit(solution)/shard_map/ppermute | solution.py:307
  23.3 4.6 %collective-permute-start.5 = (bf16[4,32,128]{2,1,0:T(8,128)(2,1)S(1)}, bf16[4,32,128]{2,1,0:T(8,128)(2,1)S(1)}, u32[]{:S(2)}, u32[]{:S(2)}) collective-permute-start(bf16[4,32,128]{2,1,0:T(8,128)(2,1)S(1)} %get-tuple-element.23), channel_id=1, source_target_pairs={{0,8},{1,9},{2,10},{3,11},{4,12},{5,13},{6,14},{7,15},{8,0},{9,1},... | collective-permute-start | bytes 98312 | tf_op jit(solution)/shard_map/ppermute | solution.py:307
  25.9 3.4 %collective-permute-start.6 = (bf16[4,32,128]{2,1,0:T(8,128)(2,1)S(1)}, bf16[4,32,128]{2,1,0:T(8,128)(2,1)S(1)}, u32[]{:S(2)}, u32[]{:S(2)}) collective-permute-start(bf16[4,32,128]{2,1,0:T(8,128)(2,1)S(1)} %get-tuple-element.22), channel_id=1, source_target_pairs={{0,12},{1,13},{2,14},{3,15},{4,0},{5,1},{6,2},{7,3},{8,4},{9,5},{1... | collective-permute-start | bytes 98312 | tf_op jit(solution)/shard_map/ppermute | solution.py:307
  31.8 18.5 %copy-start.1 = (bf16[2,8,256,128]{3,2,1,0:T(8,128)(2,1)S(1)}, bf16[2,8,256,128]{3,2,1,0:T(8,128)(2,1)}, u32[]{:S(2)}) copy-start(bf16[2,8,256,128]{3,2,1,0:T(8,128)(2,1)} %own.3) | copy-start | bytes 3145732
  31.9 5.4 %collective-permute-start.8 = (bf16[4,32,512]{2,1,0:T(8,128)(2,1)S(1)}, bf16[4,32,512]{2,1,0:T(8,128)(2,1)S(1)}, u32[]{:S(2)}, u32[]{:S(2)}) collective-permute-start(bf16[4,32,512]{2,1,0:T(8,128)(2,1)S(1)} %get-tuple-element.19), channel_id=1, source_target_pairs={{0,1},{1,2},{2,3},{3,0},{4,5},{5,6},{6,7},{7,4},{8,9},{9,10},{10,1... | collective-permute-start | bytes 393224 | tf_op jit(solution)/shard_map/ppermute | solution.py:307
  31.9 7.4 %collective-permute-start.9 = (bf16[4,32,512]{2,1,0:T(8,128)(2,1)S(1)}, bf16[4,32,512]{2,1,0:T(8,128)(2,1)S(1)}, u32[]{:S(2)}, u32[]{:S(2)}) collective-permute-start(bf16[4,32,512]{2,1,0:T(8,128)(2,1)S(1)} %get-tuple-element.18), channel_id=1, source_target_pairs={{0,2},{1,3},{2,0},{3,1},{4,6},{5,7},{6,4},{7,5},{8,10},{9,11},{10,... | collective-permute-start | bytes 393224 | tf_op jit(solution)/shard_map/ppermute | solution.py:307
  35.3 4.1 %collective-permute-start.10 = (bf16[4,32,512]{2,1,0:T(8,128)(2,1)S(1)}, bf16[4,32,512]{2,1,0:T(8,128)(2,1)S(1)}, u32[]{:S(2)}, u32[]{:S(2)}) collective-permute-start(bf16[4,32,512]{2,1,0:T(8,128)(2,1)S(1)} %get-tuple-element.20), channel_id=1, source_target_pairs={{0,3},{1,0},{2,1},{3,2},{4,7},{5,4},{6,5},{7,6},{8,11},{9,8},{10,9... | collective-permute-start | bytes 393224 | tf_op jit(solution)/shard_map/ppermute | solution.py:307
  40.3 11.6 %collective-permute-start.11 = (bf16[4,32,512]{2,1,0:T(8,128)(2,1)}, bf16[4,32,512]{2,1,0:T(8,128)(2,1)}, u32[]{:S(2)}, u32[]{:S(2)}) collective-permute-start(bf16[4,32,512]{2,1,0:T(8,128)(2,1)} %get-tuple-element.16), channel_id=1, source_target_pairs={{0,4},{1,5},{2,6},{3,7},{4,8},{5,9},{6,10},{7,11},{8,12},{9,13},{1... | collective-permute-start | bytes 393224 | tf_op jit(solution)/shard_map/ppermute | solution.py:307
  40.5 11.4 %collective-permute-start.12 = (bf16[4,32,512]{2,1,0:T(8,128)(2,1)}, bf16[4,32,512]{2,1,0:T(8,128)(2,1)}, u32[]{:S(2)}, u32[]{:S(2)}) collective-permute-start(bf16[4,32,512]{2,1,0:T(8,128)(2,1)} %get-tuple-element.15), channel_id=1, source_target_pairs={{0,8},{1,9},{2,10},{3,11},{4,12},{5,13},{6,14},{7,15},{8,0},{9,1},... | collective-permute-start | bytes 393224 | tf_op jit(solution)/shard_map/ppermute | solution.py:307
  43.8 8.1 %collective-permute-start.13 = (bf16[4,32,512]{2,1,0:T(8,128)(2,1)}, bf16[4,32,512]{2,1,0:T(8,128)(2,1)}, u32[]{:S(2)}, u32[]{:S(2)}) collective-permute-start(bf16[4,32,512]{2,1,0:T(8,128)(2,1)} %get-tuple-element.14), channel_id=1, source_target_pairs={{0,12},{1,13},{2,14},{3,15},{4,0},{5,1},{6,2},{7,3},{8,4},{9,5},{1... | collective-permute-start | bytes 393224 | tf_op jit(solution)/shard_map/ppermute | solution.py:307
  43.9 10.4 %collective-permute-start = (s32[16]{0:T(128)}, s32[16]{0:T(128)}, u32[]{:S(2)}, u32[]{:S(2)}) collective-permute-start(s32[16]{0:T(128)} %bitcast.3.own_slot), channel_id=1, source_target_pairs={{0,16},{16,0},{1,17},{17,1},{2,18},{18,2},{3,19},{19,3},{4,20},{20... | collective-permute-start | bytes 200 | tf_op jit(solution)/shard_map/ppermute | solution.py:319
  50.4 1.5 %copy-start.6 = (bf16[1,4,32,512]{3,2,1,0:T(8,128)(2,1)S(1)}, bf16[1,4,32,512]{3,2,1,0:T(8,128)(2,1)}, u32[]{:S(2)}) copy-start(bf16[1,4,32,512]{3,2,1,0:T(8,128)(2,1)} %get-tuple-element.13) | copy-start | bytes 393220
  51.8 2.5 %copy-start.2 = (bf16[4,512,256]{2,1,0:T(8,128)(2,1)}, bf16[4,512,256]{2,1,0:T(8,128)(2,1)S(1)}, u32[]{:S(2)}) copy-start(bf16[4,512,256]{2,1,0:T(8,128)(2,1)S(1)} %shard_map.84.weight) | copy-start | bytes 3145732
  54.3 38.2 %copy-start.3 = (bf16[4,512,256]{2,1,0:T(8,128)(2,1)S(1)}, bf16[4,512,256]{2,1,0:T(8,128)(2,1)}, u32[]{:S(2)}) copy-start(bf16[4,512,256]{2,1,0:T(8,128)(2,1)} %copy-done.2) | copy-start | bytes 3145732
  67.8 1.1 %copy-start.4 = (bf16[512,640]{1,0:T(8,128)(2,1)S(1)}, bf16[512,640]{1,0:T(8,128)(2,1)}, u32[]{:S(2)}) copy-start(bf16[512,640]{1,0:T(8,128)(2,1)} %maximum_maximum_fusion.query) | copy-start | bytes 1966084
  68.9 0.7 copy-start.5

commit v3 on v2

--- a/solution.py
+++ b/solution.py
@@ -21,6 +21,7 @@
 PAIR_ROWS = PAIR + 16
 BLOCK = HEADS_PER * STEPS
 ROWS = PEERS * BLOCK
+TILE = 512
 HALF = KV_RANK // 2
 DEAD = -1e30
 SCALE = 1.0 / math.sqrt(NOPE + ROPE)
@@ -166,7 +167,7 @@
 def pick_values(where, own, got):
     return pl.pallas_call(
         pick_values_kernel,
-        out_shape=jax.ShapeDtypeStruct((HEADS_PER // 2, KV_RANK, 2 * VDIM), jnp.bfloat16),
+        out_shape=jax.ShapeDtypeStruct((HEADS_PER // 2 + 1, KV_RANK, 2 * VDIM), jnp.bfloat16),
         in_specs=[SMEM, VMEM, VMEM],
         out_specs=VMEM,
         compiler_params=pltpu.CompilerParams(vmem_limit_bytes=16 << 20),
@@ -221,81 +222,73 @@
     return lax.dot_general(a, b, (((1,), (1,)), ((), ())), preferred_element_type=jnp.float32)
 
 
-def attend_kernel(where, length, own_slot, other_slot, query, fresh, pages, out, ropes, scores, result, out_sem):
-    layer = where[1]
-
-    def store(j):
-        return pltpu.make_async_copy(
-            result.at[pl.ds(j * BLOCK, BLOCK)], out.at[around(where[2], j, -1)], out_sem.at[j]
-        )
-
-    lane = lax.broadcasted_iota(jnp.int32, (1, PAIR), 1)
-
-    def live_of(source):
-        mine, theirs = own_slot[source] * PAGE, other_slot[source] * PAGE
-        first = jnp.where(layer == 0, mine, theirs)
-        second = jnp.where(layer == 0, theirs, mine) + BLOCK_KEYS
-        return lane < jnp.where(lane < PAGE, length[0] - first, length[0] - second + PAGE)
-
+def attend_kernel(where, inputs, pages, out, ropes, scores):
     for p in range(PEERS):
         for k in range(8):
             ropes[p * PAIR + 16 * k : p * PAIR + 16 * k + 16, :] = pages[
                 p, PAIR:PAIR_ROWS, ROPE * k : ROPE * k + ROPE
             ]
-    ql, qr = query[:, :KV_RANK], query[:, KV_RANK : KV_RANK + ROPE]
-    step = lax.rem(lax.broadcasted_iota(jnp.int32, (ROWS, 16), 0) // HEADS_PER, STEPS)
-    key = lax.broadcasted_iota(jnp.int32, (ROWS, 16), 1)
-    lat, rope = fresh[:, :KV_RANK], fresh[:, KV_RANK:]
-    extra = jnp.where(key <= step, dot_rows(ql, lat) + dot_rows(qr, rope), DEAD)
     width = 2 * PAIR
-    highest = jnp.full((ROWS, PAIR), DEAD, jnp.float32)
-    for n in range(0, PEERS, 2):
-        part = slice(n * PAIR, n * PAIR + width)
-        lat = pages[n : n + 2, :PAIR, :].reshape(width, KV_RANK)
-        s = dot_rows(ql, lat) + dot_rows(qr, ropes[part, :])
-        s = jnp.where(jnp.concatenate([live_of(n), live_of(n + 1)], axis=1), s, DEAD)
-        scores[:, part] = s
-        highest = jnp.maximum(highest, jnp.maximum(s[:, :PAIR], s[:, PAIR:]))
-    peak = jnp.maximum(
-        jnp.max(extra, axis=1, keepdims=True), jnp.max(highest, axis=1, keepdims=True)
-    )
-    weight = jnp.exp2((extra - peak) * TO_LOG2).astype(jnp.bfloat16)
-    total = jnp.sum(weight.astype(jnp.float32), axis=1, keepdims=True)
-    summed = jnp.dot(weight, fresh[:, :KV_RANK], preferred_element_type=jnp.float32)
-    added = jnp.zeros((ROWS, PAIR), jnp.float32)
-    for n in range(0, PEERS, 2):
-        part = slice(n * PAIR, n * PAIR + width)
-        lat = pages[n : n + 2, :PAIR, :].reshape(width, KV_RANK)
-        weight = jnp.exp2((scores[:, part] - peak) * TO_LOG2).astype(jnp.bfloat16)
-        kept = weight.astype(jnp.float32)
-        added = added + (kept[:, :PAIR] + kept[:, PAIR:])
-        summed = summed + jnp.dot(weight, lat, preferred_element_type=jnp.float32)
-    total = total + jnp.sum(added, axis=1, keepdims=True)
-    result[...] = (summed * (1.0 / total)).astype(jnp.bfloat16)
-    for j in range(PEERS):
-        store(j).start()
-    for j in range(PEERS):
-        store(j).wait()
-
-
-def attend(*args):
+    fresh = inputs[ROWS : ROWS + 16, :KV_RANK]
+    fresh_rope = inputs[ROWS : ROWS + 16, KV_RANK : KV_RANK + ROPE]
+    live = inputs[ROWS + 16 :, :PAIR].astype(jnp.float32) > 0.5
+
+    def tile(first):
+        rows = pl.ds(first, TILE)
+        ql, qr = inputs[rows, :KV_RANK], inputs[rows, KV_RANK : KV_RANK + ROPE]
+        row = lax.broadcasted_iota(jnp.int32, (TILE, 16), 0)
+        key = lax.broadcasted_iota(jnp.int32, (TILE, 16), 1)
+        extra = dot_rows(ql, fresh) + dot_rows(qr, fresh_rope)
+        extra = jnp.where(key <= lax.rem(row // HEADS_PER, STEPS), extra, DEAD)
+        highest = jnp.full((TILE, PAIR), DEAD, jnp.float32)
+        for n in range(0, PEERS, 2):
+            part = slice(n * PAIR, n * PAIR + width)
+            lat = pages[n : n + 2, :PAIR, :].reshape(width, KV_RANK)
+            s = dot_rows(ql, lat) + dot_rows(qr, ropes[part, :])
+            bound = jnp.concatenate([live[n : n + 1], live[n + 1 : n + 2]], axis=1)
+            s = jnp.where(bound, s, DEAD)
+            scores[:, part] = s
+            highest = jnp.maximum(highest, jnp.maximum(s[:, :PAIR], s[:, PAIR:]))
+        peak = jnp.maximum(
+            jnp.max(extra, axis=1, keepdims=True), jnp.max(highest, axis=1, keepdims=True)
+        )
+        weight = jnp.exp2((extra - peak) * TO_LOG2).astype(jnp.bfloat16)
+        total = jnp.sum(weight.astype(jnp.float32), axis=1, keepdims=True)
+        summed = jnp.dot(weight, fresh, preferred_element_type=jnp.float32)
+        added = jnp.zeros((TILE, PAIR), jnp.float32)
+        for n in range(0, PEERS, 2):
+            part = slice(n * PAIR, n * PAIR + width)
+            lat = pages[n : n + 2, :PAIR, :].reshape(width, KV_RANK)
+            weight = jnp.exp2((scores[:, part] - peak) * TO_LOG2).astype(jnp.bfloat16)
+            kept = weight.astype(jnp.float32)
+            added = added + (kept[:, :PAIR] + kept[:, PAIR:])
+            summed = summed + jnp.dot(weight, lat, preferred_element_type=jnp.float32)
+        total = total + jnp.sum(added, axis=1, keepdims=True)
+        result = (summed * (1.0 / total)).astype(jnp.bfloat16)
+        for k in range(TILE // BLOCK):
+            j = around(where[2], first // BLOCK + k, -1)
+            out[j] = result[k * BLOCK : (k + 1) * BLOCK]
+
+    for first in range(0, ROWS, TILE):
+        tile(first)
+
+
+def attend(where, inputs, pages):
     keys = PEERS * PAIR
     return pl.pallas_call(
         attend_kernel,
         out_shape=jax.ShapeDtypeStruct((PEERS, BLOCK, KV_RANK), jnp.bfloat16),
-        in_specs=[SMEM] * 4 + [VMEM] * 3,
-        out_specs=ANY,
+        in_specs=[SMEM, VMEM, VMEM],
+        out_specs=VMEM,
         scratch_shapes=[
             pltpu.VMEM((keys, ROPE), jnp.bfloat16),
-            pltpu.VMEM((ROWS, keys), jnp.float32),
-            pltpu.VMEM((ROWS, KV_RANK), jnp.bfloat16),
-            pltpu.SemaphoreType.DMA((PEERS,)),
+            pltpu.VMEM((TILE, keys), jnp.float32),
         ],
         compiler_params=pltpu.CompilerParams(vmem_limit_bytes=40 << 20),
         cost_estimate=pl.CostEstimate(
             flops=2 * ROWS * keys * 1088, bytes_accessed=4 << 20, transcendentals=ROWS * keys
         ),
-    )(*args)
+    )(where, inputs, pages)
 
 
 def shifted(value, dy, dx):
@@ -334,10 +327,19 @@
     values = pick_values(where, w_absorb_v, swapped(w_absorb_v))
 
     fresh = lax.dynamic_index_in_dim(new_latents, layer, 0, keepdims=False)[0]
-    fresh = jnp.pad(fresh, ((0, 16 - STEPS), (0, 0)))
-    query = jnp.concatenate([q_lat, rope, jnp.zeros_like(rope)], axis=1)
-    query, values = lax.optimization_barrier((query, values))
-    latent_out = attend(where, lengths, own_slot, swapped(own_slot), query, fresh, pages)
+    slots = jnp.stack([own_slot, swapped(own_slot)])
+    slots = jnp.where(layer == 0, slots, slots[::-1])
+    starts = slots.T * PAGE + jnp.arange(2, dtype=jnp.int32) * BLOCK_KEYS
+    live = starts[:, :, None] + jnp.arange(PAGE, dtype=jnp.int32) < lengths[0]
+    inputs = jnp.concatenate(
+        [
+            jnp.concatenate([q_lat, rope, jnp.zeros_like(rope)], axis=1),
+            jnp.pad(fresh, ((0, 16 - STEPS), (0, ROPE))),
+            jnp.pad(live.reshape(PEERS, PAIR).astype(jnp.bfloat16), ((0, 0), (0, KV_RANK))),
+        ]
+    )
+    inputs, values = lax.optimization_barrier((inputs, values))
+    latent_out = attend(where, inputs, pages)
     latent_heads = lax.all_to_all(latent_out, "req", split_axis=0, concat_axis=0, tiled=True)
     head_out = project_values(latent_heads.reshape(ROWS, KV_RANK), values)
     return lax.all_gather(head_out.reshape(PEERS, STEPS, HEADS_PER, VDIM), "seq", axis=0)

time: 97.9 us -> 94.9 us (0.969)
  starting transfers between devices: 33 us -> 25.8 us
  local copies, waits for them, and re-layouts: 4.32 us -> 8.76 us
  Pallas kernels: 14.4 us -> 13.1 us
  other arithmetic: 2.59 us -> 3.88 us
    ppermute x3, starting transfers between devices: 6.48 us -> 1.52 us  [swapped(): return lax.ppermute(value, 'seq', [(0, 1), (1, 0)])]
    add x0 -> x5, local copies, waits for them, and re-layouts: none -> 4.66 us  [the longest x4 3.33 us: shards(): live = starts[:, :, None] + jnp.arange(PAGE, dtype=jnp.int32) < lengths[0]]
    ppermute x12, starting transfers between devices: 16.4 us -> 14.2 us  [shifted(): return lax.ppermute(value, 'req', pairs)]
    ppermute x12, waiting for transfers between devices: 8.25 us -> 6.64 us  [shifted(): return lax.ppermute(value, 'req', pairs)]
    another operation x2, other arithmetic: 1.46 us -> 0.09 us  [exchange(): jnp.stack([rows[0]] + [shifted(rows[d], d, 0) for d in range(1, SIDE)])]
    add x0 -> x1, other arithmetic: none -> 1.26 us  [shards(): starts = slots.T * PAGE + jnp.arange(2, dtype=jnp.int32) * BLOCK_KEYS]
    all_to_all x1, waiting for transfers between devices: 13.4 us -> 14.7 us  [shards(): lax.all_to_all(sent, ('group', 'seq'), split_axis=0, concat_axis=0, tiled...]
    pallas_call x1, Pallas kernels: 5.8 us -> 4.62 us  [attend(): pl.pallas_call(attend_kernel, out_shape=jax.ShapeDtypeStruct((PEERS, BLOC...]
  transfers between devices with their start and end apart: 16 -> 16, of which waited for: 8 -> 6; matrix products, arithmetic and copies ran while one was open for 4% -> 11% of each run, Pallas kernels for 5% -> 5%
where the time goes in v3:
time: 94.9 us; the launch traced here: 94.5 us
  starting transfers between devices  25.8 us (27%)
  waiting for transfers between devices  21.3 us (22%)
  blocking collectives  20.7 us (22%)
  Pallas kernels  13.1 us (14%)
  local copies, waits for them, and re-layouts  8.76 us (9%)
  other arithmetic  3.88 us (4%)
    all_to_all x1, blocking collectives, shards(): lax.all_to_all(latent_out, 'req', split_axis=0, concat_axis=0, tiled=True)  17.1 us
    all_to_all x1, waiting for transfers between devices, shards(): lax.all_to_all(sent, ('group', 'seq'), split_axis=0, concat_axis=0, tiled...  14.7 us
    ppermute x12, starting transfers between devices, shifted(): return lax.ppermute(value, 'req', pairs)  14.2 us
    all_to_all x1, starting transfers between devices, shards(): lax.all_to_all(sent, ('group', 'seq'), split_axis=0, concat_axis=0, tiled...  10.1 us
    ppermute x12, waiting for transfers between devices, shifted(): return lax.ppermute(value, 'req', pairs)  6.64 us
    pallas_call x1, Pallas kernels, attend(): pl.pallas_call(attend_kernel, out_shape=jax.ShapeDtypeStruct((PEERS, BLOC...  4.62 us
    all_gather x1, blocking collectives, shards(): lax.all_gather(head_out.reshape(PEERS, STEPS, HEADS_PER, VDIM), 'seq', ax...  3.58 us
    add x4, local copies, waits for them, and re-layouts, shards(): live = starts[:, :, None] + jnp.arange(PAGE, dtype=jnp.int32) < lengths[0]  3.33 us
  transfers between devices with their start and end apart: 16, of which 6 were waited for; matrix products, arithmetic and copies ran while one was open for 11% of the time, Pallas kernels for 5%

profile of v3, /device:TPU:1, one launch (start us, length us, event | category | flops | bytes accessed | tf_op | source)
XLA Modules:
  0.0 94.5 jit_solution(6631120183958948248)
XLA Ops:
  0.0 3.3 %shard_map.85 = bf16[16,144,512]{2,1,0:T(8,128)(2,1)} custom-call(s32[16]{0:T(128)} %bitcast.89, bf16[2,16,64,576]{3,2,1,0:T(8,128)(2,1)} %bitcast.73), custom_call_target="tpu_custom_call" | custom-call | bytes 5242880 | tf_op jit(solution)/shard_map/pallas_call | solution.py:80
  3.3 10.1 %all-to-all-start = ((bf16[16,144,512]{2,1,0:T(8,128)(2,1)}), bf16[16,144,512]{2,1,0:T(8,128)(2,1)S(1)}, u32[]{:S(2)}, u32[]{:S(2)}) async-start(bf16[16,144,512]{2,1,0:T(8,128)(2,1)} %shard_map.85), calls=%async_computation | async-start | bytes 4718592 | tf_op jit(solution)/shard_map/all_to_all | solution.py:320
  14.3 0.7 shard_map.82
  15.0 2.9 %collective-permute-start.1 = (bf16[4,32,128]{2,1,0:T(8,128)(2,1)S(1)}, bf16[4,32,128]{2,1,0:T(8,128)(2,1)S(1)}, u32[]{:S(2)}, u32[]{:S(2)}) collective-permute-start(bf16[4,32,128]{2,1,0:T(8,128)(2,1)S(1)} %get-tuple-element.26), channel_id=1, source_target_pairs={{0,2},{1,3},{2,0},{3,1},{4,6},{5,7},{6,4},{7,5},{8,10},{9,11},{10,... | collective-permute-start | bytes 98312 | tf_op jit(solution)/shard_map/ppermute | solution.py:300
  18.2 2.4 %collective-permute-start.2 = (bf16[4,32,128]{2,1,0:T(8,128)(2,1)S(1)}, bf16[4,32,128]{2,1,0:T(8,128)(2,1)S(1)}, u32[]{:S(2)}, u32[]{:S(2)}) collective-permute-start(bf16[4,32,128]{2,1,0:T(8,128)(2,1)S(1)} %get-tuple-element.28), channel_id=1, source_target_pairs={{0,3},{1,0},{2,1},{3,2},{4,7},{5,4},{6,5},{7,6},{8,11},{9,8},{10,9... | collective-permute-start | bytes 98312 | tf_op jit(solution)/shard_map/ppermute | solution.py:300
  22.9 0.9 collective-permute-start.14
  23.9 2.8 %collective-permute-start.5 = (bf16[4,32,128]{2,1,0:T(8,128)(2,1)S(1)}, bf16[4,32,128]{2,1,0:T(8,128)(2,1)S(1)}, u32[]{:S(2)}, u32[]{:S(2)}) collective-permute-start(bf16[4,32,128]{2,1,0:T(8,128)(2,1)S(1)} %get-tuple-element.22), channel_id=1, source_target_pairs={{0,12},{1,13},{2,14},{3,15},{4,0},{5,1},{6,2},{7,3},{8,4},{9,5},{1... | collective-permute-start | bytes 98312 | tf_op jit(solution)/shard_map/ppermute | solution.py:300
  27.1 0.7 collective-permute-start.3
  27.8 0.6 rev.3
  28.4 2.9 %collective-permute-done.4 = bf16[4,32,128]{2,1,0:T(8,128)(2,1)S(1)} collective-permute-done((bf16[4,32,128]{2,1,0:T(8,128)(2,1)S(1)}, bf16[4,32,128]{2,1,0:T(8,128)(2,1)S(1)}, u32[]{:S(2)}, u32[]{:S(2)}) %collective-permute-start.4) | collective-permute-done | bytes 32800 | tf_op jit(solution)/shard_map/ppermute | solution.py:300
  31.7 2.5 %shard_map.83 = bf16[512,512]{1,0:T(8,128)(2,1)S(1)} custom-call(s32[3]{0:T(128)S(1)} %pad_add_fusion.1.where, bf16[512,128]{1,0:T(8,128)(2,1)S(1)} %bitcast.69, bf16[2,8,128,256]{3,2,1,0:T(8,128)(2,1)} %own.2, bf16[2,8,128,256]{3,2,1,0:T(8,128)(2,1)} %collective-permute-done.6.got), custom_call_target="tpu_custom_call" | custom-call | flops 536870912 | bytes 2097152 | tf_op jit(solution)/shard_map/pallas_call | solution.py:205
  34.2 0.8 fusion.5
  35.0 1.5 %collective-permute-start.7 = (bf16[4,32,512]{2,1,0:T(8,128)(2,1)}, bf16[4,32,512]{2,1,0:T(8,128)(2,1)}, u32[]{:S(2)}, u32[]{:S(2)}) collective-permute-start(bf16[4,32,512]{2,1,0:T(8,128)(2,1)} %get-tuple-element.19), channel_id=1, source_target_pairs={{0,1},{1,2},{2,3},{3,0},{4,5},{5,6},{6,7},{7,4},{8,9},{9,10},{10,1... | collective-permute-start | bytes 393224 | tf_op jit(solution)/shard_map/ppermute | solution.py:300
  36.5 1.2 %collective-permute-start.9 = (bf16[4,32,512]{2,1,0:T(8,128)(2,1)}, bf16[4,32,512]{2,1,0:T(8,128)(2,1)}, u32[]{:S(2)}, u32[]{:S(2)}) collective-permute-start(bf16[4,32,512]{2,1,0:T(8,128)(2,1)} %get-tuple-element.20), channel_id=1, source_target_pairs={{0,3},{1,0},{2,1},{3,2},{4,7},{5,4},{6,5},{7,6},{8,11},{9,8},{10,9... | collective-permute-start | bytes 393224 | tf_op jit(solution)/shard_map/ppermute | solution.py:300
  37.7 1.3 %add_bitcast_fusion = s32[16,2]{0,1:T(2,128)} fusion(s32[2,16]{1,0:T(2,128)S(1)} %copy-done.7, pred[]{:T(512)S(6)} %eq.3, s32[2]{0:T(128)S(1)} %copy-done.11, s32[1,16]{1,0:T(1,128)} %bitcast.88, s32[1,16]{1,0:T(1,128)S(1)} %bitcast.86), kind=kLoop, calls=%fused_computation.26 | loop fusion | flops 128 | bytes 393 | tf_op jit(solution)/shard_map/add | solution.py:332
  38.9 1.3 %copy.24 = s32[16,2]{1,0:T(8,128)} copy(s32[16,2]{0,1:T(2,128)} %add_bitcast_fusion) | data formatting | bytes 256 | tf_op jit(solution)/shard_map/add | solution.py:332
  40.3 1.4 %add.41 = s32[16,2,64]{2,1,0:T(2,128)} broadcast(s32[16,2]{1,0:T(8,128)} %copy.24), dimensions={0,1} | broadcast | bytes 8320 | tf_op jit(solution)/shard_map/add | solution.py:333
  41.6 1.4 %add.42 = s32[16,128]{1,0:T(8,128)} reshape(s32[16,2,64]{2,1,0:T(2,128)} %add.41) | data formatting | bytes 16384 | tf_op jit(solution)/shard_map/add | solution.py:333
  43.0 0.9 collective-permute-done.7
  43.9 1.2 %pad_maximum_fusion = bf16[4,4,32,512]{3,2,1,0:T(8,128)(2,1)S(1)} fusion(bf16[4,1,32,512]{3,2,1,0:T(8,128)(2,1)} %bitcast.23, bf16[4,1,32,512]{3,2,1,0:T(8,128)(2,1)} %bitcast.21, bf16[4,1,32,512]{3,2,1,0:T(8,128)(2,1)} %bitcast.19, bf16[4,1,32,512]{3,2,1,0:T(8,128)(2,1)} %get-tuple-element.17), kind=kLoop, calls=%fused_computation.6 | loop fusion | flops 786432 | bytes 1048576 | tf_op jit(solution)/shard_map/stack | solution.py:306
  45.5 1.0 %collective-permute-start.11 = (bf16[4,32,512]{2,1,0:T(8,128)(2,1)S(1)}, bf16[4,32,512]{2,1,0:T(8,128)(2,1)S(1)}, u32[]{:S(2)}, u32[]{:S(2)}) collective-permute-start(bf16[4,32,512]{2,1,0:T(8,128)(2,1)S(1)} %get-tuple-element.15), channel_id=1, source_target_pairs={{0,8},{1,9},{2,10},{3,11},{4,12},{5,13},{6,14},{7,15},{8,0},{9,1},... | collective-permute-start | bytes 393224 | tf_op jit(solution)/shard_map/ppermute | solution.py:300
  46.5 0.8 collective-permute-start.10
  47.9 1.4 %shard_map.84.weight = bf16[5,512,256]{2,1,0:T(8,128)(2,1)S(1)} custom-call(s32[3]{0:T(128)S(1)} %pad_add_fusion.1.where, bf16[2,8,256,128]{3,2,1,0:T(8,128)(2,1)S(1)} %copy-done.3, bf16[2,8,256,128]{3,2,1,0:T(8,128)(2,1)} %collective-permute-done.14.got), custom_call_target="tpu_custom_call" | custom-call | bytes 3145728 | tf_op jit(solution)/shard_map/pallas_call | solution.py:168
  49.3 1.1 %copy-done.1 = bf16[5,512,256]{2,1,0:T(8,128)(2,1)} copy-done((bf16[5,512,256]{2,1,0:T(8,128)(2,1)}, bf16[5,512,256]{2,1,0:T(8,128)(2,1)S(1)}, u32[]{:S(2)}) %copy-start.1) | copy-done | bytes 1310744
  50.4 0.8 collective-permute-done.11
  51.1 1.7 %collective-permute-done.10 = bf16[4,32,512]{2,1,0:T(8,128)(2,1)S(1)} collective-permute-done((bf16[4,32,512]{2,1,0:T(8,128)(2,1)S(1)}, bf16[4,32,512]{2,1,0:T(8,128)(2,1)S(1)}, u32[]{:S(2)}, u32[]{:S(2)}) %collective-permute-start.10) | collective-permute-done | bytes 131104 | tf_op jit(solution)/shard_map/ppermute | solution.py:300
  53.1 14.7 %all-to-all-done.pages = bf16[16,144,512]{2,1,0:T(8,128)(2,1)S(1)} async-done(((bf16[16,144,512]{2,1,0:T(8,128)(2,1)}), bf16[16,144,512]{2,1,0:T(8,128)(2,1)S(1)}, u32[]{:S(2)}, u32[]{:S(2)}) %all-to-all-start) | async-done | bytes 2359328 | tf_op jit(solution)/shard_map/all_to_all | solution.py:320
  67.8 4.6 %shard_map.86 = bf16[16,32,512]{2,1,0:T(8,128)(2,1)S(1)} custom-call(s32[3]{0:T(128)S(1)} %pad_add_fusion.1.where, bf16[544,640]{1,0:T(8,128)(2,1)S(1)} %fusion.3.inputs, bf16[16,144,512]{2,1,0:T(8,128)(2,1)S(1)} %all-to-all-done.pages), custom_call_target="tpu_custom_call" | custom-call | flops 2281701376 | bytes 4194304 | tf_op jit(solution)/shard_map/pallas_call | solution.py:278
  72.4 17.1 %all_to_all.10 = bf16[16,32,512]{2,1,0:T(8,128)(2,1)S(1)} all-to-all(bf16[16,32,512]{2,1,0:T(8,128)(2,1)S(1)} %shard_map.86), channel_id=1, replica_groups=mesh['group'=8,'seq'=2,'req'=16] {'req'}, dimensions={0} | all-to-all | bytes 1048576 | tf_op jit(solution)/shard_map/all_to_all | solution.py:343
  89.5 0.7 shard_map.87
  90.2 3.6 %all_gather.3 = bf16[2,16,4,8,128]{4,3,2,1,0:T(8,128)(2,1)S(1)} all-gather(bf16[1,16,4,8,128]{4,3,2,1,0:T(8,128)(2,1)S(1)} %bitcast.71), channel_id=1, replica_groups=mesh['group'=8,'seq'=2,'req'=16] {'seq'}, dimensions={0}, use_global_device_ids=true | all-gather | bytes 393216 | tf_op jit(solution)/shard_map/all_gather | solution.py:345
  93.8 0.7 copy.33
  (57 shorter events, 5.0 us)
Async XLA Ops:
  0.0 20.5 %copy-start = (bf16[2,1,4,576]{3,2,1,0:T(4,128)(2,1)S(1)}, bf16[2,1,4,576]{3,2,1,0:T(4,128)(2,1)}, u32[]{:S(2)}) copy-start(bf16[2,1,4,576]{3,2,1,0:T(4,128)(2,1)} %param.15) | copy-start | bytes 27652
  3.3 10.2 %copy-start.8 = (s32[1,1,16]{2,1,0:T(1,128)S(1)}, s32[1,1,16]{2,1,0:T(1,128)}, u32[]{:S(2)}) copy-start(s32[1,1,16]{2,1,0:T(1,128)} %param.13) | copy-start | bytes 196
  3.3 10.8 %copy-start.4 = (bf16[2,1,4,128,192]{3,4,2,1,0:T(8,128)(2,1)S(1)}, bf16[2,1,4,128,192]{3,4,2,1,0:T(8,128)(2,1)}, u32[]{:S(2)}) copy-start(bf16[2,1,4,128,192]{3,4,2,1,0:T(8,128)(2,1)} %param.8) | copy-start | bytes 1179652
  3.3 64.5 %all-to-all-start = ((bf16[16,144,512]{2,1,0:T(8,128)(2,1)}), bf16[16,144,512]{2,1,0:T(8,128)(2,1)S(1)}, u32[]{:S(2)}, u32[]{:S(2)}) async-start(bf16[16,144,512]{2,1,0:T(8,128)(2,1)} %shard_map.85), calls=%async_computation | async-start | bytes 4718592 | tf_op jit(solution)/shard_map/all_to_all | solution.py:320
  13.4 13.7 %collective-permute-start.13 = (s32[16]{0:T(128)S(1)}, s32[16]{0:T(128)S(1)}, u32[]{:S(2)}, u32[]{:S(2)}) collective-permute-start(s32[16]{0:T(128)S(1)} %bitcast.84), channel_id=1, source_target_pairs={{0,16},{16,0},{1,17},{17,1},{2,18},{18,2},{3,19},{19,3},{4,20},{20... | collective-permute-start | bytes 200 | tf_op jit(solution)/shard_map/ppermute | solution.py:312
  13.6 18.1 %collective-permute-start.6 = (bf16[2,8,128,256]{3,2,1,0:T(8,128)(2,1)}, bf16[2,8,128,256]{3,2,1,0:T(8,128)(2,1)}, u32[]{:S(2)}, u32[]{:S(2)}) collective-permute-start(bf16[2,8,128,256]{3,2,1,0:T(8,128)(2,1)} %own.2), channel_id=1, source_target_pairs={{0,16},{16,0},{1,17},{17,1},{2,18},{18,2},{3,19},{19,3},{4,20},{20... | collective-permute-start | bytes 3145736 | tf_op jit(solution)/shard_map/ppermute | solution.py:312
  15.0 7.9 %collective-permute-start.1 = (bf16[4,32,128]{2,1,0:T(8,128)(2,1)S(1)}, bf16[4,32,128]{2,1,0:T(8,128)(2,1)S(1)}, u32[]{:S(2)}, u32[]{:S(2)}) collective-permute-start(bf16[4,32,128]{2,1,0:T(8,128)(2,1)S(1)} %get-tuple-element.26), channel_id=1, source_target_pairs={{0,2},{1,3},{2,0},{3,1},{4,6},{5,7},{6,4},{7,5},{8,10},{9,11},{10,... | collective-permute-start | bytes 98312 | tf_op jit(solution)/shard_map/ppermute | solution.py:300
  17.9 6.0 %collective-permute-start = (bf16[4,32,128]{2,1,0:T(8,128)(2,1)S(1)}, bf16[4,32,128]{2,1,0:T(8,128)(2,1)S(1)}, u32[]{:S(2)}, u32[]{:S(2)}) collective-permute-start(bf16[4,32,128]{2,1,0:T(8,128)(2,1)S(1)} %get-tuple-element.27), channel_id=1, source_target_pairs={{0,1},{1,2},{2,3},{3,0},{4,5},{5,6},{6,7},{7,4},{8,9},{9,10},{10,1... | collective-permute-start | bytes 98312 | tf_op jit(solution)/shard_map/ppermute | solution.py:300
  18.2 5.7 %collective-permute-start.2 = (bf16[4,32,128]{2,1,0:T(8,128)(2,1)S(1)}, bf16[4,32,128]{2,1,0:T(8,128)(2,1)S(1)}, u32[]{:S(2)}, u32[]{:S(2)}) collective-permute-start(bf16[4,32,128]{2,1,0:T(8,128)(2,1)S(1)} %get-tuple-element.28), channel_id=1, source_target_pairs={{0,3},{1,0},{2,1},{3,2},{4,7},{5,4},{6,5},{7,6},{8,11},{9,8},{10,9... | collective-permute-start | bytes 98312 | tf_op jit(solution)/shard_map/ppermute | solution.py:300
  22.9 24.9 %collective-permute-start.14 = (bf16[2,8,256,128]{3,2,1,0:T(8,128)(2,1)}, bf16[2,8,256,128]{3,2,1,0:T(8,128)(2,1)}, u32[]{:S(2)}, u32[]{:S(2)}) collective-permute-start(bf16[2,8,256,128]{3,2,1,0:T(8,128)(2,1)} %own.3), channel_id=1, source_target_pairs={{0,16},{16,0},{1,17},{17,1},{2,18},{18,2},{3,19},{19,3},{4,20},{20... | collective-permute-start | bytes 3145736 | tf_op jit(solution)/shard_map/ppermute | solution.py:312
  23.9 4.5 %collective-permute-start.5 = (bf16[4,32,128]{2,1,0:T(8,128)(2,1)S(1)}, bf16[4,32,128]{2,1,0:T(8,128)(2,1)S(1)}, u32[]{:S(2)}, u32[]{:S(2)}) collective-permute-start(bf16[4,32,128]{2,1,0:T(8,128)(2,1)S(1)} %get-tuple-element.22), channel_id=1, source_target_pairs={{0,12},{1,13},{2,14},{3,15},{4,0},{5,1},{6,2},{7,3},{8,4},{9,5},{1... | collective-permute-start | bytes 98312 | tf_op jit(solution)/shard_map/ppermute | solution.py:300
  26.7 4.6 %collective-permute-start.4 = (bf16[4,32,128]{2,1,0:T(8,128)(2,1)S(1)}, bf16[4,32,128]{2,1,0:T(8,128)(2,1)S(1)}, u32[]{:S(2)}, u32[]{:S(2)}) collective-permute-start(bf16[4,32,128]{2,1,0:T(8,128)(2,1)S(1)} %get-tuple-element.23), channel_id=1, source_target_pairs={{0,8},{1,9},{2,10},{3,11},{4,12},{5,13},{6,14},{7,15},{8,0},{9,1},... | collective-permute-start | bytes 98312 | tf_op jit(solution)/shard_map/ppermute | solution.py:300
  27.1 7.1 %copy-start.10 = (s32[16]{0:T(128)}, s32[16]{0:T(128)S(1)}, u32[]{:S(2)}) copy-start(s32[16]{0:T(128)S(1)} %collective-permute-done.13) | copy-start | bytes 196
  27.1 4.6 %collective-permute-start.3 = (bf16[4,32,128]{2,1,0:T(8,128)(2,1)S(1)}, bf16[4,32,128]{2,1,0:T(8,128)(2,1)S(1)}, u32[]{:S(2)}, u32[]{:S(2)}) collective-permute-start(bf16[4,32,128]{2,1,0:T(8,128)(2,1)S(1)} %get-tuple-element.24), channel_id=1, source_target_pairs={{0,4},{1,5},{2,6},{3,7},{4,8},{5,9},{6,10},{7,11},{8,12},{9,13},{1... | collective-permute-start | bytes 98312 | tf_op jit(solution)/shard_map/ppermute | solution.py:300
  31.7 6.0 %copy-start.7 = (s32[2,16]{1,0:T(2,128)S(1)}, s32[2,16]{1,0:T(2,128)}, u32[]{:S(2)}) copy-start(s32[2,16]{1,0:T(2,128)} %rev.3) | copy-start | bytes 388
  31.7 6.0 %copy-start.9 = (s32[1,1,16]{2,1,0:T(1,128)S(1)}, s32[1,1,16]{2,1,0:T(1,128)}, u32[]{:S(2)}) copy-start(s32[1,1,16]{2,1,0:T(1,128)} %param.13) | copy-start | bytes 196
  31.7 6.0 %copy-start.11 = (s32[2]{0:T(128)S(1)}, s32[2]{0:T(128)}, u32[]{:S(2)}) copy-start(s32[2]{0:T(128)} %iota_multiply_fusion) | copy-start | bytes 28
  34.2 13.7 %copy-start.3 = (bf16[2,8,256,128]{3,2,1,0:T(8,128)(2,1)S(1)}, bf16[2,8,256,128]{3,2,1,0:T(8,128)(2,1)}, u32[]{:S(2)}) copy-start(bf16[2,8,256,128]{3,2,1,0:T(8,128)(2,1)} %own.3) | copy-start | bytes 3145732
  35.0 8.1 %collective-permute-start.8 = (bf16[4,32,512]{2,1,0:T(8,128)(2,1)}, bf16[4,32,512]{2,1,0:T(8,128)(2,1)}, u32[]{:S(2)}, u32[]{:S(2)}) collective-permute-start(bf16[4,32,512]{2,1,0:T(8,128)(2,1)} %get-tuple-element.18), channel_id=1, source_target_pairs={{0,2},{1,3},{2,0},{3,1},{4,6},{5,7},{6,4},{7,5},{8,10},{9,11},{10,... | collective-permute-start | bytes 393224 | tf_op jit(solution)/shard_map/ppermute | solution.py:300
  35.0 8.9 %collective-permute-start.7 = (bf16[4,32,512]{2,1,0:T(8,128)(2,1)}, bf16[4,32,512]{2,1,0:T(8,128)(2,1)}, u32[]{:S(2)}, u32[]{:S(2)}) collective-permute-start(bf16[4,32,512]{2,1,0:T(8,128)(2,1)} %get-tuple-element.19), channel_id=1, source_target_pairs={{0,1},{1,2},{2,3},{3,0},{4,5},{5,6},{6,7},{7,4},{8,9},{9,10},{10,1... | collective-permute-start | bytes 393224 | tf_op jit(solution)/shard_map/ppermute | solution.py:300
  36.5 7.4 %collective-permute-start.9 = (bf16[4,32,512]{2,1,0:T(8,128)(2,1)}, bf16[4,32,512]{2,1,0:T(8,128)(2,1)}, u32[]{:S(2)}, u32[]{:S(2)}) collective-permute-start(bf16[4,32,512]{2,1,0:T(8,128)(2,1)} %get-tuple-element.20), channel_id=1, source_target_pairs={{0,3},{1,0},{2,1},{3,2},{4,7},{5,4},{6,5},{7,6},{8,11},{9,8},{10,9... | collective-permute-start | bytes 393224 | tf_op jit(solution)/shard_map/ppermute | solution.py:300
  43.0 4.2 %copy-start.5 = (s32[16,128]{1,0:T(8,128)S(1)}, s32[16,128]{1,0:T(8,128)}, u32[]{:S(2)}) copy-start(s32[16,128]{1,0:T(8,128)} %add.42) | copy-start | bytes 24580
  45.1 5.2 %collective-permute-start.12 = (bf16[4,32,512]{2,1,0:T(8,128)(2,1)S(1)}, bf16[4,32,512]{2,1,0:T(8,128)(2,1)S(1)}, u32[]{:S(2)}, u32[]{:S(2)}) collective-permute-start(bf16[4,32,512]{2,1,0:T(8,128)(2,1)S(1)} %get-tuple-element.14), channel_id=1, source_target_pairs={{0,12},{1,13},{2,14},{3,15},{4,0},{5,1},{6,2},{7,3},{8,4},{9,5},{1... | collective-permute-start | bytes 393224 | tf_op jit(solution)/shard_map/ppermute | solution.py:300
  45.5 5.6 %collective-permute-start.11 = (bf16[4,32,512]{2,1,0:T(8,128)(2,1)S(1)}, bf16[4,32,512]{2,1,0:T(8,128)(2,1)S(1)}, u32[]{:S(2)}, u32[]{:S(2)}) collective-permute-start(bf16[4,32,512]{2,1,0:T(8,128)(2,1)S(1)} %get-tuple-element.15), channel_id=1, source_target_pairs={{0,8},{1,9},{2,10},{3,11},{4,12},{5,13},{6,14},{7,15},{8,0},{9,1},... | collective-permute-start | bytes 393224 | tf_op jit(solution)/shard_map/ppermute | solution.py:300
  46.5 6.4 %collective-permute-start.10 = (bf16[4,32,512]{2,1,0:T(8,128)(2,1)S(1)}, bf16[4,32,512]{2,1,0:T(8,128)(2,1)S(1)}, u32[]{:S(2)}, u32[]{:S(2)}) collective-permute-start(bf16[4,32,512]{2,1,0:T(8,128)(2,1)S(1)} %get-tuple-element.16), channel_id=1, source_target_pairs={{0,4},{1,5},{2,6},{3,7},{4,8},{5,9},{6,10},{7,11},{8,12},{9,13},{1... | collective-permute-start | bytes 393224 | tf_op jit(solution)/shard_map/ppermute | solution.py:300
  47.8 5.1 %copy-start.6 = (bf16[4,576]{1,0:T(4,128)(2,1)S(1)}, bf16[4,576]{1,0:T(4,128)(2,1)}, u32[]{:S(2)}) copy-start(bf16[4,576]{1,0:T(4,128)(2,1)} %dynamic-slice_bitcast_fusion) | copy-start | bytes 13828
  49.3 1.1 %copy-start.1 = (bf16[5,512,256]{2,1,0:T(8,128)(2,1)}, bf16[5,512,256]{2,1,0:T(8,128)(2,1)S(1)}, u32[]{:S(2)}) copy-start(bf16[5,512,256]{2,1,0:T(8,128)(2,1)S(1)} %shard_map.84.weight) | copy-start | bytes 3932164
  67.8 21.7 %copy-start.2 = (bf16[5,512,256]{2,1,0:T(8,128)(2,1)S(1)}, bf16[5,512,256]{2,1,0:T(8,128)(2,1)}, u32[]{:S(2)}) copy-start(bf16[5,512,256]{2,1,0:T(8,128)(2,1)} %copy-done.1) | copy-start | bytes 3932164

commit v4 on v3

--- a/solution.py
+++ b/solution.py
@@ -22,6 +22,7 @@
 BLOCK = HEADS_PER * STEPS
 ROWS = PEERS * BLOCK
 TILE = 512
+CHUNK = 2
 HALF = KV_RANK // 2
 DEAD = -1e30
 SCALE = 1.0 / math.sqrt(NOPE + ROPE)
@@ -32,48 +33,44 @@
 ANY = pl.BlockSpec(memory_space=pl.ANY)
 
 
-def send_kernel(send_to, pages, out, target_of, page_of, held, packed, target_sem, in_sem, lat_sem, rope_sem):
+def send_kernel(send_to, pages, out, target_of, held, packed, target_sem, in_sem, lat_sem, rope_sem):
     targets = pltpu.make_async_copy(send_to, target_of, target_sem)
     targets.start()
 
-    def fetch(layer):
-        return pltpu.make_async_copy(pages.at[layer], held.at[layer], in_sem.at[layer])
-
-    def latents(dest, half):
-        index = dest * 2 + half
+    def fetch(part):
+        some = pl.ds(part * CHUNK, CHUNK)
+        return pltpu.make_async_copy(pages.at[:, some], held.at[:, some], in_sem.at[part])
+
+    def latents(layer, page):
+        target = target_of[page]
         return pltpu.make_async_copy(
-            held.at[dest % 2, page_of[dest - dest % 2 + half], :, pl.ds(0, KV_RANK)],
-            out.at[dest, pl.ds(half * PAGE, PAGE)],
-            lat_sem.at[index],
+            held.at[layer, page, :, pl.ds(0, KV_RANK)],
+            out.at[target // 2 * 2 + layer, pl.ds(target % 2 * PAGE, PAGE)],
+            lat_sem.at[layer, page],
         )
 
-    def ropes(dest):
-        return pltpu.make_async_copy(
-            packed.at[dest], out.at[dest, pl.ds(PAIR, 16)], rope_sem.at[dest]
-        )
-
-    for layer in range(2):
-        fetch(layer).start()
+    for part in range(PEERS // CHUNK):
+        fetch(part).start()
     targets.wait()
+    for part in range(PEERS // CHUNK):
+        fetch(part).wait()
+        for page in range(part * CHUNK, (part + 1) * CHUNK):
+            for layer in range(2):
+                latents(layer, page).start()
+        for page in range(part * CHUNK, (part + 1) * CHUNK):
+            target = target_of[page]
+            columns = pl.ds(pl.multiple_of(target % 2 * (KV_RANK // 2), KV_RANK // 2), KV_RANK // 2)
+            for layer in range(2):
+                packed[target // 2 * 2 + layer, :, columns] = jnp.concatenate(
+                    [held[layer, page, 16 * k : 16 * k + 16, KV_RANK:] for k in range(PAGE // 16)],
+                    axis=1,
+                )
+    ropes = pltpu.make_async_copy(packed, out.at[:, pl.ds(PAIR, 16)], rope_sem)
+    ropes.start()
     for page in range(PEERS):
-        page_of[target_of[page]] = page
-    for layer in range(2):
-        fetch(layer).wait()
-        for dest in range(layer, PEERS, 2):
-            for half in range(2):
-                latents(dest, half).start()
-        for dest in range(layer, PEERS, 2):
-            groups = [
-                held[layer, page_of[dest - layer + half], 16 * k : 16 * k + 16, KV_RANK:]
-                for half in range(2)
-                for k in range(PAGE // 16)
-            ]
-            packed[dest] = jnp.concatenate(groups, axis=1)
-            ropes(dest).start()
-    for dest in range(PEERS):
-        for half in range(2):
-            latents(dest, half).wait()
-        ropes(dest).wait()
+        for layer in range(2):
+            latents(layer, page).wait()
+    ropes.wait()
 
 
 def gather_pages(send_to, pages):
@@ -84,13 +81,12 @@
         out_specs=ANY,
         scratch_shapes=[
             pltpu.SMEM((PEERS,), jnp.int32),
-            pltpu.SMEM((PEERS,), jnp.int32),
             pltpu.VMEM(pages.shape, jnp.bfloat16),
             pltpu.VMEM((PEERS, 16, KV_RANK), jnp.bfloat16),
             pltpu.SemaphoreType.DMA,
-            pltpu.SemaphoreType.DMA((2,)),
-            pltpu.SemaphoreType.DMA((2 * PEERS,)),
-            pltpu.SemaphoreType.DMA((PEERS,)),
+            pltpu.SemaphoreType.DMA((PEERS // CHUNK,)),
+            pltpu.SemaphoreType.DMA((2, PEERS)),
+            pltpu.SemaphoreType.DMA,
         ],
         compiler_params=pltpu.CompilerParams(vmem_limit_bytes=60 << 20),
         cost_estimate=pl.CostEstimate(flops=0, bytes_accessed=5 << 20, transcendentals=0),
@@ -228,7 +224,7 @@
             ropes[p * PAIR + 16 * k : p * PAIR + 16 * k + 16, :] = pages[
                 p, PAIR:PAIR_ROWS, ROPE * k : ROPE * k + ROPE
             ]
-    width = 2 * PAIR
+    width = 4 * PAIR
     fresh = inputs[ROWS : ROWS + 16, :KV_RANK]
     fresh_rope = inputs[ROWS : ROWS + 16, KV_RANK : KV_RANK + ROPE]
     live = inputs[ROWS + 16 :, :PAIR].astype(jnp.float32) > 0.5
@@ -241,14 +237,15 @@
         extra = dot_rows(ql, fresh) + dot_rows(qr, fresh_rope)
         extra = jnp.where(key <= lax.rem(row // HEADS_PER, STEPS), extra, DEAD)
         highest = jnp.full((TILE, PAIR), DEAD, jnp.float32)
-        for n in range(0, PEERS, 2):
+        for n in range(0, PEERS, 4):
             part = slice(n * PAIR, n * PAIR + width)
-            lat = pages[n : n + 2, :PAIR, :].reshape(width, KV_RANK)
+            lat = pages[n : n + 4, :PAIR, :].reshape(width, KV_RANK)
             s = dot_rows(ql, lat) + dot_rows(qr, ropes[part, :])
-            bound = jnp.concatenate([live[n : n + 1], live[n + 1 : n + 2]], axis=1)
+            bound = jnp.concatenate([live[p : p + 1] for p in range(n, n + 4)], axis=1)
             s = jnp.where(bound, s, DEAD)
             scores[:, part] = s
-            highest = jnp.maximum(highest, jnp.maximum(s[:, :PAIR], s[:, PAIR:]))
+            for k in range(0, width, PAIR):
+                highest = jnp.maximum(highest, s[:, k : k + PAIR])
         peak = jnp.maximum(
             jnp.max(extra, axis=1, keepdims=True), jnp.max(highest, axis=1, keepdims=True)
         )
@@ -256,12 +253,13 @@
         total = jnp.sum(weight.astype(jnp.float32), axis=1, keepdims=True)
         summed = jnp.dot(weight, fresh, preferred_element_type=jnp.float32)
         added = jnp.zeros((TILE, PAIR), jnp.float32)
-        for n in range(0, PEERS, 2):
+        for n in range(0, PEERS, 4):
             part = slice(n * PAIR, n * PAIR + width)
-            lat = pages[n : n + 2, :PAIR, :].reshape(width, KV_RANK)
+            lat = pages[n : n + 4, :PAIR, :].reshape(width, KV_RANK)
             weight = jnp.exp2((scores[:, part] - peak) * TO_LOG2).astype(jnp.bfloat16)
             kept = weight.astype(jnp.float32)
-            added = added + (kept[:, :PAIR] + kept[:, PAIR:])
+            for k in range(0, width, PAIR):
+                added = added + kept[:, k : k + PAIR]
             summed = summed + jnp.dot(weight, lat, preferred_element_type=jnp.float32)
         total = total + jnp.sum(added, axis=1, keepdims=True)
         result = (summed * (1.0 / total)).astype(jnp.bfloat16)
@@ -342,7 +340,9 @@
     latent_out = attend(where, inputs, pages)
     latent_heads = lax.all_to_all(latent_out, "req", split_axis=0, concat_axis=0, tiled=True)
     head_out = project_values(latent_heads.reshape(ROWS, KV_RANK), values)
-    return lax.all_gather(head_out.reshape(PEERS, STEPS, HEADS_PER, VDIM), "seq", axis=0)
+    own = head_out.reshape(PEERS, STEPS, HEADS_PER, VDIM)
+    got = swapped(own)
+    return jnp.where(layer == 0, jnp.stack([own, got]), jnp.stack([got, own]))
 
 
 def solution(mesh):

time: 94.9 us -> 93.9 us (0.989)
  blocking collectives: 20.7 us -> 17.1 us
  starting transfers between devices: 25.8 us -> 27.9 us
  waiting for transfers between devices: 21.3 us -> 22.3 us
    all_gather x1 -> x0, blocking collectives: 3.58 us -> none  [shards(): lax.all_gather(head_out.reshape(PEERS, STEPS, HEADS_PER, VDIM), 'seq', ax...]
    ppermute x3 -> x4, starting transfers between devices: 1.52 us -> 3.57 us  [swapped(): return lax.ppermute(value, 'seq', [(0, 1), (1, 0)])]
    ppermute x3 -> x4, waiting for transfers between devices: 0.01 us -> 0.99 us  [swapped(): return lax.ppermute(value, 'seq', [(0, 1), (1, 0)])]
    unnamed x26 -> x25, local copies, waits for them, and re-layouts: 2.02 us -> 1.33 us
  transfers between devices with their start and end apart: 16 -> 17, of which waited for: 6 -> 7; matrix products, arithmetic and copies ran while one was open for 11% -> 12% of each run, Pallas kernels for 5% -> 5%
where the time goes in v4:
time: 93.9 us; the launch traced here: 93.5 us
  starting transfers between devices  27.9 us (30%)
  waiting for transfers between devices  22.3 us (24%)
  blocking collectives  17.1 us (18%)
  Pallas kernels  12.6 us (13%)
  local copies, waits for them, and re-layouts  8.1 us (9%)
  other arithmetic  4.61 us (5%)
    all_to_all x1, blocking collectives, shards(): lax.all_to_all(latent_out, 'req', split_axis=0, concat_axis=0, tiled=True)  17.1 us
    all_to_all x1, waiting for transfers between devices, shards(): lax.all_to_all(sent, ('group', 'seq'), split_axis=0, concat_axis=0, tiled...  14.4 us
    ppermute x12, starting transfers between devices, shifted(): return lax.ppermute(value, 'req', pairs)  14.2 us
    all_to_all x1, starting transfers between devices, shards(): lax.all_to_all(sent, ('group', 'seq'), split_axis=0, concat_axis=0, tiled...  10.1 us
    ppermute x12, waiting for transfers between devices, shifted(): return lax.ppermute(value, 'req', pairs)  6.85 us
    pallas_call x1, Pallas kernels, attend(): pl.pallas_call(attend_kernel, out_shape=jax.ShapeDtypeStruct((PEERS, BLOC...  4.47 us
    ppermute x4, starting transfers between devices, swapped(): return lax.ppermute(value, 'seq', [(0, 1), (1, 0)])  3.57 us
    add x4, local copies, waits for them, and re-layouts, shards(): live = starts[:, :, None] + jnp.arange(PAGE, dtype=jnp.int32) < lengths[0]  3.42 us
  transfers between devices with their start and end apart: 17, of which 7 were waited for; matrix products, arithmetic and copies ran while one was open for 12% of the time, Pallas kernels for 5%

profile of v4, /device:TPU:1, one launch (start us, length us, event | category | flops | bytes accessed | tf_op | source)
XLA Modules:
  0.0 93.5 jit_solution(3199753595979698919)
XLA Ops:
  0.0 2.9 %shard_map.85 = bf16[16,144,512]{2,1,0:T(8,128)(2,1)} custom-call(s32[16]{0:T(128)} %bitcast.93, bf16[2,16,64,576]{3,2,1,0:T(8,128)(2,1)} %bitcast.76), custom_call_target="tpu_custom_call" | custom-call | bytes 5242880 | tf_op jit(solution)/shard_map/pallas_call | solution.py:77
  2.9 10.1 %all-to-all-start = ((bf16[16,144,512]{2,1,0:T(8,128)(2,1)}), bf16[16,144,512]{2,1,0:T(8,128)(2,1)S(1)}, u32[]{:S(2)}, u32[]{:S(2)}) async-start(bf16[16,144,512]{2,1,0:T(8,128)(2,1)} %shard_map.85), calls=%async_computation | async-start | bytes 4718592 | tf_op jit(solution)/shard_map/all_to_all | solution.py:318
  14.0 0.7 shard_map.82
  14.7 2.8 %collective-permute-start.1 = (bf16[4,32,128]{2,1,0:T(8,128)(2,1)S(1)}, bf16[4,32,128]{2,1,0:T(8,128)(2,1)S(1)}, u32[]{:S(2)}, u32[]{:S(2)}) collective-permute-start(bf16[4,32,128]{2,1,0:T(8,128)(2,1)S(1)} %get-tuple-element.26), channel_id=1, source_target_pairs={{0,2},{1,3},{2,0},{3,1},{4,6},{5,7},{6,4},{7,5},{8,10},{9,11},{10,... | collective-permute-start | bytes 98312 | tf_op jit(solution)/shard_map/ppermute | solution.py:298
  17.8 2.4 %collective-permute-start.2 = (bf16[4,32,128]{2,1,0:T(8,128)(2,1)S(1)}, bf16[4,32,128]{2,1,0:T(8,128)(2,1)S(1)}, u32[]{:S(2)}, u32[]{:S(2)}) collective-permute-start(bf16[4,32,128]{2,1,0:T(8,128)(2,1)S(1)} %get-tuple-element.28), channel_id=1, source_target_pairs={{0,3},{1,0},{2,1},{3,2},{4,7},{5,4},{6,5},{7,6},{8,11},{9,8},{10,9... | collective-permute-start | bytes 98312 | tf_op jit(solution)/shard_map/ppermute | solution.py:298
  22.6 0.9 collective-permute-start.14
  23.6 2.8 %collective-permute-start.5 = (bf16[4,32,128]{2,1,0:T(8,128)(2,1)S(1)}, bf16[4,32,128]{2,1,0:T(8,128)(2,1)S(1)}, u32[]{:S(2)}, u32[]{:S(2)}) collective-permute-start(bf16[4,32,128]{2,1,0:T(8,128)(2,1)S(1)} %get-tuple-element.22), channel_id=1, source_target_pairs={{0,12},{1,13},{2,14},{3,15},{4,0},{5,1},{6,2},{7,3},{8,4},{9,5},{1... | collective-permute-start | bytes 98312 | tf_op jit(solution)/shard_map/ppermute | solution.py:298
  26.8 0.7 collective-permute-start.3
  28.1 2.9 %collective-permute-done.4 = bf16[4,32,128]{2,1,0:T(8,128)(2,1)S(1)} collective-permute-done((bf16[4,32,128]{2,1,0:T(8,128)(2,1)S(1)}, bf16[4,32,128]{2,1,0:T(8,128)(2,1)S(1)}, u32[]{:S(2)}, u32[]{:S(2)}) %collective-permute-start.4) | collective-permute-done | bytes 32800 | tf_op jit(solution)/shard_map/ppermute | solution.py:298
  31.4 2.5 %shard_map.83 = bf16[512,512]{1,0:T(8,128)(2,1)S(1)} custom-call(s32[3]{0:T(128)S(1)} %pad_add_fusion.1.where, bf16[512,128]{1,0:T(8,128)(2,1)S(1)} %bitcast.71, bf16[2,8,128,256]{3,2,1,0:T(8,128)(2,1)} %own.2, bf16[2,8,128,256]{3,2,1,0:T(8,128)(2,1)} %collective-permute-done.6.got), custom_call_target="tpu_custom_call" | custom-call | flops 536870912 | bytes 2097152 | tf_op jit(solution)/shard_map/pallas_call | solution.py:201
  33.9 0.8 fusion.5
  34.7 1.5 %collective-permute-start.7 = (bf16[4,32,512]{2,1,0:T(8,128)(2,1)}, bf16[4,32,512]{2,1,0:T(8,128)(2,1)}, u32[]{:S(2)}, u32[]{:S(2)}) collective-permute-start(bf16[4,32,512]{2,1,0:T(8,128)(2,1)} %get-tuple-element.19), channel_id=1, source_target_pairs={{0,1},{1,2},{2,3},{3,0},{4,5},{5,6},{6,7},{7,4},{8,9},{9,10},{10,1... | collective-permute-start | bytes 393224 | tf_op jit(solution)/shard_map/ppermute | solution.py:298
  36.2 1.2 %collective-permute-start.9 = (bf16[4,32,512]{2,1,0:T(8,128)(2,1)}, bf16[4,32,512]{2,1,0:T(8,128)(2,1)}, u32[]{:S(2)}, u32[]{:S(2)}) collective-permute-start(bf16[4,32,512]{2,1,0:T(8,128)(2,1)} %get-tuple-element.20), channel_id=1, source_target_pairs={{0,3},{1,0},{2,1},{3,2},{4,7},{5,4},{6,5},{7,6},{8,11},{9,8},{10,9... | collective-permute-start | bytes 393224 | tf_op jit(solution)/shard_map/ppermute | solution.py:298
  37.4 1.2 %add_bitcast_fusion = s32[16,2]{0,1:T(2,128)} fusion(s32[2,16]{1,0:T(2,128)S(1)} %copy-done.7, pred[]{:T(512)S(6)} %eq.4, s32[2]{0:T(128)S(1)} %copy-done.11, s32[1,16]{1,0:T(1,128)} %bitcast.92, s32[1,16]{1,0:T(1,128)S(1)} %bitcast.90), kind=kLoop, calls=%fused_computation.27 | loop fusion | flops 128 | bytes 393 | tf_op jit(solution)/shard_map/add | solution.py:330
  38.6 1.3 %copy.16 = s32[16,2]{1,0:T(8,128)} copy(s32[16,2]{0,1:T(2,128)} %add_bitcast_fusion) | data formatting | bytes 256 | tf_op jit(solution)/shard_map/add | solution.py:330
  39.9 1.4 %add.41 = s32[16,2,64]{2,1,0:T(2,128)} broadcast(s32[16,2]{1,0:T(8,128)} %copy.16), dimensions={0,1} | broadcast | bytes 8320 | tf_op jit(solution)/shard_map/add | solution.py:331
  41.3 1.4 %add.42 = s32[16,128]{1,0:T(8,128)} reshape(s32[16,2,64]{2,1,0:T(2,128)} %add.41) | data formatting | bytes 16384 | tf_op jit(solution)/shard_map/add | solution.py:331
  42.6 1.0 %collective-permute-done.7 = bf16[4,32,512]{2,1,0:T(8,128)(2,1)} collective-permute-done((bf16[4,32,512]{2,1,0:T(8,128)(2,1)}, bf16[4,32,512]{2,1,0:T(8,128)(2,1)}, u32[]{:S(2)}, u32[]{:S(2)}) %collective-permute-start.7) | collective-permute-done | bytes 131104 | tf_op jit(solution)/shard_map/ppermute | solution.py:298
  43.7 1.2 %pad_maximum_fusion = bf16[4,4,32,512]{3,2,1,0:T(8,128)(2,1)S(1)} fusion(bf16[4,1,32,512]{3,2,1,0:T(8,128)(2,1)} %bitcast.23, bf16[4,1,32,512]{3,2,1,0:T(8,128)(2,1)} %bitcast.21, bf16[4,1,32,512]{3,2,1,0:T(8,128)(2,1)} %bitcast.19, bf16[4,1,32,512]{3,2,1,0:T(8,128)(2,1)} %get-tuple-element.17), kind=kLoop, calls=%fused_computation.6 | loop fusion | flops 786432 | bytes 1048576 | tf_op jit(solution)/shard_map/stack | solution.py:304
  45.2 1.0 %collective-permute-start.11 = (bf16[4,32,512]{2,1,0:T(8,128)(2,1)S(1)}, bf16[4,32,512]{2,1,0:T(8,128)(2,1)S(1)}, u32[]{:S(2)}, u32[]{:S(2)}) collective-permute-start(bf16[4,32,512]{2,1,0:T(8,128)(2,1)S(1)} %get-tuple-element.15), channel_id=1, source_target_pairs={{0,8},{1,9},{2,10},{3,11},{4,12},{5,13},{6,14},{7,15},{8,0},{9,1},... | collective-permute-start | bytes 393224 | tf_op jit(solution)/shard_map/ppermute | solution.py:298
  46.2 0.8 collective-permute-start.10
  47.0 0.7 add_compare_fusion
  47.7 1.4 %shard_map.84.weight = bf16[5,512,256]{2,1,0:T(8,128)(2,1)S(1)} custom-call(s32[3]{0:T(128)S(1)} %pad_add_fusion.1.where, bf16[2,8,256,128]{3,2,1,0:T(8,128)(2,1)S(1)} %copy-done.3, bf16[2,8,256,128]{3,2,1,0:T(8,128)(2,1)} %collective-permute-done.14.got), custom_call_target="tpu_custom_call" | custom-call | bytes 3145728 | tf_op jit(solution)/shard_map/pallas_call | solution.py:164
  49.1 1.1 %copy-done.1 = bf16[5,512,256]{2,1,0:T(8,128)(2,1)} copy-done((bf16[5,512,256]{2,1,0:T(8,128)(2,1)}, bf16[5,512,256]{2,1,0:T(8,128)(2,1)S(1)}, u32[]{:S(2)}) %copy-start.1) | copy-done | bytes 1310744
  50.9 1.9 %collective-permute-done.10 = bf16[4,32,512]{2,1,0:T(8,128)(2,1)S(1)} collective-permute-done((bf16[4,32,512]{2,1,0:T(8,128)(2,1)S(1)}, bf16[4,32,512]{2,1,0:T(8,128)(2,1)S(1)}, u32[]{:S(2)}, u32[]{:S(2)}) %collective-permute-start.10) | collective-permute-done | bytes 131104 | tf_op jit(solution)/shard_map/ppermute | solution.py:298
  53.0 14.4 %all-to-all-done.pages = bf16[16,144,512]{2,1,0:T(8,128)(2,1)S(1)} async-done(((bf16[16,144,512]{2,1,0:T(8,128)(2,1)}), bf16[16,144,512]{2,1,0:T(8,128)(2,1)S(1)}, u32[]{:S(2)}, u32[]{:S(2)}) %all-to-all-start) | async-done | bytes 2359328 | tf_op jit(solution)/shard_map/all_to_all | solution.py:318
  67.4 4.5 %shard_map.86 = bf16[16,32,512]{2,1,0:T(8,128)(2,1)S(1)} custom-call(s32[3]{0:T(128)S(1)} %pad_add_fusion.1.where, bf16[544,640]{1,0:T(8,128)(2,1)S(1)} %fusion.3.inputs, bf16[16,144,512]{2,1,0:T(8,128)(2,1)S(1)} %all-to-all-done.pages), custom_call_target="tpu_custom_call" | custom-call | flops 2281701376 | bytes 4194304 | tf_op jit(solution)/shard_map/pallas_call | solution.py:276
  71.9 17.1 %all_to_all.10 = bf16[16,32,512]{2,1,0:T(8,128)(2,1)S(1)} all-to-all(bf16[16,32,512]{2,1,0:T(8,128)(2,1)S(1)} %shard_map.86), channel_id=1, replica_groups=mesh['group'=8,'seq'=2,'req'=16] {'req'}, dimensions={0} | all-to-all | bytes 1048576 | tf_op jit(solution)/shard_map/all_to_all | solution.py:341
  89.0 0.7 shard_map.87
  89.7 2.1 %collective-permute-start.15 = (bf16[16,4,8,128]{3,2,1,0:T(8,128)(2,1)S(1)}, bf16[16,4,8,128]{3,2,1,0:T(8,128)(2,1)S(1)}, u32[]{:S(2)}, u32[]{:S(2)}) collective-permute-start(bf16[16,4,8,128]{3,2,1,0:T(8,128)(2,1)S(1)} %bitcast.73), channel_id=1, source_target_pairs={{0,16},{16,0},{1,17},{17,1},{2,18},{18,2},{3,19},{19,3},{4,20},{20... | collective-permute-start | bytes 393224 | tf_op jit(solution)/shard_map/ppermute | solution.py:310
  91.8 1.0 %collective-permute-done.15 = bf16[16,4,8,128]{3,2,1,0:T(8,128)(2,1)S(1)} collective-permute-done((bf16[16,4,8,128]{3,2,1,0:T(8,128)(2,1)S(1)}, bf16[16,4,8,128]{3,2,1,0:T(8,128)(2,1)S(1)}, u32[]{:S(2)}, u32[]{:S(2)}) %collective-permute-start.15) | collective-permute-done | bytes 131104 | tf_op jit(solution)/shard_map/ppermute | solution.py:310
  92.7 0.7 maximum_select_fusion
  (58 shorter events, 5.7 us)
Async XLA Ops:
  0.0 20.2 %copy-start = (bf16[2,1,4,576]{3,2,1,0:T(4,128)(2,1)S(1)}, bf16[2,1,4,576]{3,2,1,0:T(4,128)(2,1)}, u32[]{:S(2)}) copy-start(bf16[2,1,4,576]{3,2,1,0:T(4,128)(2,1)} %param.15) | copy-start | bytes 27652
  2.9 10.2 %copy-start.8 = (s32[1,1,16]{2,1,0:T(1,128)S(1)}, s32[1,1,16]{2,1,0:T(1,128)}, u32[]{:S(2)}) copy-start(s32[1,1,16]{2,1,0:T(1,128)} %param.13) | copy-start | bytes 196
  2.9 10.8 %copy-start.4 = (bf16[2,1,4,128,192]{3,4,2,1,0:T(8,128)(2,1)S(1)}, bf16[2,1,4,128,192]{3,4,2,1,0:T(8,128)(2,1)}, u32[]{:S(2)}) copy-start(bf16[2,1,4,128,192]{3,4,2,1,0:T(8,128)(2,1)} %param.8) | copy-start | bytes 1179652
  2.9 64.5 %all-to-all-start = ((bf16[16,144,512]{2,1,0:T(8,128)(2,1)}), bf16[16,144,512]{2,1,0:T(8,128)(2,1)S(1)}, u32[]{:S(2)}, u32[]{:S(2)}) async-start(bf16[16,144,512]{2,1,0:T(8,128)(2,1)} %shard_map.85), calls=%async_computation | async-start | bytes 4718592 | tf_op jit(solution)/shard_map/all_to_all | solution.py:318
  13.1 13.7 %collective-permute-start.13 = (s32[16]{0:T(128)S(1)}, s32[16]{0:T(128)S(1)}, u32[]{:S(2)}, u32[]{:S(2)}) collective-permute-start(s32[16]{0:T(128)S(1)} %bitcast.88), channel_id=1, source_target_pairs={{0,16},{16,0},{1,17},{17,1},{2,18},{18,2},{3,19},{19,3},{4,20},{20... | collective-permute-start | bytes 200 | tf_op jit(solution)/shard_map/ppermute | solution.py:310
  13.3 18.1 %collective-permute-start.6 = (bf16[2,8,128,256]{3,2,1,0:T(8,128)(2,1)}, bf16[2,8,128,256]{3,2,1,0:T(8,128)(2,1)}, u32[]{:S(2)}, u32[]{:S(2)}) collective-permute-start(bf16[2,8,128,256]{3,2,1,0:T(8,128)(2,1)} %own.2), channel_id=1, source_target_pairs={{0,16},{16,0},{1,17},{17,1},{2,18},{18,2},{3,19},{19,3},{4,20},{20... | collective-permute-start | bytes 3145736 | tf_op jit(solution)/shard_map/ppermute | solution.py:310
  14.7 8.0 %collective-permute-start.1 = (bf16[4,32,128]{2,1,0:T(8,128)(2,1)S(1)}, bf16[4,32,128]{2,1,0:T(8,128)(2,1)S(1)}, u32[]{:S(2)}, u32[]{:S(2)}) collective-permute-start(bf16[4,32,128]{2,1,0:T(8,128)(2,1)S(1)} %get-tuple-element.26), channel_id=1, source_target_pairs={{0,2},{1,3},{2,0},{3,1},{4,6},{5,7},{6,4},{7,5},{8,10},{9,11},{10,... | collective-permute-start | bytes 98312 | tf_op jit(solution)/shard_map/ppermute | solution.py:298
  17.5 6.0 %collective-permute-start = (bf16[4,32,128]{2,1,0:T(8,128)(2,1)S(1)}, bf16[4,32,128]{2,1,0:T(8,128)(2,1)S(1)}, u32[]{:S(2)}, u32[]{:S(2)}) collective-permute-start(bf16[4,32,128]{2,1,0:T(8,128)(2,1)S(1)} %get-tuple-element.27), channel_id=1, source_target_pairs={{0,1},{1,2},{2,3},{3,0},{4,5},{5,6},{6,7},{7,4},{8,9},{9,10},{10,1... | collective-permute-start | bytes 98312 | tf_op jit(solution)/shard_map/ppermute | solution.py:298
  17.8 5.7 %collective-permute-start.2 = (bf16[4,32,128]{2,1,0:T(8,128)(2,1)S(1)}, bf16[4,32,128]{2,1,0:T(8,128)(2,1)S(1)}, u32[]{:S(2)}, u32[]{:S(2)}) collective-permute-start(bf16[4,32,128]{2,1,0:T(8,128)(2,1)S(1)} %get-tuple-element.28), channel_id=1, source_target_pairs={{0,3},{1,0},{2,1},{3,2},{4,7},{5,4},{6,5},{7,6},{8,11},{9,8},{10,9... | collective-permute-start | bytes 98312 | tf_op jit(solution)/shard_map/ppermute | solution.py:298
  22.6 25.0 %collective-permute-start.14 = (bf16[2,8,256,128]{3,2,1,0:T(8,128)(2,1)}, bf16[2,8,256,128]{3,2,1,0:T(8,128)(2,1)}, u32[]{:S(2)}, u32[]{:S(2)}) collective-permute-start(bf16[2,8,256,128]{3,2,1,0:T(8,128)(2,1)} %own.3), channel_id=1, source_target_pairs={{0,16},{16,0},{1,17},{17,1},{2,18},{18,2},{3,19},{19,3},{4,20},{20... | collective-permute-start | bytes 3145736 | tf_op jit(solution)/shard_map/ppermute | solution.py:310
  23.6 4.5 %collective-permute-start.5 = (bf16[4,32,128]{2,1,0:T(8,128)(2,1)S(1)}, bf16[4,32,128]{2,1,0:T(8,128)(2,1)S(1)}, u32[]{:S(2)}, u32[]{:S(2)}) collective-permute-start(bf16[4,32,128]{2,1,0:T(8,128)(2,1)S(1)} %get-tuple-element.22), channel_id=1, source_target_pairs={{0,12},{1,13},{2,14},{3,15},{4,0},{5,1},{6,2},{7,3},{8,4},{9,5},{1... | collective-permute-start | bytes 98312 | tf_op jit(solution)/shard_map/ppermute | solution.py:298
  26.4 4.6 %collective-permute-start.4 = (bf16[4,32,128]{2,1,0:T(8,128)(2,1)S(1)}, bf16[4,32,128]{2,1,0:T(8,128)(2,1)S(1)}, u32[]{:S(2)}, u32[]{:S(2)}) collective-permute-start(bf16[4,32,128]{2,1,0:T(8,128)(2,1)S(1)} %get-tuple-element.23), channel_id=1, source_target_pairs={{0,8},{1,9},{2,10},{3,11},{4,12},{5,13},{6,14},{7,15},{8,0},{9,1},... | collective-permute-start | bytes 98312 | tf_op jit(solution)/shard_map/ppermute | solution.py:298
  26.8 7.1 %copy-start.10 = (s32[16]{0:T(128)}, s32[16]{0:T(128)S(1)}, u32[]{:S(2)}) copy-start(s32[16]{0:T(128)S(1)} %collective-permute-done.13) | copy-start | bytes 196
  26.8 4.6 %collective-permute-start.3 = (bf16[4,32,128]{2,1,0:T(8,128)(2,1)S(1)}, bf16[4,32,128]{2,1,0:T(8,128)(2,1)S(1)}, u32[]{:S(2)}, u32[]{:S(2)}) collective-permute-start(bf16[4,32,128]{2,1,0:T(8,128)(2,1)S(1)} %get-tuple-element.24), channel_id=1, source_target_pairs={{0,4},{1,5},{2,6},{3,7},{4,8},{5,9},{6,10},{7,11},{8,12},{9,13},{1... | collective-permute-start | bytes 98312 | tf_op jit(solution)/shard_map/ppermute | solution.py:298
  31.4 6.0 %copy-start.7 = (s32[2,16]{1,0:T(2,128)S(1)}, s32[2,16]{1,0:T(2,128)}, u32[]{:S(2)}) copy-start(s32[2,16]{1,0:T(2,128)} %rev.3) | copy-start | bytes 388
  31.4 6.0 %copy-start.9 = (s32[1,1,16]{2,1,0:T(1,128)S(1)}, s32[1,1,16]{2,1,0:T(1,128)}, u32[]{:S(2)}) copy-start(s32[1,1,16]{2,1,0:T(1,128)} %param.13) | copy-start | bytes 196
  31.4 6.0 %copy-start.11 = (s32[2]{0:T(128)S(1)}, s32[2]{0:T(128)}, u32[]{:S(2)}) copy-start(s32[2]{0:T(128)} %iota_multiply_fusion) | copy-start | bytes 28
  33.9 13.8 %copy-start.3 = (bf16[2,8,256,128]{3,2,1,0:T(8,128)(2,1)S(1)}, bf16[2,8,256,128]{3,2,1,0:T(8,128)(2,1)}, u32[]{:S(2)}) copy-start(bf16[2,8,256,128]{3,2,1,0:T(8,128)(2,1)} %own.3) | copy-start | bytes 3145732
  34.7 8.0 %collective-permute-start.8 = (bf16[4,32,512]{2,1,0:T(8,128)(2,1)}, bf16[4,32,512]{2,1,0:T(8,128)(2,1)}, u32[]{:S(2)}, u32[]{:S(2)}) collective-permute-start(bf16[4,32,512]{2,1,0:T(8,128)(2,1)} %get-tuple-element.18), channel_id=1, source_target_pairs={{0,2},{1,3},{2,0},{3,1},{4,6},{5,7},{6,4},{7,5},{8,10},{9,11},{10,... | collective-permute-start | bytes 393224 | tf_op jit(solution)/shard_map/ppermute | solution.py:298
  34.7 9.0 %collective-permute-start.7 = (bf16[4,32,512]{2,1,0:T(8,128)(2,1)}, bf16[4,32,512]{2,1,0:T(8,128)(2,1)}, u32[]{:S(2)}, u32[]{:S(2)}) collective-permute-start(bf16[4,32,512]{2,1,0:T(8,128)(2,1)} %get-tuple-element.19), channel_id=1, source_target_pairs={{0,1},{1,2},{2,3},{3,0},{4,5},{5,6},{6,7},{7,4},{8,9},{9,10},{10,1... | collective-permute-start | bytes 393224 | tf_op jit(solution)/shard_map/ppermute | solution.py:298
  36.2 7.5 %collective-permute-start.9 = (bf16[4,32,512]{2,1,0:T(8,128)(2,1)}, bf16[4,32,512]{2,1,0:T(8,128)(2,1)}, u32[]{:S(2)}, u32[]{:S(2)}) collective-permute-start(bf16[4,32,512]{2,1,0:T(8,128)(2,1)} %get-tuple-element.20), channel_id=1, source_target_pairs={{0,3},{1,0},{2,1},{3,2},{4,7},{5,4},{6,5},{7,6},{8,11},{9,8},{10,9... | collective-permute-start | bytes 393224 | tf_op jit(solution)/shard_map/ppermute | solution.py:298
  42.6 4.3 %copy-start.5 = (s32[16,128]{1,0:T(8,128)S(1)}, s32[16,128]{1,0:T(8,128)}, u32[]{:S(2)}) copy-start(s32[16,128]{1,0:T(8,128)} %add.42) | copy-start | bytes 24580
  44.9 5.3 %collective-permute-start.12 = (bf16[4,32,512]{2,1,0:T(8,128)(2,1)S(1)}, bf16[4,32,512]{2,1,0:T(8,128)(2,1)S(1)}, u32[]{:S(2)}, u32[]{:S(2)}) collective-permute-start(bf16[4,32,512]{2,1,0:T(8,128)(2,1)S(1)} %get-tuple-element.14), channel_id=1, source_target_pairs={{0,12},{1,13},{2,14},{3,15},{4,0},{5,1},{6,2},{7,3},{8,4},{9,5},{1... | collective-permute-start | bytes 393224 | tf_op jit(solution)/shard_map/ppermute | solution.py:298
  45.2 5.6 %collective-permute-start.11 = (bf16[4,32,512]{2,1,0:T(8,128)(2,1)S(1)}, bf16[4,32,512]{2,1,0:T(8,128)(2,1)S(1)}, u32[]{:S(2)}, u32[]{:S(2)}) collective-permute-start(bf16[4,32,512]{2,1,0:T(8,128)(2,1)S(1)} %get-tuple-element.15), channel_id=1, source_target_pairs={{0,8},{1,9},{2,10},{3,11},{4,12},{5,13},{6,14},{7,15},{8,0},{9,1},... | collective-permute-start | bytes 393224 | tf_op jit(solution)/shard_map/ppermute | solution.py:298
  46.2 6.5 %collective-permute-start.10 = (bf16[4,32,512]{2,1,0:T(8,128)(2,1)S(1)}, bf16[4,32,512]{2,1,0:T(8,128)(2,1)S(1)}, u32[]{:S(2)}, u32[]{:S(2)}) collective-permute-start(bf16[4,32,512]{2,1,0:T(8,128)(2,1)S(1)} %get-tuple-element.16), channel_id=1, source_target_pairs={{0,4},{1,5},{2,6},{3,7},{4,8},{5,9},{6,10},{7,11},{8,12},{9,13},{1... | collective-permute-start | bytes 393224 | tf_op jit(solution)/shard_map/ppermute | solution.py:298
  47.7 5.2 %copy-start.6 = (bf16[4,576]{1,0:T(4,128)(2,1)S(1)}, bf16[4,576]{1,0:T(4,128)(2,1)}, u32[]{:S(2)}) copy-start(bf16[4,576]{1,0:T(4,128)(2,1)} %dynamic-slice_bitcast_fusion) | copy-start | bytes 13828
  49.1 1.1 %copy-start.1 = (bf16[5,512,256]{2,1,0:T(8,128)(2,1)}, bf16[5,512,256]{2,1,0:T(8,128)(2,1)S(1)}, u32[]{:S(2)}) copy-start(bf16[5,512,256]{2,1,0:T(8,128)(2,1)S(1)} %shard_map.84.weight) | copy-start | bytes 3932164
  67.4 21.5 %copy-start.2 = (bf16[5,512,256]{2,1,0:T(8,128)(2,1)S(1)}, bf16[5,512,256]{2,1,0:T(8,128)(2,1)}, u32[]{:S(2)}) copy-start(bf16[5,512,256]{2,1,0:T(8,128)(2,1)} %copy-done.1) | copy-start | bytes 3932164
  89.7 3.0 %collective-permute-start.15 = (bf16[16,4,8,128]{3,2,1,0:T(8,128)(2,1)S(1)}, bf16[16,4,8,128]{3,2,1,0:T(8,128)(2,1)S(1)}, u32[]{:S(2)}, u32[]{:S(2)}) collective-permute-start(bf16[16,4,8,128]{3,2,1,0:T(8,128)(2,1)S(1)} %bitcast.73), channel_id=1, source_target_pairs={{0,16},{16,0},{1,17},{17,1},{2,18},{18,2},{3,19},{19,3},{4,20},{20... | collective-permute-start | bytes 393224 | tf_op jit(solution)/shard_map/ppermute | solution.py:310

commit v5 on v4

--- a/solution.py
+++ b/solution.py
@@ -3,6 +3,7 @@
 
 import jax
 import jax.numpy as jnp
+import numpy as np
 from jax import lax
 from jax.experimental import pallas as pl
 from jax.experimental.pallas import tpu as pltpu
@@ -23,6 +24,8 @@
 ROWS = PEERS * BLOCK
 TILE = 512
 CHUNK = 2
+COLUMN = (12, 15, 2, 1, 8, 0, 13, 6, 9, 3, 7, 4, 11, 10, 14, 5)
+PLANE = (2, 11, 3, 10, 0, 4, 7, 5, 14, 12, 6, 9, 13, 8, 1, 15)
 HALF = KV_RANK // 2
 DEAD = -1e30
 SCALE = 1.0 / math.sqrt(NOPE + ROPE)
@@ -33,9 +36,11 @@
 ANY = pl.BlockSpec(memory_space=pl.ANY)
 
 
-def send_kernel(send_to, pages, out, target_of, held, packed, target_sem, in_sem, lat_sem, rope_sem):
-    targets = pltpu.make_async_copy(send_to, target_of, target_sem)
+def send_kernel(send_to, order, pages, out, target_of, rank_of, held, packed, target_sem, in_sem, lat_sem, rope_sem):
+    targets = pltpu.make_async_copy(send_to, target_of, target_sem.at[0])
+    ranks = pltpu.make_async_copy(order, rank_of, target_sem.at[1])
     targets.start()
+    ranks.start()
 
     def fetch(part):
         some = pl.ds(part * CHUNK, CHUNK)
@@ -45,13 +50,14 @@
         target = target_of[page]
         return pltpu.make_async_copy(
             held.at[layer, page, :, pl.ds(0, KV_RANK)],
-            out.at[target // 2 * 2 + layer, pl.ds(target % 2 * PAGE, PAGE)],
+            out.at[rank_of[target // 2 * 2 + layer], pl.ds(target % 2 * PAGE, PAGE)],
             lat_sem.at[layer, page],
         )
 
     for part in range(PEERS // CHUNK):
         fetch(part).start()
     targets.wait()
+    ranks.wait()
     for part in range(PEERS // CHUNK):
         fetch(part).wait()
         for page in range(part * CHUNK, (part + 1) * CHUNK):
@@ -61,7 +67,7 @@
             target = target_of[page]
             columns = pl.ds(pl.multiple_of(target % 2 * (KV_RANK // 2), KV_RANK // 2), KV_RANK // 2)
             for layer in range(2):
-                packed[target // 2 * 2 + layer, :, columns] = jnp.concatenate(
+                packed[rank_of[target // 2 * 2 + layer], :, columns] = jnp.concatenate(
                     [held[layer, page, 16 * k : 16 * k + 16, KV_RANK:] for k in range(PAGE // 16)],
                     axis=1,
                 )
@@ -77,20 +83,21 @@
     return pl.pallas_call(
         send_kernel,
         out_shape=jax.ShapeDtypeStruct((PEERS, PAIR_ROWS, KV_RANK), jnp.bfloat16),
-        in_specs=[ANY, ANY],
+        in_specs=[ANY, ANY, ANY],
         out_specs=ANY,
         scratch_shapes=[
             pltpu.SMEM((PEERS,), jnp.int32),
+            pltpu.SMEM((PEERS,), jnp.int32),
             pltpu.VMEM(pages.shape, jnp.bfloat16),
             pltpu.VMEM((PEERS, 16, KV_RANK), jnp.bfloat16),
-            pltpu.SemaphoreType.DMA,
+            pltpu.SemaphoreType.DMA((2,)),
             pltpu.SemaphoreType.DMA((PEERS // CHUNK,)),
             pltpu.SemaphoreType.DMA((2, PEERS)),
             pltpu.SemaphoreType.DMA,
         ],
         compiler_params=pltpu.CompilerParams(vmem_limit_bytes=60 << 20),
         cost_estimate=pl.CostEstimate(flops=0, bytes_accessed=5 << 20, transcendentals=0),
-    )(send_to, pages)
+    )(send_to, jnp.asarray(np.argsort(COLUMN), jnp.int32), pages)
 
 
 def around(place, step, sign):
@@ -179,7 +186,9 @@
         both = jnp.dot(rows, weight[p], preferred_element_type=jnp.float32)
         result = jnp.where(head == 2 * p, both[:, :VDIM], result)
         result = jnp.where(head == 2 * p + 1, both[:, VDIM:], result)
-    out[...] = result.astype(jnp.bfloat16)
+    result = result.astype(jnp.bfloat16)
+    for k, place in enumerate(PLANE):
+        out[place * BLOCK : (place + 1) * BLOCK, :] = result[k * BLOCK : (k + 1) * BLOCK]
 
 
 def project_values(latent, weight):
@@ -264,8 +273,8 @@
         total = total + jnp.sum(added, axis=1, keepdims=True)
         result = (summed * (1.0 / total)).astype(jnp.bfloat16)
         for k in range(TILE // BLOCK):
-            j = around(where[2], first // BLOCK + k, -1)
-            out[j] = result[k * BLOCK : (k + 1) * BLOCK]
+            rank = where[3 + around(where[2], first // BLOCK + k, -1)]
+            out[rank] = result[k * BLOCK : (k + 1) * BLOCK]
 
     for first in range(0, ROWS, TILE):
         tile(first)
@@ -306,6 +315,12 @@
     return back.reshape((ROWS,) + back.shape[3:])
 
 
+def ordered_all_to_all(value, axis, order):
+    return lax.all_to_all(
+        value, axis, split_axis=0, concat_axis=0, tiled=True, axis_index_groups=[list(order)]
+    )
+
+
 def swapped(value):
     return lax.ppermute(value, "seq", [(0, 1), (1, 0)])
 
@@ -313,9 +328,10 @@
 def shards(queries, w_absorb_k, w_absorb_v, prefill_pages, send_to, slot_of, lengths, new_latents):
     layer = lax.axis_index("seq")
     where = jnp.stack([lax.axis_index("group"), layer, lax.axis_index("req")]).astype(jnp.int32)
+    where = jnp.concatenate([where, jnp.asarray(np.argsort(PLANE), jnp.int32)])
 
     sent = gather_pages(send_to[0, 0], prefill_pages[0, 0])
-    pages = lax.all_to_all(sent, ("group", "seq"), split_axis=0, concat_axis=0, tiled=True)
+    pages = ordered_all_to_all(sent, ("group", "seq"), COLUMN)
 
     own_slot = slot_of[0, 0]
     nope, rope = split_queries(where, queries)
@@ -333,12 +349,15 @@
         [
             jnp.concatenate([q_lat, rope, jnp.zeros_like(rope)], axis=1),
             jnp.pad(fresh, ((0, 16 - STEPS), (0, ROPE))),
-            jnp.pad(live.reshape(PEERS, PAIR).astype(jnp.bfloat16), ((0, 0), (0, KV_RANK))),
+            jnp.pad(
+                live.reshape(PEERS, PAIR).astype(jnp.bfloat16)[np.array(COLUMN)],
+                ((0, 0), (0, KV_RANK)),
+            ),
         ]
     )
     inputs, values = lax.optimization_barrier((inputs, values))
     latent_out = attend(where, inputs, pages)
-    latent_heads = lax.all_to_all(latent_out, "req", split_axis=0, concat_axis=0, tiled=True)
+    latent_heads = ordered_all_to_all(latent_out, "req", PLANE)
     head_out = project_values(latent_heads.reshape(ROWS, KV_RANK), values)
     own = head_out.reshape(PEERS, STEPS, HEADS_PER, VDIM)
     got = swapped(own)

time: 93.9 us -> 91 us (0.969)
  waiting for transfers between devices: 22.3 us -> 13.7 us
  local copies, waits for them, and re-layouts: 8.1 us -> 10.8 us
  other arithmetic: 4.61 us -> 6.91 us
  blocking collectives: 17.1 us -> 15.6 us
  starting transfers between devices: 27.9 us -> 29.3 us
    all_to_all x1, waiting for transfers between devices: 14.4 us -> 6.41 us  [ordered_all_to_all(): lax.all_to_all(value, axis, split_axis=0, concat_axis=0, tiled=True, axis...]
    gather x0 -> x1, local copies, waits for them, and re-layouts: none -> 1.96 us  [shards(): live.reshape(PEERS, PAIR).astype(jnp.bfloat16)[np.array(COLUMN)]]
    all_to_all x1, blocking collectives: 17.1 us -> 15.6 us  [ordered_all_to_all(): lax.all_to_all(value, axis, split_axis=0, concat_axis=0, tiled=True, axis...]
    convert_element_type x0 -> x1, other arithmetic: none -> 1.23 us  [shards(): live.reshape(PEERS, PAIR).astype(jnp.bfloat16)[np.array(COLUMN)]]
    another operation x2, other arithmetic: 0.09 us -> 1.12 us  [exchange(): jnp.stack([rows[0]] + [shifted(rows[d], d, 0) for d in range(1, SIDE)])]
    all_to_all x1, starting transfers between devices: 10.1 us -> 11.1 us  [ordered_all_to_all(): lax.all_to_all(value, axis, split_axis=0, concat_axis=0, tiled=True, axis...]
  transfers between devices with their start and end apart: 17 -> 17, of which waited for: 7 -> 6; matrix products, arithmetic and copies ran while one was open for 12% -> 18% of each run, Pallas kernels for 5% -> 5%
where the time goes in v5:
time: 91 us; the launch traced here: 90 us
  starting transfers between devices  29.3 us (32%)
  blocking collectives  15.6 us (17%)
  waiting for transfers between devices  13.7 us (15%)
  Pallas kernels  12.7 us (14%)
  local copies, waits for them, and re-layouts  10.8 us (12%)
  other arithmetic  6.91 us (8%)
  between operations  0.92 us (1%)
    all_to_all x1, blocking collectives, ordered_all_to_all(): lax.all_to_all(value, axis, split_axis=0, concat_axis=0, tiled=True, axis...  15.6 us
    ppermute x12, starting transfers between devices, shifted(): return lax.ppermute(value, 'req', pairs)  14 us
    all_to_all x1, starting transfers between devices, ordered_all_to_all(): lax.all_to_all(value, axis, split_axis=0, concat_axis=0, tiled=True, axis...  11.1 us
    all_to_all x1, waiting for transfers between devices, ordered_all_to_all(): lax.all_to_all(value, axis, split_axis=0, concat_axis=0, tiled=True, axis...  6.41 us
    ppermute x12, waiting for transfers between devices, shifted(): return lax.ppermute(value, 'req', pairs)  6.33 us
    pallas_call x1, Pallas kernels, attend(): pl.pallas_call(attend_kernel, out_shape=jax.ShapeDtypeStruct((PEERS, BLOC...  4.48 us
    ppermute x4, starting transfers between devices, swapped(): return lax.ppermute(value, 'seq', [(0, 1), (1, 0)])  4.2 us
    add x4, local copies, waits for them, and re-layouts, shards(): live = starts[:, :, None] + jnp.arange(PAGE, dtype=jnp.int32) < lengths[0]  3.4 us
  transfers between devices with their start and end apart: 17, of which 6 were waited for; matrix products, arithmetic and copies ran while one was open for 18% of the time, Pallas kernels for 5%

profile of v5, /device:TPU:1, one launch (start us, length us, event | category | flops | bytes accessed | tf_op | source)
XLA Modules:
  0.0 90.0 jit_solution(9051741759589746878)
XLA Ops:
  0.0 2.9 %shard_map.121 = bf16[16,144,512]{2,1,0:T(8,128)(2,1)} custom-call(s32[16]{0:T(128)} %bitcast.90, s32[16]{0:T(128)} %constant.40.clone.order, bf16[2,16,64,576]{3,2,1,0:T(8,128)(2,1)} %bitcast.76), custom_call_target="tpu_custom_call" | custom-call | bytes 5242880 | tf_op jit(solution)/shard_map/pallas_call | solution.py:83
  2.9 11.1 %all-to-all-start = ((bf16[16,144,512]{2,1,0:T(8,128)(2,1)}), bf16[16,144,512]{2,1,0:T(8,128)(2,1)S(1)}, u32[]{:S(2)}, u32[]{:S(2)}) async-start(bf16[16,144,512]{2,1,0:T(8,128)(2,1)} %shard_map.121), calls=%async_computation | async-start | bytes 4718592 | tf_op jit(solution)/shard_map/all_to_all | solution.py:319
  15.7 2.8 %collective-permute-start.1 = (bf16[4,32,128]{2,1,0:T(8,128)(2,1)S(1)}, bf16[4,32,128]{2,1,0:T(8,128)(2,1)S(1)}, u32[]{:S(2)}, u32[]{:S(2)}) collective-permute-start(bf16[4,32,128]{2,1,0:T(8,128)(2,1)S(1)} %get-tuple-element.26), channel_id=1, source_target_pairs={{0,2},{1,3},{2,0},{3,1},{4,6},{5,7},{6,4},{7,5},{8,10},{9,11},{10,... | collective-permute-start | bytes 98312 | tf_op jit(solution)/shard_map/ppermute | solution.py:307
  18.8 2.4 %collective-permute-start.2 = (bf16[4,32,128]{2,1,0:T(8,128)(2,1)S(1)}, bf16[4,32,128]{2,1,0:T(8,128)(2,1)S(1)}, u32[]{:S(2)}, u32[]{:S(2)}) collective-permute-start(bf16[4,32,128]{2,1,0:T(8,128)(2,1)S(1)} %get-tuple-element.28), channel_id=1, source_target_pairs={{0,3},{1,0},{2,1},{3,2},{4,7},{5,4},{6,5},{7,6},{8,11},{9,8},{10,9... | collective-permute-start | bytes 98312 | tf_op jit(solution)/shard_map/ppermute | solution.py:307
  24.2 1.3 %collective-permute-start.14 = (bf16[2,8,256,128]{3,2,1,0:T(8,128)(2,1)}, bf16[2,8,256,128]{3,2,1,0:T(8,128)(2,1)}, u32[]{:S(2)}, u32[]{:S(2)}) collective-permute-start(bf16[2,8,256,128]{3,2,1,0:T(8,128)(2,1)} %own.3), channel_id=1, source_target_pairs={{0,16},{16,0},{1,17},{17,1},{2,18},{18,2},{3,19},{19,3},{4,20},{20... | collective-permute-start | bytes 3145736 | tf_op jit(solution)/shard_map/ppermute | solution.py:325
  25.5 2.8 %collective-permute-start.5 = (bf16[4,32,128]{2,1,0:T(8,128)(2,1)S(1)}, bf16[4,32,128]{2,1,0:T(8,128)(2,1)S(1)}, u32[]{:S(2)}, u32[]{:S(2)}) collective-permute-start(bf16[4,32,128]{2,1,0:T(8,128)(2,1)S(1)} %get-tuple-element.22), channel_id=1, source_target_pairs={{0,12},{1,13},{2,14},{3,15},{4,0},{5,1},{6,2},{7,3},{8,4},{9,5},{1... | collective-permute-start | bytes 98312 | tf_op jit(solution)/shard_map/ppermute | solution.py:307
  29.9 3.0 %collective-permute-done.4 = bf16[4,32,128]{2,1,0:T(8,128)(2,1)S(1)} collective-permute-done((bf16[4,32,128]{2,1,0:T(8,128)(2,1)S(1)}, bf16[4,32,128]{2,1,0:T(8,128)(2,1)S(1)}, u32[]{:S(2)}, u32[]{:S(2)}) %collective-permute-start.4) | collective-permute-done | bytes 32800 | tf_op jit(solution)/shard_map/ppermute | solution.py:307
  33.3 2.5 %shard_map.119 = bf16[512,512]{1,0:T(8,128)(2,1)S(1)} custom-call(s32[19]{0:T(128)S(1)} %pad_add_fusion.1.where, bf16[512,128]{1,0:T(8,128)(2,1)S(1)} %bitcast.71, bf16[2,8,128,256]{3,2,1,0:T(8,128)(2,1)} %own.2, bf16[2,8,128,256]{3,2,1,0:T(8,128)(2,1)} %collective-permute-done.6.got), custom_call_target="tpu_custom_call" | custom-call | flops 536870912 | bytes 2097152 | tf_op jit(solution)/shard_map/pallas_call | solution.py:210
  35.8 0.8 fusion.7
  36.9 2.4 %collective-permute-start.9 = (bf16[4,32,512]{2,1,0:T(8,128)(2,1)}, bf16[4,32,512]{2,1,0:T(8,128)(2,1)}, u32[]{:S(2)}, u32[]{:S(2)}) collective-permute-start(bf16[4,32,512]{2,1,0:T(8,128)(2,1)} %get-tuple-element.20), channel_id=1, source_target_pairs={{0,3},{1,0},{2,1},{3,2},{4,7},{5,4},{6,5},{7,6},{8,11},{9,8},{10,9... | collective-permute-start | bytes 393224 | tf_op jit(solution)/shard_map/ppermute | solution.py:307
  39.3 1.3 %add_bitcast_fusion = s32[16,2]{0,1:T(2,128)} fusion(s32[2,16]{1,0:T(2,128)S(1)} %copy-done.9, pred[]{:T(512)S(6)} %eq.4, s32[2]{0:T(128)S(1)} %copy-done.15, s32[1,16]{1,0:T(1,128)} %bitcast.89, s32[1,16]{1,0:T(1,128)S(1)} %bitcast.87), kind=kLoop, calls=%fused_computation.31 | loop fusion | flops 128 | bytes 393 | tf_op jit(solution)/shard_map/add | solution.py:346
  40.6 1.3 %copy.20 = s32[16,2]{1,0:T(8,128)} copy(s32[16,2]{0,1:T(2,128)} %add_bitcast_fusion) | data formatting | bytes 256 | tf_op jit(solution)/shard_map/add | solution.py:346
  41.9 1.4 %add.46 = s32[16,2,64]{2,1,0:T(2,128)} broadcast(s32[16,2]{1,0:T(8,128)} %copy.20), dimensions={0,1} | broadcast | bytes 8320 | tf_op jit(solution)/shard_map/add | solution.py:347
  43.3 1.4 %add.47 = s32[16,128]{1,0:T(8,128)} reshape(s32[16,2,64]{2,1,0:T(2,128)} %add.46) | data formatting | bytes 16384 | tf_op jit(solution)/shard_map/add | solution.py:347
  44.7 1.2 %collective-permute-done.7 = bf16[4,32,512]{2,1,0:T(8,128)(2,1)} collective-permute-done((bf16[4,32,512]{2,1,0:T(8,128)(2,1)}, bf16[4,32,512]{2,1,0:T(8,128)(2,1)}, u32[]{:S(2)}, u32[]{:S(2)}) %collective-permute-start.7) | collective-permute-done | bytes 131104 | tf_op jit(solution)/shard_map/ppermute | solution.py:307
  45.9 1.2 %pad_maximum_fusion = bf16[4,4,32,512]{3,2,1,0:T(8,128)(2,1)S(1)} fusion(bf16[4,1,32,512]{3,2,1,0:T(8,128)(2,1)} %bitcast.23, bf16[4,1,32,512]{3,2,1,0:T(8,128)(2,1)} %bitcast.21, bf16[4,1,32,512]{3,2,1,0:T(8,128)(2,1)} %bitcast.19, bf16[4,1,32,512]{3,2,1,0:T(8,128)(2,1)} %get-tuple-element.17), kind=kLoop, calls=%fused_computation.9 | loop fusion | flops 786432 | bytes 1048576 | tf_op jit(solution)/shard_map/stack | solution.py:313
  47.0 0.8 fusion.6
  48.1 0.9 %collective-permute-start.11 = (bf16[4,32,512]{2,1,0:T(8,128)(2,1)}, bf16[4,32,512]{2,1,0:T(8,128)(2,1)}, u32[]{:S(2)}, u32[]{:S(2)}) collective-permute-start(bf16[4,32,512]{2,1,0:T(8,128)(2,1)} %get-tuple-element.15), channel_id=1, source_target_pairs={{0,8},{1,9},{2,10},{3,11},{4,12},{5,13},{6,14},{7,15},{8,0},{9,1},... | collective-permute-start | bytes 393224 | tf_op jit(solution)/shard_map/ppermute | solution.py:307
  49.1 0.8 collective-permute-start.10
  49.9 1.2 %fusion.5 = bf16[16,128]{1,0:T(8,128)(2,1)} fusion(s32[16,128]{1,0:T(8,128)S(1)} %copy-done.6, s32[]{:T(128)} %bitcast.69, s32[128]{0:T(128)} %add.49), kind=kLoop, calls=%fused_computation.27 | loop fusion | flops 6144 | bytes 12804 | tf_op jit(solution)/shard_map/convert_element_type | solution.py:353
  51.1 2.0 %gather_fusion = bf16[16,128]{1,0:T(8,128)(2,1)} fusion(bf16[16,128]{1,0:T(8,128)(2,1)} %fusion.5, s32[1024]{0:T(1024)} %pad_clamp_fusion), kind=kCustom, calls=%fused_computation | custom fusion | bytes 8256 | tf_op jit(solution)/shard_map/gather | solution.py:353
  53.1 1.5 %shard_map.120.weight = bf16[5,512,256]{2,1,0:T(8,128)(2,1)S(1)} custom-call(s32[19]{0:T(128)S(1)} %pad_add_fusion.1.where, bf16[2,8,256,128]{3,2,1,0:T(8,128)(2,1)S(1)} %copy-done.3, bf16[2,8,256,128]{3,2,1,0:T(8,128)(2,1)} %collective-permute-done.14.got), custom_call_target="tpu_custom_call" | custom-call | bytes 3145728 | tf_op jit(solution)/shard_map/pallas_call | solution.py:171
  54.6 1.1 %copy-done.1 = bf16[5,512,256]{2,1,0:T(8,128)(2,1)} copy-done((bf16[5,512,256]{2,1,0:T(8,128)(2,1)}, bf16[5,512,256]{2,1,0:T(8,128)(2,1)S(1)}, u32[]{:S(2)}) %copy-start.1) | copy-done | bytes 1310744
  55.6 1.8 %collective-permute-done.10 = bf16[4,32,512]{2,1,0:T(8,128)(2,1)} collective-permute-done((bf16[4,32,512]{2,1,0:T(8,128)(2,1)}, bf16[4,32,512]{2,1,0:T(8,128)(2,1)}, u32[]{:S(2)}, u32[]{:S(2)}) %collective-permute-start.10) | collective-permute-done | bytes 131104 | tf_op jit(solution)/shard_map/ppermute | solution.py:307
  57.5 1.1 %pad_maximum_fusion.1 = bf16[4,4,32,512]{3,2,1,0:T(8,128)(2,1)S(1)} fusion(bf16[1,4,32,512]{3,2,1,0:T(8,128)(2,1)} %bitcast.29, bf16[1,4,32,512]{3,2,1,0:T(8,128)(2,1)} %bitcast.27, bf16[1,4,32,512]{3,2,1,0:T(8,128)(2,1)} %bitcast.25, bf16[1,4,32,512]{3,2,1,0:T(8,128)(2,1)S(1)} %copy-done.4), kind=kLoop, calls=%fused_computation.10 | loop fusion | flops 786432 | bytes 1048576 | tf_op jit(solution)/shard_map/stack | solution.py:314
  58.8 6.4 %all-to-all-done.pages = bf16[16,144,512]{2,1,0:T(8,128)(2,1)S(1)} async-done(((bf16[16,144,512]{2,1,0:T(8,128)(2,1)}), bf16[16,144,512]{2,1,0:T(8,128)(2,1)S(1)}, u32[]{:S(2)}, u32[]{:S(2)}) %all-to-all-start) | async-done | bytes 2359328 | tf_op jit(solution)/shard_map/all_to_all | solution.py:319
  65.2 4.5 %shard_map.122 = bf16[16,32,512]{2,1,0:T(8,128)(2,1)S(1)} custom-call(s32[19]{0:T(128)S(1)} %pad_add_fusion.1.where, bf16[544,640]{1,0:T(8,128)(2,1)S(1)} %fusion.4.inputs, bf16[16,144,512]{2,1,0:T(8,128)(2,1)S(1)} %all-to-all-done.pages), custom_call_target="tpu_custom_call" | custom-call | flops 2281701376 | bytes 4194304 | tf_op jit(solution)/shard_map/pallas_call | solution.py:285
  69.6 15.6 %all_to_all.10 = bf16[16,32,512]{2,1,0:T(8,128)(2,1)S(1)} all-to-all(bf16[16,32,512]{2,1,0:T(8,128)(2,1)S(1)} %shard_map.122), channel_id=1, replica_groups={{2,11,3,10,0,4,7,5,14,12,6,9,13,8,1,15},{18,27,19,26,16,20,23,21,30,28,..., dimensions={0} | all-to-all | bytes 1048576 | tf_op jit(solution)/shard_map/all_to_all | solution.py:319
  85.3 0.7 shard_map.123
  86.0 2.3 %collective-permute-start.15 = (bf16[16,4,8,128]{3,2,1,0:T(8,128)(2,1)S(1)}, bf16[16,4,8,128]{3,2,1,0:T(8,128)(2,1)S(1)}, u32[]{:S(2)}, u32[]{:S(2)}) collective-permute-start(bf16[16,4,8,128]{3,2,1,0:T(8,128)(2,1)S(1)} %bitcast.73), channel_id=1, source_target_pairs={{0,16},{16,0},{1,17},{17,1},{2,18},{18,2},{3,19},{19,3},{4,20},{20... | collective-permute-start | bytes 393224 | tf_op jit(solution)/shard_map/ppermute | solution.py:325
  88.3 1.0 %collective-permute-done.15 = bf16[16,4,8,128]{3,2,1,0:T(8,128)(2,1)S(1)} collective-permute-done((bf16[16,4,8,128]{3,2,1,0:T(8,128)(2,1)S(1)}, bf16[16,4,8,128]{3,2,1,0:T(8,128)(2,1)S(1)}, u32[]{:S(2)}, u32[]{:S(2)}) %collective-permute-start.15) | collective-permute-done | bytes 131104 | tf_op jit(solution)/shard_map/ppermute | solution.py:325
  89.3 0.7 maximum_select_fusion
  (67 shorter events, 7.1 us)
Async XLA Ops:
  0.0 21.8 %copy-start = (bf16[2,1,4,576]{3,2,1,0:T(4,128)(2,1)S(1)}, bf16[2,1,4,576]{3,2,1,0:T(4,128)(2,1)}, u32[]{:S(2)}) copy-start(bf16[2,1,4,576]{3,2,1,0:T(4,128)(2,1)} %param.19) | copy-start | bytes 27652
  2.9 11.1 %copy-start.10 = (s32[1,1,16]{2,1,0:T(1,128)S(1)}, s32[1,1,16]{2,1,0:T(1,128)}, u32[]{:S(2)}) copy-start(s32[1,1,16]{2,1,0:T(1,128)} %param.17) | copy-start | bytes 196
  2.9 11.8 %copy-start.5 = (bf16[2,1,4,128,192]{3,4,2,1,0:T(8,128)(2,1)S(1)}, bf16[2,1,4,128,192]{3,4,2,1,0:T(8,128)(2,1)}, u32[]{:S(2)}) copy-start(bf16[2,1,4,128,192]{3,4,2,1,0:T(8,128)(2,1)} %param.12) | copy-start | bytes 1179652
  2.9 12.0 %copy-start.14 = (s32[16]{0:T(128)S(1)}, s32[16]{0:T(128)}, u32[]{:S(2)}) copy-start(s32[16]{0:T(128)} %constant.39.clone) | copy-start | bytes 196
  2.9 62.2 %all-to-all-start = ((bf16[16,144,512]{2,1,0:T(8,128)(2,1)}), bf16[16,144,512]{2,1,0:T(8,128)(2,1)S(1)}, u32[]{:S(2)}, u32[]{:S(2)}) async-start(bf16[16,144,512]{2,1,0:T(8,128)(2,1)} %shard_map.121), calls=%async_computation | async-start | bytes 4718592 | tf_op jit(solution)/shard_map/all_to_all | solution.py:319
  14.0 7.2 %copy-start.13 = (s32[16]{0:T(128)S(1)}, s32[16]{0:T(128)}, u32[]{:S(2)}) copy-start(s32[16]{0:T(128)} %constant.56) | copy-start | bytes 196
  14.1 14.6 %collective-permute-start.13 = (s32[16]{0:T(128)S(1)}, s32[16]{0:T(128)S(1)}, u32[]{:S(2)}, u32[]{:S(2)}) collective-permute-start(s32[16]{0:T(128)S(1)} %bitcast.85), channel_id=1, source_target_pairs={{0,16},{16,0},{1,17},{17,1},{2,18},{18,2},{3,19},{19,3},{4,20},{20... | collective-permute-start | bytes 200 | tf_op jit(solution)/shard_map/ppermute | solution.py:325
  14.6 18.7 %collective-permute-start.6 = (bf16[2,8,128,256]{3,2,1,0:T(8,128)(2,1)}, bf16[2,8,128,256]{3,2,1,0:T(8,128)(2,1)}, u32[]{:S(2)}, u32[]{:S(2)}) collective-permute-start(bf16[2,8,128,256]{3,2,1,0:T(8,128)(2,1)} %own.2), channel_id=1, source_target_pairs={{0,16},{16,0},{1,17},{17,1},{2,18},{18,2},{3,19},{19,3},{4,20},{20... | collective-permute-start | bytes 3145736 | tf_op jit(solution)/shard_map/ppermute | solution.py:325
  15.7 8.5 %collective-permute-start.1 = (bf16[4,32,128]{2,1,0:T(8,128)(2,1)S(1)}, bf16[4,32,128]{2,1,0:T(8,128)(2,1)S(1)}, u32[]{:S(2)}, u32[]{:S(2)}) collective-permute-start(bf16[4,32,128]{2,1,0:T(8,128)(2,1)S(1)} %get-tuple-element.26), channel_id=1, source_target_pairs={{0,2},{1,3},{2,0},{3,1},{4,6},{5,7},{6,4},{7,5},{8,10},{9,11},{10,... | collective-permute-start | bytes 98312 | tf_op jit(solution)/shard_map/ppermute | solution.py:307
  18.5 7.0 %collective-permute-start = (bf16[4,32,128]{2,1,0:T(8,128)(2,1)S(1)}, bf16[4,32,128]{2,1,0:T(8,128)(2,1)S(1)}, u32[]{:S(2)}, u32[]{:S(2)}) collective-permute-start(bf16[4,32,128]{2,1,0:T(8,128)(2,1)S(1)} %get-tuple-element.27), channel_id=1, source_target_pairs={{0,1},{1,2},{2,3},{3,0},{4,5},{5,6},{6,7},{7,4},{8,9},{9,10},{10,1... | collective-permute-start | bytes 98312 | tf_op jit(solution)/shard_map/ppermute | solution.py:307
  18.8 6.7 %collective-permute-start.2 = (bf16[4,32,128]{2,1,0:T(8,128)(2,1)S(1)}, bf16[4,32,128]{2,1,0:T(8,128)(2,1)S(1)}, u32[]{:S(2)}, u32[]{:S(2)}) collective-permute-start(bf16[4,32,128]{2,1,0:T(8,128)(2,1)S(1)} %get-tuple-element.28), channel_id=1, source_target_pairs={{0,3},{1,0},{2,1},{3,2},{4,7},{5,4},{6,5},{7,6},{8,11},{9,8},{10,9... | collective-permute-start | bytes 98312 | tf_op jit(solution)/shard_map/ppermute | solution.py:307
  24.2 28.9 %collective-permute-start.14 = (bf16[2,8,256,128]{3,2,1,0:T(8,128)(2,1)}, bf16[2,8,256,128]{3,2,1,0:T(8,128)(2,1)}, u32[]{:S(2)}, u32[]{:S(2)}) collective-permute-start(bf16[2,8,256,128]{3,2,1,0:T(8,128)(2,1)} %own.3), channel_id=1, source_target_pairs={{0,16},{16,0},{1,17},{17,1},{2,18},{18,2},{3,19},{19,3},{4,20},{20... | collective-permute-start | bytes 3145736 | tf_op jit(solution)/shard_map/ppermute | solution.py:325
  25.5 4.4 %collective-permute-start.5 = (bf16[4,32,128]{2,1,0:T(8,128)(2,1)S(1)}, bf16[4,32,128]{2,1,0:T(8,128)(2,1)S(1)}, u32[]{:S(2)}, u32[]{:S(2)}) collective-permute-start(bf16[4,32,128]{2,1,0:T(8,128)(2,1)S(1)} %get-tuple-element.22), channel_id=1, source_target_pairs={{0,12},{1,13},{2,14},{3,15},{4,0},{5,1},{6,2},{7,3},{8,4},{9,5},{1... | collective-permute-start | bytes 98312 | tf_op jit(solution)/shard_map/ppermute | solution.py:307
  28.3 4.6 %collective-permute-start.4 = (bf16[4,32,128]{2,1,0:T(8,128)(2,1)S(1)}, bf16[4,32,128]{2,1,0:T(8,128)(2,1)S(1)}, u32[]{:S(2)}, u32[]{:S(2)}) collective-permute-start(bf16[4,32,128]{2,1,0:T(8,128)(2,1)S(1)} %get-tuple-element.23), channel_id=1, source_target_pairs={{0,8},{1,9},{2,10},{3,11},{4,12},{5,13},{6,14},{7,15},{8,0},{9,1},... | collective-permute-start | bytes 98312 | tf_op jit(solution)/shard_map/ppermute | solution.py:307
  28.7 7.1 %copy-start.12 = (s32[16]{0:T(128)}, s32[16]{0:T(128)S(1)}, u32[]{:S(2)}) copy-start(s32[16]{0:T(128)S(1)} %collective-permute-done.13) | copy-start | bytes 196
  28.7 4.6 %collective-permute-start.3 = (bf16[4,32,128]{2,1,0:T(8,128)(2,1)S(1)}, bf16[4,32,128]{2,1,0:T(8,128)(2,1)S(1)}, u32[]{:S(2)}, u32[]{:S(2)}) collective-permute-start(bf16[4,32,128]{2,1,0:T(8,128)(2,1)S(1)} %get-tuple-element.24), channel_id=1, source_target_pairs={{0,4},{1,5},{2,6},{3,7},{4,8},{5,9},{6,10},{7,11},{8,12},{9,13},{1... | collective-permute-start | bytes 98312 | tf_op jit(solution)/shard_map/ppermute | solution.py:307
  33.3 6.0 %copy-start.9 = (s32[2,16]{1,0:T(2,128)S(1)}, s32[2,16]{1,0:T(2,128)}, u32[]{:S(2)}) copy-start(s32[2,16]{1,0:T(2,128)} %rev.3) | copy-start | bytes 388
  33.3 6.0 %copy-start.11 = (s32[1,1,16]{2,1,0:T(1,128)S(1)}, s32[1,1,16]{2,1,0:T(1,128)}, u32[]{:S(2)}) copy-start(s32[1,1,16]{2,1,0:T(1,128)} %param.17) | copy-start | bytes 196
  33.3 6.0 %copy-start.15 = (s32[2]{0:T(128)S(1)}, s32[2]{0:T(128)}, u32[]{:S(2)}) copy-start(s32[2]{0:T(128)} %iota_multiply_fusion) | copy-start | bytes 28
  35.8 17.3 %copy-start.3 = (bf16[2,8,256,128]{3,2,1,0:T(8,128)(2,1)S(1)}, bf16[2,8,256,128]{3,2,1,0:T(8,128)(2,1)}, u32[]{:S(2)}) copy-start(bf16[2,8,256,128]{3,2,1,0:T(8,128)(2,1)} %own.3) | copy-start | bytes 3145732
  36.6 8.1 %collective-permute-start.8 = (bf16[4,32,512]{2,1,0:T(8,128)(2,1)}, bf16[4,32,512]{2,1,0:T(8,128)(2,1)}, u32[]{:S(2)}, u32[]{:S(2)}) collective-permute-start(bf16[4,32,512]{2,1,0:T(8,128)(2,1)} %get-tuple-element.18), channel_id=1, source_target_pairs={{0,2},{1,3},{2,0},{3,1},{4,6},{5,7},{6,4},{7,5},{8,10},{9,11},{10,... | collective-permute-start | bytes 393224 | tf_op jit(solution)/shard_map/ppermute | solution.py:307
  36.6 9.3 %collective-permute-start.7 = (bf16[4,32,512]{2,1,0:T(8,128)(2,1)}, bf16[4,32,512]{2,1,0:T(8,128)(2,1)}, u32[]{:S(2)}, u32[]{:S(2)}) collective-permute-start(bf16[4,32,512]{2,1,0:T(8,128)(2,1)} %get-tuple-element.19), channel_id=1, source_target_pairs={{0,1},{1,2},{2,3},{3,0},{4,5},{5,6},{6,7},{7,4},{8,9},{9,10},{10,1... | collective-permute-start | bytes 393224 | tf_op jit(solution)/shard_map/ppermute | solution.py:307
  36.9 9.0 %collective-permute-start.9 = (bf16[4,32,512]{2,1,0:T(8,128)(2,1)}, bf16[4,32,512]{2,1,0:T(8,128)(2,1)}, u32[]{:S(2)}, u32[]{:S(2)}) collective-permute-start(bf16[4,32,512]{2,1,0:T(8,128)(2,1)} %get-tuple-element.20), channel_id=1, source_target_pairs={{0,3},{1,0},{2,1},{3,2},{4,7},{5,4},{6,5},{7,6},{8,11},{9,8},{10,9... | collective-permute-start | bytes 393224 | tf_op jit(solution)/shard_map/ppermute | solution.py:307
  44.7 5.2 %copy-start.6 = (s32[16,128]{1,0:T(8,128)S(1)}, s32[16,128]{1,0:T(8,128)}, u32[]{:S(2)}) copy-start(s32[16,128]{1,0:T(8,128)} %add.47) | copy-start | bytes 24580
  47.8 7.8 %collective-permute-start.12 = (bf16[4,32,512]{2,1,0:T(8,128)(2,1)}, bf16[4,32,512]{2,1,0:T(8,128)(2,1)}, u32[]{:S(2)}, u32[]{:S(2)}) collective-permute-start(bf16[4,32,512]{2,1,0:T(8,128)(2,1)} %get-tuple-element.14), channel_id=1, source_target_pairs={{0,12},{1,13},{2,14},{3,15},{4,0},{5,1},{6,2},{7,3},{8,4},{9,5},{1... | collective-permute-start | bytes 393224 | tf_op jit(solution)/shard_map/ppermute | solution.py:307
  48.1 7.5 %collective-permute-start.11 = (bf16[4,32,512]{2,1,0:T(8,128)(2,1)}, bf16[4,32,512]{2,1,0:T(8,128)(2,1)}, u32[]{:S(2)}, u32[]{:S(2)}) collective-permute-start(bf16[4,32,512]{2,1,0:T(8,128)(2,1)} %get-tuple-element.15), channel_id=1, source_target_pairs={{0,8},{1,9},{2,10},{3,11},{4,12},{5,13},{6,14},{7,15},{8,0},{9,1},... | collective-permute-start | bytes 393224 | tf_op jit(solution)/shard_map/ppermute | solution.py:307
  49.1 8.4 %collective-permute-start.10 = (bf16[4,32,512]{2,1,0:T(8,128)(2,1)}, bf16[4,32,512]{2,1,0:T(8,128)(2,1)}, u32[]{:S(2)}, u32[]{:S(2)}) collective-permute-start(bf16[4,32,512]{2,1,0:T(8,128)(2,1)} %get-tuple-element.16), channel_id=1, source_target_pairs={{0,4},{1,5},{2,6},{3,7},{4,8},{5,9},{6,10},{7,11},{8,12},{9,13},{1... | collective-permute-start | bytes 393224 | tf_op jit(solution)/shard_map/ppermute | solution.py:307
  53.1 4.4 %copy-start.4 = (bf16[1,4,32,512]{3,2,1,0:T(8,128)(2,1)S(1)}, bf16[1,4,32,512]{3,2,1,0:T(8,128)(2,1)}, u32[]{:S(2)}) copy-start(bf16[1,4,32,512]{3,2,1,0:T(8,128)(2,1)} %get-tuple-element.13) | copy-start | bytes 393220
  53.1 5.5 %copy-start.7 = (bf16[4,576]{1,0:T(4,128)(2,1)S(1)}, bf16[4,576]{1,0:T(4,128)(2,1)}, u32[]{:S(2)}) copy-start(bf16[4,576]{1,0:T(4,128)(2,1)} %dynamic-slice_bitcast_fusion) | copy-start | bytes 13828
  53.1 5.5 %copy-start.8 = (bf16[16,128]{1,0:T(8,128)(2,1)S(1)}, bf16[16,128]{1,0:T(8,128)(2,1)}, u32[]{:S(2)}) copy-start(bf16[16,128]{1,0:T(8,128)(2,1)} %gather_fusion) | copy-start | bytes 12292
  65.2 20.1 %copy-start.2 = (bf16[5,512,256]{2,1,0:T(8,128)(2,1)S(1)}, bf16[5,512,256]{2,1,0:T(8,128)(2,1)}, u32[]{:S(2)}) copy-start(bf16[5,512,256]{2,1,0:T(8,128)(2,1)} %copy-done.1) | copy-start | bytes 3932164
  86.0 3.3 %collective-permute-start.15 = (bf16[16,4,8,128]{3,2,1,0:T(8,128)(2,1)S(1)}, bf16[16,4,8,128]{3,2,1,0:T(8,128)(2,1)S(1)}, u32[]{:S(2)}, u32[]{:S(2)}) collective-permute-start(bf16[16,4,8,128]{3,2,1,0:T(8,128)(2,1)S(1)} %bitcast.73), channel_id=1, source_target_pairs={{0,16},{16,0},{1,17},{17,1},{2,18},{18,2},{3,19},{19,3},{4,20},{20... | collective-permute-start | bytes 393224 | tf_op jit(solution)/shard_map/ppermute | solution.py:325
  (1 other events, 1.1 us)

commit v6 on v5

--- a/solution.py
+++ b/solution.py
@@ -24,8 +24,8 @@
 ROWS = PEERS * BLOCK
 TILE = 512
 CHUNK = 2
-COLUMN = (12, 15, 2, 1, 8, 0, 13, 6, 9, 3, 7, 4, 11, 10, 14, 5)
-PLANE = (2, 11, 3, 10, 0, 4, 7, 5, 14, 12, 6, 9, 13, 8, 1, 15)
+COLUMN = (12, 15, 2, 1, 13, 0, 8, 6, 9, 7, 3, 4, 11, 10, 14, 5)
+PLANE = (2, 13, 11, 3, 12, 0, 4, 7, 5, 14, 10, 6, 9, 8, 1, 15)
 HALF = KV_RANK // 2
 DEAD = -1e30
 SCALE = 1.0 / math.sqrt(NOPE + ROPE)

time: 91 us -> 90.6 us (level)
  no operation moved by 1% of the time
where the time goes in v6:
time: 90.6 us; the launch traced here: 90.1 us
  starting transfers between devices  29.2 us (32%)
  blocking collectives  15.1 us (17%)
  waiting for transfers between devices  14.5 us (16%)
  Pallas kernels  12.7 us (14%)
  local copies, waits for them, and re-layouts  10.8 us (12%)
  other arithmetic  6.91 us (8%)
  between operations  0.92 us (1%)
    all_to_all x1, blocking collectives, ordered_all_to_all(): lax.all_to_all(value, axis, split_axis=0, concat_axis=0, tiled=True, axis...  15.1 us
    ppermute x12, starting transfers between devices, shifted(): return lax.ppermute(value, 'req', pairs)  14.1 us
    all_to_all x1, starting transfers between devices, ordered_all_to_all(): lax.all_to_all(value, axis, split_axis=0, concat_axis=0, tiled=True, axis...  11.1 us
    all_to_all x1, waiting for transfers between devices, ordered_all_to_all(): lax.all_to_all(value, axis, split_axis=0, concat_axis=0, tiled=True, axis...  7.2 us
    ppermute x12, waiting for transfers between devices, shifted(): return lax.ppermute(value, 'req', pairs)  6.27 us
    pallas_call x1, Pallas kernels, attend(): pl.pallas_call(attend_kernel, out_shape=jax.ShapeDtypeStruct((PEERS, BLOC...  4.48 us
    ppermute x4, starting transfers between devices, swapped(): return lax.ppermute(value, 'seq', [(0, 1), (1, 0)])  4.01 us
    add x4, local copies, waits for them, and re-layouts, shards(): live = starts[:, :, None] + jnp.arange(PAGE, dtype=jnp.int32) < lengths[0]  3.4 us
  transfers between devices with their start and end apart: 17, of which 6 were waited for; matrix products, arithmetic and copies ran while one was open for 18% of the time, Pallas kernels for 5%

profile of v6, /device:TPU:1, one launch (start us, length us, event | category | flops | bytes accessed | tf_op | source)
XLA Modules:
  0.0 90.1 jit_solution(16456643975148128823)
XLA Ops:
  0.0 2.9 %shard_map.121 = bf16[16,144,512]{2,1,0:T(8,128)(2,1)} custom-call(s32[16]{0:T(128)} %bitcast.90, s32[16]{0:T(128)} %constant.40.clone.order, bf16[2,16,64,576]{3,2,1,0:T(8,128)(2,1)} %bitcast.76), custom_call_target="tpu_custom_call" | custom-call | bytes 5242880 | tf_op jit(solution)/shard_map/pallas_call | solution.py:83
  2.9 11.1 %all-to-all-start = ((bf16[16,144,512]{2,1,0:T(8,128)(2,1)}), bf16[16,144,512]{2,1,0:T(8,128)(2,1)S(1)}, u32[]{:S(2)}, u32[]{:S(2)}) async-start(bf16[16,144,512]{2,1,0:T(8,128)(2,1)} %shard_map.121), calls=%async_computation | async-start | bytes 4718592 | tf_op jit(solution)/shard_map/all_to_all | solution.py:319
  15.7 2.8 %collective-permute-start.1 = (bf16[4,32,128]{2,1,0:T(8,128)(2,1)S(1)}, bf16[4,32,128]{2,1,0:T(8,128)(2,1)S(1)}, u32[]{:S(2)}, u32[]{:S(2)}) collective-permute-start(bf16[4,32,128]{2,1,0:T(8,128)(2,1)S(1)} %get-tuple-element.26), channel_id=1, source_target_pairs={{0,2},{1,3},{2,0},{3,1},{4,6},{5,7},{6,4},{7,5},{8,10},{9,11},{10,... | collective-permute-start | bytes 98312 | tf_op jit(solution)/shard_map/ppermute | solution.py:307
  18.8 2.4 %collective-permute-start.2 = (bf16[4,32,128]{2,1,0:T(8,128)(2,1)S(1)}, bf16[4,32,128]{2,1,0:T(8,128)(2,1)S(1)}, u32[]{:S(2)}, u32[]{:S(2)}) collective-permute-start(bf16[4,32,128]{2,1,0:T(8,128)(2,1)S(1)} %get-tuple-element.28), channel_id=1, source_target_pairs={{0,3},{1,0},{2,1},{3,2},{4,7},{5,4},{6,5},{7,6},{8,11},{9,8},{10,9... | collective-permute-start | bytes 98312 | tf_op jit(solution)/shard_map/ppermute | solution.py:307
  24.2 1.3 %collective-permute-start.14 = (bf16[2,8,256,128]{3,2,1,0:T(8,128)(2,1)}, bf16[2,8,256,128]{3,2,1,0:T(8,128)(2,1)}, u32[]{:S(2)}, u32[]{:S(2)}) collective-permute-start(bf16[2,8,256,128]{3,2,1,0:T(8,128)(2,1)} %own.3), channel_id=1, source_target_pairs={{0,16},{16,0},{1,17},{17,1},{2,18},{18,2},{3,19},{19,3},{4,20},{20... | collective-permute-start | bytes 3145736 | tf_op jit(solution)/shard_map/ppermute | solution.py:325
  25.5 2.8 %collective-permute-start.5 = (bf16[4,32,128]{2,1,0:T(8,128)(2,1)S(1)}, bf16[4,32,128]{2,1,0:T(8,128)(2,1)S(1)}, u32[]{:S(2)}, u32[]{:S(2)}) collective-permute-start(bf16[4,32,128]{2,1,0:T(8,128)(2,1)S(1)} %get-tuple-element.22), channel_id=1, source_target_pairs={{0,12},{1,13},{2,14},{3,15},{4,0},{5,1},{6,2},{7,3},{8,4},{9,5},{1... | collective-permute-start | bytes 98312 | tf_op jit(solution)/shard_map/ppermute | solution.py:307
  29.9 3.0 %collective-permute-done.4 = bf16[4,32,128]{2,1,0:T(8,128)(2,1)S(1)} collective-permute-done((bf16[4,32,128]{2,1,0:T(8,128)(2,1)S(1)}, bf16[4,32,128]{2,1,0:T(8,128)(2,1)S(1)}, u32[]{:S(2)}, u32[]{:S(2)}) %collective-permute-start.4) | collective-permute-done | bytes 32800 | tf_op jit(solution)/shard_map/ppermute | solution.py:307
  33.3 2.5 %shard_map.119 = bf16[512,512]{1,0:T(8,128)(2,1)S(1)} custom-call(s32[19]{0:T(128)S(1)} %pad_add_fusion.1.where, bf16[512,128]{1,0:T(8,128)(2,1)S(1)} %bitcast.71, bf16[2,8,128,256]{3,2,1,0:T(8,128)(2,1)} %own.2, bf16[2,8,128,256]{3,2,1,0:T(8,128)(2,1)} %collective-permute-done.6.got), custom_call_target="tpu_custom_call" | custom-call | flops 536870912 | bytes 2097152 | tf_op jit(solution)/shard_map/pallas_call | solution.py:210
  35.8 0.8 fusion.7
  36.9 2.4 %collective-permute-start.9 = (bf16[4,32,512]{2,1,0:T(8,128)(2,1)}, bf16[4,32,512]{2,1,0:T(8,128)(2,1)}, u32[]{:S(2)}, u32[]{:S(2)}) collective-permute-start(bf16[4,32,512]{2,1,0:T(8,128)(2,1)} %get-tuple-element.20), channel_id=1, source_target_pairs={{0,3},{1,0},{2,1},{3,2},{4,7},{5,4},{6,5},{7,6},{8,11},{9,8},{10,9... | collective-permute-start | bytes 393224 | tf_op jit(solution)/shard_map/ppermute | solution.py:307
  39.3 1.3 %add_bitcast_fusion = s32[16,2]{0,1:T(2,128)} fusion(s32[2,16]{1,0:T(2,128)S(1)} %copy-done.9, pred[]{:T(512)S(6)} %eq.4, s32[2]{0:T(128)S(1)} %copy-done.15, s32[1,16]{1,0:T(1,128)} %bitcast.89, s32[1,16]{1,0:T(1,128)S(1)} %bitcast.87), kind=kLoop, calls=%fused_computation.31 | loop fusion | flops 128 | bytes 393 | tf_op jit(solution)/shard_map/add | solution.py:346
  40.6 1.3 %copy.20 = s32[16,2]{1,0:T(8,128)} copy(s32[16,2]{0,1:T(2,128)} %add_bitcast_fusion) | data formatting | bytes 256 | tf_op jit(solution)/shard_map/add | solution.py:346
  41.9 1.4 %add.46 = s32[16,2,64]{2,1,0:T(2,128)} broadcast(s32[16,2]{1,0:T(8,128)} %copy.20), dimensions={0,1} | broadcast | bytes 8320 | tf_op jit(solution)/shard_map/add | solution.py:347
  43.3 1.4 %add.47 = s32[16,128]{1,0:T(8,128)} reshape(s32[16,2,64]{2,1,0:T(2,128)} %add.46) | data formatting | bytes 16384 | tf_op jit(solution)/shard_map/add | solution.py:347
  44.7 1.1 %collective-permute-done.7 = bf16[4,32,512]{2,1,0:T(8,128)(2,1)} collective-permute-done((bf16[4,32,512]{2,1,0:T(8,128)(2,1)}, bf16[4,32,512]{2,1,0:T(8,128)(2,1)}, u32[]{:S(2)}, u32[]{:S(2)}) %collective-permute-start.7) | collective-permute-done | bytes 131104 | tf_op jit(solution)/shard_map/ppermute | solution.py:307
  45.9 1.2 %pad_maximum_fusion = bf16[4,4,32,512]{3,2,1,0:T(8,128)(2,1)S(1)} fusion(bf16[4,1,32,512]{3,2,1,0:T(8,128)(2,1)} %bitcast.23, bf16[4,1,32,512]{3,2,1,0:T(8,128)(2,1)} %bitcast.21, bf16[4,1,32,512]{3,2,1,0:T(8,128)(2,1)} %bitcast.19, bf16[4,1,32,512]{3,2,1,0:T(8,128)(2,1)} %get-tuple-element.17), kind=kLoop, calls=%fused_computation.9 | loop fusion | flops 786432 | bytes 1048576 | tf_op jit(solution)/shard_map/stack | solution.py:313
  47.0 0.8 fusion.6
  48.1 0.9 %collective-permute-start.11 = (bf16[4,32,512]{2,1,0:T(8,128)(2,1)}, bf16[4,32,512]{2,1,0:T(8,128)(2,1)}, u32[]{:S(2)}, u32[]{:S(2)}) collective-permute-start(bf16[4,32,512]{2,1,0:T(8,128)(2,1)} %get-tuple-element.15), channel_id=1, source_target_pairs={{0,8},{1,9},{2,10},{3,11},{4,12},{5,13},{6,14},{7,15},{8,0},{9,1},... | collective-permute-start | bytes 393224 | tf_op jit(solution)/shard_map/ppermute | solution.py:307
  49.1 0.9 collective-permute-start.10
  49.9 1.2 %fusion.5 = bf16[16,128]{1,0:T(8,128)(2,1)} fusion(s32[16,128]{1,0:T(8,128)S(1)} %copy-done.6, s32[]{:T(128)} %bitcast.69, s32[128]{0:T(128)} %add.49), kind=kLoop, calls=%fused_computation.27 | loop fusion | flops 6144 | bytes 12804 | tf_op jit(solution)/shard_map/convert_element_type | solution.py:353
  51.2 2.0 %gather_fusion = bf16[16,128]{1,0:T(8,128)(2,1)} fusion(bf16[16,128]{1,0:T(8,128)(2,1)} %fusion.5, s32[1024]{0:T(1024)} %pad_clamp_fusion), kind=kCustom, calls=%fused_computation | custom fusion | bytes 8256 | tf_op jit(solution)/shard_map/gather | solution.py:353
  53.1 1.5 %shard_map.120.weight = bf16[5,512,256]{2,1,0:T(8,128)(2,1)S(1)} custom-call(s32[19]{0:T(128)S(1)} %pad_add_fusion.1.where, bf16[2,8,256,128]{3,2,1,0:T(8,128)(2,1)S(1)} %copy-done.3, bf16[2,8,256,128]{3,2,1,0:T(8,128)(2,1)} %collective-permute-done.14.got), custom_call_target="tpu_custom_call" | custom-call | bytes 3145728 | tf_op jit(solution)/shard_map/pallas_call | solution.py:171
  54.6 1.1 %copy-done.1 = bf16[5,512,256]{2,1,0:T(8,128)(2,1)} copy-done((bf16[5,512,256]{2,1,0:T(8,128)(2,1)}, bf16[5,512,256]{2,1,0:T(8,128)(2,1)S(1)}, u32[]{:S(2)}) %copy-start.1) | copy-done | bytes 1310744
  55.7 1.8 %collective-permute-done.10 = bf16[4,32,512]{2,1,0:T(8,128)(2,1)} collective-permute-done((bf16[4,32,512]{2,1,0:T(8,128)(2,1)}, bf16[4,32,512]{2,1,0:T(8,128)(2,1)}, u32[]{:S(2)}, u32[]{:S(2)}) %collective-permute-start.10) | collective-permute-done | bytes 131104 | tf_op jit(solution)/shard_map/ppermute | solution.py:307
  57.5 1.1 %pad_maximum_fusion.1 = bf16[4,4,32,512]{3,2,1,0:T(8,128)(2,1)S(1)} fusion(bf16[1,4,32,512]{3,2,1,0:T(8,128)(2,1)} %bitcast.29, bf16[1,4,32,512]{3,2,1,0:T(8,128)(2,1)} %bitcast.27, bf16[1,4,32,512]{3,2,1,0:T(8,128)(2,1)} %bitcast.25, bf16[1,4,32,512]{3,2,1,0:T(8,128)(2,1)S(1)} %copy-done.4), kind=kLoop, calls=%fused_computation.10 | loop fusion | flops 786432 | bytes 1048576 | tf_op jit(solution)/shard_map/stack | solution.py:314
  58.8 7.2 %all-to-all-done.pages = bf16[16,144,512]{2,1,0:T(8,128)(2,1)S(1)} async-done(((bf16[16,144,512]{2,1,0:T(8,128)(2,1)}), bf16[16,144,512]{2,1,0:T(8,128)(2,1)S(1)}, u32[]{:S(2)}, u32[]{:S(2)}) %all-to-all-start) | async-done | bytes 2359328 | tf_op jit(solution)/shard_map/all_to_all | solution.py:319
  66.0 4.5 %shard_map.122 = bf16[16,32,512]{2,1,0:T(8,128)(2,1)S(1)} custom-call(s32[19]{0:T(128)S(1)} %pad_add_fusion.1.where, bf16[544,640]{1,0:T(8,128)(2,1)S(1)} %fusion.4.inputs, bf16[16,144,512]{2,1,0:T(8,128)(2,1)S(1)} %all-to-all-done.pages), custom_call_target="tpu_custom_call" | custom-call | flops 2281701376 | bytes 4194304 | tf_op jit(solution)/shard_map/pallas_call | solution.py:285
  70.5 15.1 %all_to_all.10 = bf16[16,32,512]{2,1,0:T(8,128)(2,1)S(1)} all-to-all(bf16[16,32,512]{2,1,0:T(8,128)(2,1)S(1)} %shard_map.122), channel_id=1, replica_groups={{2,13,11,3,12,0,4,7,5,14,10,6,9,8,1,15},{18,29,27,19,28,16,20,23,21,30,..., dimensions={0} | all-to-all | bytes 1048576 | tf_op jit(solution)/shard_map/all_to_all | solution.py:319
  85.6 0.7 shard_map.123
  86.3 2.1 %collective-permute-start.15 = (bf16[16,4,8,128]{3,2,1,0:T(8,128)(2,1)S(1)}, bf16[16,4,8,128]{3,2,1,0:T(8,128)(2,1)S(1)}, u32[]{:S(2)}, u32[]{:S(2)}) collective-permute-start(bf16[16,4,8,128]{3,2,1,0:T(8,128)(2,1)S(1)} %bitcast.73), channel_id=1, source_target_pairs={{0,16},{16,0},{1,17},{17,1},{2,18},{18,2},{3,19},{19,3},{4,20},{20... | collective-permute-start | bytes 393224 | tf_op jit(solution)/shard_map/ppermute | solution.py:325
  88.4 1.0 %collective-permute-done.15 = bf16[16,4,8,128]{3,2,1,0:T(8,128)(2,1)S(1)} collective-permute-done((bf16[16,4,8,128]{3,2,1,0:T(8,128)(2,1)S(1)}, bf16[16,4,8,128]{3,2,1,0:T(8,128)(2,1)S(1)}, u32[]{:S(2)}, u32[]{:S(2)}) %collective-permute-start.15) | collective-permute-done | bytes 131104 | tf_op jit(solution)/shard_map/ppermute | solution.py:325
  89.4 0.7 maximum_select_fusion
  (67 shorter events, 7.1 us)
Async XLA Ops:
  0.0 21.8 %copy-start = (bf16[2,1,4,576]{3,2,1,0:T(4,128)(2,1)S(1)}, bf16[2,1,4,576]{3,2,1,0:T(4,128)(2,1)}, u32[]{:S(2)}) copy-start(bf16[2,1,4,576]{3,2,1,0:T(4,128)(2,1)} %param.19) | copy-start | bytes 27652
  2.9 11.2 %copy-start.10 = (s32[1,1,16]{2,1,0:T(1,128)S(1)}, s32[1,1,16]{2,1,0:T(1,128)}, u32[]{:S(2)}) copy-start(s32[1,1,16]{2,1,0:T(1,128)} %param.17) | copy-start | bytes 196
  2.9 11.8 %copy-start.5 = (bf16[2,1,4,128,192]{3,4,2,1,0:T(8,128)(2,1)S(1)}, bf16[2,1,4,128,192]{3,4,2,1,0:T(8,128)(2,1)}, u32[]{:S(2)}) copy-start(bf16[2,1,4,128,192]{3,4,2,1,0:T(8,128)(2,1)} %param.12) | copy-start | bytes 1179652
  2.9 12.0 %copy-start.14 = (s32[16]{0:T(128)S(1)}, s32[16]{0:T(128)}, u32[]{:S(2)}) copy-start(s32[16]{0:T(128)} %constant.39.clone) | copy-start | bytes 196
  2.9 63.0 %all-to-all-start = ((bf16[16,144,512]{2,1,0:T(8,128)(2,1)}), bf16[16,144,512]{2,1,0:T(8,128)(2,1)S(1)}, u32[]{:S(2)}, u32[]{:S(2)}) async-start(bf16[16,144,512]{2,1,0:T(8,128)(2,1)} %shard_map.121), calls=%async_computation | async-start | bytes 4718592 | tf_op jit(solution)/shard_map/all_to_all | solution.py:319
  14.1 7.1 %copy-start.13 = (s32[16]{0:T(128)S(1)}, s32[16]{0:T(128)}, u32[]{:S(2)}) copy-start(s32[16]{0:T(128)} %constant.56) | copy-start | bytes 196
  14.1 14.6 %collective-permute-start.13 = (s32[16]{0:T(128)S(1)}, s32[16]{0:T(128)S(1)}, u32[]{:S(2)}, u32[]{:S(2)}) collective-permute-start(s32[16]{0:T(128)S(1)} %bitcast.85), channel_id=1, source_target_pairs={{0,16},{16,0},{1,17},{17,1},{2,18},{18,2},{3,19},{19,3},{4,20},{20... | collective-permute-start | bytes 200 | tf_op jit(solution)/shard_map/ppermute | solution.py:325
  14.6 18.7 %collective-permute-start.6 = (bf16[2,8,128,256]{3,2,1,0:T(8,128)(2,1)}, bf16[2,8,128,256]{3,2,1,0:T(8,128)(2,1)}, u32[]{:S(2)}, u32[]{:S(2)}) collective-permute-start(bf16[2,8,128,256]{3,2,1,0:T(8,128)(2,1)} %own.2), channel_id=1, source_target_pairs={{0,16},{16,0},{1,17},{17,1},{2,18},{18,2},{3,19},{19,3},{4,20},{20... | collective-permute-start | bytes 3145736 | tf_op jit(solution)/shard_map/ppermute | solution.py:325
  15.7 8.5 %collective-permute-start.1 = (bf16[4,32,128]{2,1,0:T(8,128)(2,1)S(1)}, bf16[4,32,128]{2,1,0:T(8,128)(2,1)S(1)}, u32[]{:S(2)}, u32[]{:S(2)}) collective-permute-start(bf16[4,32,128]{2,1,0:T(8,128)(2,1)S(1)} %get-tuple-element.26), channel_id=1, source_target_pairs={{0,2},{1,3},{2,0},{3,1},{4,6},{5,7},{6,4},{7,5},{8,10},{9,11},{10,... | collective-permute-start | bytes 98312 | tf_op jit(solution)/shard_map/ppermute | solution.py:307
  18.5 7.0 %collective-permute-start = (bf16[4,32,128]{2,1,0:T(8,128)(2,1)S(1)}, bf16[4,32,128]{2,1,0:T(8,128)(2,1)S(1)}, u32[]{:S(2)}, u32[]{:S(2)}) collective-permute-start(bf16[4,32,128]{2,1,0:T(8,128)(2,1)S(1)} %get-tuple-element.27), channel_id=1, source_target_pairs={{0,1},{1,2},{2,3},{3,0},{4,5},{5,6},{6,7},{7,4},{8,9},{9,10},{10,1... | collective-permute-start | bytes 98312 | tf_op jit(solution)/shard_map/ppermute | solution.py:307
  18.8 6.7 %collective-permute-start.2 = (bf16[4,32,128]{2,1,0:T(8,128)(2,1)S(1)}, bf16[4,32,128]{2,1,0:T(8,128)(2,1)S(1)}, u32[]{:S(2)}, u32[]{:S(2)}) collective-permute-start(bf16[4,32,128]{2,1,0:T(8,128)(2,1)S(1)} %get-tuple-element.28), channel_id=1, source_target_pairs={{0,3},{1,0},{2,1},{3,2},{4,7},{5,4},{6,5},{7,6},{8,11},{9,8},{10,9... | collective-permute-start | bytes 98312 | tf_op jit(solution)/shard_map/ppermute | solution.py:307
  24.2 28.9 %collective-permute-start.14 = (bf16[2,8,256,128]{3,2,1,0:T(8,128)(2,1)}, bf16[2,8,256,128]{3,2,1,0:T(8,128)(2,1)}, u32[]{:S(2)}, u32[]{:S(2)}) collective-permute-start(bf16[2,8,256,128]{3,2,1,0:T(8,128)(2,1)} %own.3), channel_id=1, source_target_pairs={{0,16},{16,0},{1,17},{17,1},{2,18},{18,2},{3,19},{19,3},{4,20},{20... | collective-permute-start | bytes 3145736 | tf_op jit(solution)/shard_map/ppermute | solution.py:325
  25.5 4.4 %collective-permute-start.5 = (bf16[4,32,128]{2,1,0:T(8,128)(2,1)S(1)}, bf16[4,32,128]{2,1,0:T(8,128)(2,1)S(1)}, u32[]{:S(2)}, u32[]{:S(2)}) collective-permute-start(bf16[4,32,128]{2,1,0:T(8,128)(2,1)S(1)} %get-tuple-element.22), channel_id=1, source_target_pairs={{0,12},{1,13},{2,14},{3,15},{4,0},{5,1},{6,2},{7,3},{8,4},{9,5},{1... | collective-permute-start | bytes 98312 | tf_op jit(solution)/shard_map/ppermute | solution.py:307
  28.3 4.6 %collective-permute-start.4 = (bf16[4,32,128]{2,1,0:T(8,128)(2,1)S(1)}, bf16[4,32,128]{2,1,0:T(8,128)(2,1)S(1)}, u32[]{:S(2)}, u32[]{:S(2)}) collective-permute-start(bf16[4,32,128]{2,1,0:T(8,128)(2,1)S(1)} %get-tuple-element.23), channel_id=1, source_target_pairs={{0,8},{1,9},{2,10},{3,11},{4,12},{5,13},{6,14},{7,15},{8,0},{9,1},... | collective-permute-start | bytes 98312 | tf_op jit(solution)/shard_map/ppermute | solution.py:307
  28.7 7.1 %copy-start.12 = (s32[16]{0:T(128)}, s32[16]{0:T(128)S(1)}, u32[]{:S(2)}) copy-start(s32[16]{0:T(128)S(1)} %collective-permute-done.13) | copy-start | bytes 196
  28.7 4.5 %collective-permute-start.3 = (bf16[4,32,128]{2,1,0:T(8,128)(2,1)S(1)}, bf16[4,32,128]{2,1,0:T(8,128)(2,1)S(1)}, u32[]{:S(2)}, u32[]{:S(2)}) collective-permute-start(bf16[4,32,128]{2,1,0:T(8,128)(2,1)S(1)} %get-tuple-element.24), channel_id=1, source_target_pairs={{0,4},{1,5},{2,6},{3,7},{4,8},{5,9},{6,10},{7,11},{8,12},{9,13},{1... | collective-permute-start | bytes 98312 | tf_op jit(solution)/shard_map/ppermute | solution.py:307
  33.3 6.0 %copy-start.9 = (s32[2,16]{1,0:T(2,128)S(1)}, s32[2,16]{1,0:T(2,128)}, u32[]{:S(2)}) copy-start(s32[2,16]{1,0:T(2,128)} %rev.3) | copy-start | bytes 388
  33.3 6.0 %copy-start.11 = (s32[1,1,16]{2,1,0:T(1,128)S(1)}, s32[1,1,16]{2,1,0:T(1,128)}, u32[]{:S(2)}) copy-start(s32[1,1,16]{2,1,0:T(1,128)} %param.17) | copy-start | bytes 196
  33.3 6.0 %copy-start.15 = (s32[2]{0:T(128)S(1)}, s32[2]{0:T(128)}, u32[]{:S(2)}) copy-start(s32[2]{0:T(128)} %iota_multiply_fusion) | copy-start | bytes 28
  35.8 17.3 %copy-start.3 = (bf16[2,8,256,128]{3,2,1,0:T(8,128)(2,1)S(1)}, bf16[2,8,256,128]{3,2,1,0:T(8,128)(2,1)}, u32[]{:S(2)}) copy-start(bf16[2,8,256,128]{3,2,1,0:T(8,128)(2,1)} %own.3) | copy-start | bytes 3145732
  36.6 8.1 %collective-permute-start.8 = (bf16[4,32,512]{2,1,0:T(8,128)(2,1)}, bf16[4,32,512]{2,1,0:T(8,128)(2,1)}, u32[]{:S(2)}, u32[]{:S(2)}) collective-permute-start(bf16[4,32,512]{2,1,0:T(8,128)(2,1)} %get-tuple-element.18), channel_id=1, source_target_pairs={{0,2},{1,3},{2,0},{3,1},{4,6},{5,7},{6,4},{7,5},{8,10},{9,11},{10,... | collective-permute-start | bytes 393224 | tf_op jit(solution)/shard_map/ppermute | solution.py:307
  36.6 9.3 %collective-permute-start.7 = (bf16[4,32,512]{2,1,0:T(8,128)(2,1)}, bf16[4,32,512]{2,1,0:T(8,128)(2,1)}, u32[]{:S(2)}, u32[]{:S(2)}) collective-permute-start(bf16[4,32,512]{2,1,0:T(8,128)(2,1)} %get-tuple-element.19), channel_id=1, source_target_pairs={{0,1},{1,2},{2,3},{3,0},{4,5},{5,6},{6,7},{7,4},{8,9},{9,10},{10,1... | collective-permute-start | bytes 393224 | tf_op jit(solution)/shard_map/ppermute | solution.py:307
  36.9 9.0 %collective-permute-start.9 = (bf16[4,32,512]{2,1,0:T(8,128)(2,1)}, bf16[4,32,512]{2,1,0:T(8,128)(2,1)}, u32[]{:S(2)}, u32[]{:S(2)}) collective-permute-start(bf16[4,32,512]{2,1,0:T(8,128)(2,1)} %get-tuple-element.20), channel_id=1, source_target_pairs={{0,3},{1,0},{2,1},{3,2},{4,7},{5,4},{6,5},{7,6},{8,11},{9,8},{10,9... | collective-permute-start | bytes 393224 | tf_op jit(solution)/shard_map/ppermute | solution.py:307
  44.7 5.2 %copy-start.6 = (s32[16,128]{1,0:T(8,128)S(1)}, s32[16,128]{1,0:T(8,128)}, u32[]{:S(2)}) copy-start(s32[16,128]{1,0:T(8,128)} %add.47) | copy-start | bytes 24580
  47.8 7.8 %collective-permute-start.12 = (bf16[4,32,512]{2,1,0:T(8,128)(2,1)}, bf16[4,32,512]{2,1,0:T(8,128)(2,1)}, u32[]{:S(2)}, u32[]{:S(2)}) collective-permute-start(bf16[4,32,512]{2,1,0:T(8,128)(2,1)} %get-tuple-element.14), channel_id=1, source_target_pairs={{0,12},{1,13},{2,14},{3,15},{4,0},{5,1},{6,2},{7,3},{8,4},{9,5},{1... | collective-permute-start | bytes 393224 | tf_op jit(solution)/shard_map/ppermute | solution.py:307
  48.1 7.5 %collective-permute-start.11 = (bf16[4,32,512]{2,1,0:T(8,128)(2,1)}, bf16[4,32,512]{2,1,0:T(8,128)(2,1)}, u32[]{:S(2)}, u32[]{:S(2)}) collective-permute-start(bf16[4,32,512]{2,1,0:T(8,128)(2,1)} %get-tuple-element.15), channel_id=1, source_target_pairs={{0,8},{1,9},{2,10},{3,11},{4,12},{5,13},{6,14},{7,15},{8,0},{9,1},... | collective-permute-start | bytes 393224 | tf_op jit(solution)/shard_map/ppermute | solution.py:307
  49.1 8.4 %collective-permute-start.10 = (bf16[4,32,512]{2,1,0:T(8,128)(2,1)}, bf16[4,32,512]{2,1,0:T(8,128)(2,1)}, u32[]{:S(2)}, u32[]{:S(2)}) collective-permute-start(bf16[4,32,512]{2,1,0:T(8,128)(2,1)} %get-tuple-element.16), channel_id=1, source_target_pairs={{0,4},{1,5},{2,6},{3,7},{4,8},{5,9},{6,10},{7,11},{8,12},{9,13},{1... | collective-permute-start | bytes 393224 | tf_op jit(solution)/shard_map/ppermute | solution.py:307
  53.1 4.4 %copy-start.4 = (bf16[1,4,32,512]{3,2,1,0:T(8,128)(2,1)S(1)}, bf16[1,4,32,512]{3,2,1,0:T(8,128)(2,1)}, u32[]{:S(2)}) copy-start(bf16[1,4,32,512]{3,2,1,0:T(8,128)(2,1)} %get-tuple-element.13) | copy-start | bytes 393220
  53.1 5.5 %copy-start.7 = (bf16[4,576]{1,0:T(4,128)(2,1)S(1)}, bf16[4,576]{1,0:T(4,128)(2,1)}, u32[]{:S(2)}) copy-start(bf16[4,576]{1,0:T(4,128)(2,1)} %dynamic-slice_bitcast_fusion) | copy-start | bytes 13828
  53.1 5.5 %copy-start.8 = (bf16[16,128]{1,0:T(8,128)(2,1)S(1)}, bf16[16,128]{1,0:T(8,128)(2,1)}, u32[]{:S(2)}) copy-start(bf16[16,128]{1,0:T(8,128)(2,1)} %gather_fusion) | copy-start | bytes 12292
  66.0 19.6 %copy-start.2 = (bf16[5,512,256]{2,1,0:T(8,128)(2,1)S(1)}, bf16[5,512,256]{2,1,0:T(8,128)(2,1)}, u32[]{:S(2)}) copy-start(bf16[5,512,256]{2,1,0:T(8,128)(2,1)} %copy-done.1) | copy-start | bytes 3932164
  86.3 3.1 %collective-permute-start.15 = (bf16[16,4,8,128]{3,2,1,0:T(8,128)(2,1)S(1)}, bf16[16,4,8,128]{3,2,1,0:T(8,128)(2,1)S(1)}, u32[]{:S(2)}, u32[]{:S(2)}) collective-permute-start(bf16[16,4,8,128]{3,2,1,0:T(8,128)(2,1)S(1)} %bitcast.73), channel_id=1, source_target_pairs={{0,16},{16,0},{1,17},{17,1},{2,18},{18,2},{3,19},{19,3},{4,20},{20... | collective-permute-start | bytes 393224 | tf_op jit(solution)/shard_map/ppermute | solution.py:325
  (1 other events, 1.1 us)

commit v7 on v6

--- a/solution.py
+++ b/solution.py
@@ -23,7 +23,7 @@
 BLOCK = HEADS_PER * STEPS
 ROWS = PEERS * BLOCK
 TILE = 512
-CHUNK = 2
+CHUNK = 1
 COLUMN = (12, 15, 2, 1, 13, 0, 8, 6, 9, 7, 3, 4, 11, 10, 14, 5)
 PLANE = (2, 13, 11, 3, 12, 0, 4, 7, 5, 14, 10, 6, 9, 8, 1, 15)
 HALF = KV_RANK // 2

time: 90.6 us -> 91 us (level)
  no operation moved by 1% of the time
where the time goes in v7:
time: 91 us; the launch traced here: 90.6 us
  starting transfers between devices  29.2 us (32%)
  blocking collectives  15.1 us (17%)
  waiting for transfers between devices  14.5 us (16%)
  Pallas kernels  13.1 us (14%)
  local copies, waits for them, and re-layouts  10.8 us (12%)
  other arithmetic  6.91 us (8%)
  between operations  0.92 us (1%)
    all_to_all x1, blocking collectives, ordered_all_to_all(): lax.all_to_all(value, axis, split_axis=0, concat_axis=0, tiled=True, axis...  15.1 us
    ppermute x12, starting transfers between devices, shifted(): return lax.ppermute(value, 'req', pairs)  14.1 us
    all_to_all x1, starting transfers between devices, ordered_all_to_all(): lax.all_to_all(value, axis, split_axis=0, concat_axis=0, tiled=True, axis...  11.1 us
    all_to_all x1, waiting for transfers between devices, ordered_all_to_all(): lax.all_to_all(value, axis, split_axis=0, concat_axis=0, tiled=True, axis...  7.21 us
    ppermute x12, waiting for transfers between devices, shifted(): return lax.ppermute(value, 'req', pairs)  6.28 us
    pallas_call x1, Pallas kernels, attend(): pl.pallas_call(attend_kernel, out_shape=jax.ShapeDtypeStruct((PEERS, BLOC...  4.48 us
    ppermute x4, starting transfers between devices, swapped(): return lax.ppermute(value, 'seq', [(0, 1), (1, 0)])  4.01 us
    add x4, local copies, waits for them, and re-layouts, shards(): live = starts[:, :, None] + jnp.arange(PAGE, dtype=jnp.int32) < lengths[0]  3.4 us
  transfers between devices with their start and end apart: 17, of which 6 were waited for; matrix products, arithmetic and copies ran while one was open for 18% of the time, Pallas kernels for 5%

profile of v7, /device:TPU:1, one launch (start us, length us, event | category | flops | bytes accessed | tf_op | source)
XLA Modules:
  0.0 90.6 jit_solution(14651928631254733501)
XLA Ops:
  0.0 3.3 %shard_map.121 = bf16[16,144,512]{2,1,0:T(8,128)(2,1)} custom-call(s32[16]{0:T(128)} %bitcast.90, s32[16]{0:T(128)} %constant.40.clone.order, bf16[2,16,64,576]{3,2,1,0:T(8,128)(2,1)} %bitcast.76), custom_call_target="tpu_custom_call" | custom-call | bytes 5242880 | tf_op jit(solution)/shard_map/pallas_call | solution.py:83
  3.4 11.1 %all-to-all-start = ((bf16[16,144,512]{2,1,0:T(8,128)(2,1)}), bf16[16,144,512]{2,1,0:T(8,128)(2,1)S(1)}, u32[]{:S(2)}, u32[]{:S(2)}) async-start(bf16[16,144,512]{2,1,0:T(8,128)(2,1)} %shard_map.121), calls=%async_computation | async-start | bytes 4718592 | tf_op jit(solution)/shard_map/all_to_all | solution.py:319
  16.1 2.8 %collective-permute-start.1 = (bf16[4,32,128]{2,1,0:T(8,128)(2,1)S(1)}, bf16[4,32,128]{2,1,0:T(8,128)(2,1)S(1)}, u32[]{:S(2)}, u32[]{:S(2)}) collective-permute-start(bf16[4,32,128]{2,1,0:T(8,128)(2,1)S(1)} %get-tuple-element.26), channel_id=1, source_target_pairs={{0,2},{1,3},{2,0},{3,1},{4,6},{5,7},{6,4},{7,5},{8,10},{9,11},{10,... | collective-permute-start | bytes 98312 | tf_op jit(solution)/shard_map/ppermute | solution.py:307
  19.2 2.4 %collective-permute-start.2 = (bf16[4,32,128]{2,1,0:T(8,128)(2,1)S(1)}, bf16[4,32,128]{2,1,0:T(8,128)(2,1)S(1)}, u32[]{:S(2)}, u32[]{:S(2)}) collective-permute-start(bf16[4,32,128]{2,1,0:T(8,128)(2,1)S(1)} %get-tuple-element.28), channel_id=1, source_target_pairs={{0,3},{1,0},{2,1},{3,2},{4,7},{5,4},{6,5},{7,6},{8,11},{9,8},{10,9... | collective-permute-start | bytes 98312 | tf_op jit(solution)/shard_map/ppermute | solution.py:307
  24.6 1.3 %collective-permute-start.14 = (bf16[2,8,256,128]{3,2,1,0:T(8,128)(2,1)}, bf16[2,8,256,128]{3,2,1,0:T(8,128)(2,1)}, u32[]{:S(2)}, u32[]{:S(2)}) collective-permute-start(bf16[2,8,256,128]{3,2,1,0:T(8,128)(2,1)} %own.3), channel_id=1, source_target_pairs={{0,16},{16,0},{1,17},{17,1},{2,18},{18,2},{3,19},{19,3},{4,20},{20... | collective-permute-start | bytes 3145736 | tf_op jit(solution)/shard_map/ppermute | solution.py:325
  25.9 2.8 %collective-permute-start.5 = (bf16[4,32,128]{2,1,0:T(8,128)(2,1)S(1)}, bf16[4,32,128]{2,1,0:T(8,128)(2,1)S(1)}, u32[]{:S(2)}, u32[]{:S(2)}) collective-permute-start(bf16[4,32,128]{2,1,0:T(8,128)(2,1)S(1)} %get-tuple-element.22), channel_id=1, source_target_pairs={{0,12},{1,13},{2,14},{3,15},{4,0},{5,1},{6,2},{7,3},{8,4},{9,5},{1... | collective-permute-start | bytes 98312 | tf_op jit(solution)/shard_map/ppermute | solution.py:307
  30.4 2.9 %collective-permute-done.4 = bf16[4,32,128]{2,1,0:T(8,128)(2,1)S(1)} collective-permute-done((bf16[4,32,128]{2,1,0:T(8,128)(2,1)S(1)}, bf16[4,32,128]{2,1,0:T(8,128)(2,1)S(1)}, u32[]{:S(2)}, u32[]{:S(2)}) %collective-permute-start.4) | collective-permute-done | bytes 32800 | tf_op jit(solution)/shard_map/ppermute | solution.py:307
  33.7 2.5 %shard_map.119 = bf16[512,512]{1,0:T(8,128)(2,1)S(1)} custom-call(s32[19]{0:T(128)S(1)} %pad_add_fusion.1.where, bf16[512,128]{1,0:T(8,128)(2,1)S(1)} %bitcast.71, bf16[2,8,128,256]{3,2,1,0:T(8,128)(2,1)} %own.2, bf16[2,8,128,256]{3,2,1,0:T(8,128)(2,1)} %collective-permute-done.6.got), custom_call_target="tpu_custom_call" | custom-call | flops 536870912 | bytes 2097152 | tf_op jit(solution)/shard_map/pallas_call | solution.py:210
  36.2 0.8 fusion.7
  37.3 2.4 %collective-permute-start.9 = (bf16[4,32,512]{2,1,0:T(8,128)(2,1)}, bf16[4,32,512]{2,1,0:T(8,128)(2,1)}, u32[]{:S(2)}, u32[]{:S(2)}) collective-permute-start(bf16[4,32,512]{2,1,0:T(8,128)(2,1)} %get-tuple-element.20), channel_id=1, source_target_pairs={{0,3},{1,0},{2,1},{3,2},{4,7},{5,4},{6,5},{7,6},{8,11},{9,8},{10,9... | collective-permute-start | bytes 393224 | tf_op jit(solution)/shard_map/ppermute | solution.py:307
  39.7 1.3 %add_bitcast_fusion = s32[16,2]{0,1:T(2,128)} fusion(s32[2,16]{1,0:T(2,128)S(1)} %copy-done.9, pred[]{:T(512)S(6)} %eq.4, s32[2]{0:T(128)S(1)} %copy-done.15, s32[1,16]{1,0:T(1,128)} %bitcast.89, s32[1,16]{1,0:T(1,128)S(1)} %bitcast.87), kind=kLoop, calls=%fused_computation.31 | loop fusion | flops 128 | bytes 393 | tf_op jit(solution)/shard_map/add | solution.py:346
  41.0 1.3 %copy.20 = s32[16,2]{1,0:T(8,128)} copy(s32[16,2]{0,1:T(2,128)} %add_bitcast_fusion) | data formatting | bytes 256 | tf_op jit(solution)/shard_map/add | solution.py:346
  42.4 1.4 %add.46 = s32[16,2,64]{2,1,0:T(2,128)} broadcast(s32[16,2]{1,0:T(8,128)} %copy.20), dimensions={0,1} | broadcast | bytes 8320 | tf_op jit(solution)/shard_map/add | solution.py:347
  43.7 1.4 %add.47 = s32[16,128]{1,0:T(8,128)} reshape(s32[16,2,64]{2,1,0:T(2,128)} %add.46) | data formatting | bytes 16384 | tf_op jit(solution)/shard_map/add | solution.py:347
  45.1 1.2 %collective-permute-done.7 = bf16[4,32,512]{2,1,0:T(8,128)(2,1)} collective-permute-done((bf16[4,32,512]{2,1,0:T(8,128)(2,1)}, bf16[4,32,512]{2,1,0:T(8,128)(2,1)}, u32[]{:S(2)}, u32[]{:S(2)}) %collective-permute-start.7) | collective-permute-done | bytes 131104 | tf_op jit(solution)/shard_map/ppermute | solution.py:307
  46.3 1.2 %pad_maximum_fusion = bf16[4,4,32,512]{3,2,1,0:T(8,128)(2,1)S(1)} fusion(bf16[4,1,32,512]{3,2,1,0:T(8,128)(2,1)} %bitcast.23, bf16[4,1,32,512]{3,2,1,0:T(8,128)(2,1)} %bitcast.21, bf16[4,1,32,512]{3,2,1,0:T(8,128)(2,1)} %bitcast.19, bf16[4,1,32,512]{3,2,1,0:T(8,128)(2,1)} %get-tuple-element.17), kind=kLoop, calls=%fused_computation.9 | loop fusion | flops 786432 | bytes 1048576 | tf_op jit(solution)/shard_map/stack | solution.py:313
  47.5 0.8 fusion.6
  48.6 1.0 %collective-permute-start.11 = (bf16[4,32,512]{2,1,0:T(8,128)(2,1)}, bf16[4,32,512]{2,1,0:T(8,128)(2,1)}, u32[]{:S(2)}, u32[]{:S(2)}) collective-permute-start(bf16[4,32,512]{2,1,0:T(8,128)(2,1)} %get-tuple-element.15), channel_id=1, source_target_pairs={{0,8},{1,9},{2,10},{3,11},{4,12},{5,13},{6,14},{7,15},{8,0},{9,1},... | collective-permute-start | bytes 393224 | tf_op jit(solution)/shard_map/ppermute | solution.py:307
  49.6 0.8 collective-permute-start.10
  50.3 1.2 %fusion.5 = bf16[16,128]{1,0:T(8,128)(2,1)} fusion(s32[16,128]{1,0:T(8,128)S(1)} %copy-done.6, s32[]{:T(128)} %bitcast.69, s32[128]{0:T(128)} %add.49), kind=kLoop, calls=%fused_computation.27 | loop fusion | flops 6144 | bytes 12804 | tf_op jit(solution)/shard_map/convert_element_type | solution.py:353
  51.5 2.0 %gather_fusion = bf16[16,128]{1,0:T(8,128)(2,1)} fusion(bf16[16,128]{1,0:T(8,128)(2,1)} %fusion.5, s32[1024]{0:T(1024)} %pad_clamp_fusion), kind=kCustom, calls=%fused_computation | custom fusion | bytes 8256 | tf_op jit(solution)/shard_map/gather | solution.py:353
  53.5 1.5 %shard_map.120.weight = bf16[5,512,256]{2,1,0:T(8,128)(2,1)S(1)} custom-call(s32[19]{0:T(128)S(1)} %pad_add_fusion.1.where, bf16[2,8,256,128]{3,2,1,0:T(8,128)(2,1)S(1)} %copy-done.3, bf16[2,8,256,128]{3,2,1,0:T(8,128)(2,1)} %collective-permute-done.14.got), custom_call_target="tpu_custom_call" | custom-call | bytes 3145728 | tf_op jit(solution)/shard_map/pallas_call | solution.py:171
  55.0 1.1 %copy-done.1 = bf16[5,512,256]{2,1,0:T(8,128)(2,1)} copy-done((bf16[5,512,256]{2,1,0:T(8,128)(2,1)}, bf16[5,512,256]{2,1,0:T(8,128)(2,1)S(1)}, u32[]{:S(2)}) %copy-start.1) | copy-done | bytes 1310744
  56.1 1.8 %collective-permute-done.10 = bf16[4,32,512]{2,1,0:T(8,128)(2,1)} collective-permute-done((bf16[4,32,512]{2,1,0:T(8,128)(2,1)}, bf16[4,32,512]{2,1,0:T(8,128)(2,1)}, u32[]{:S(2)}, u32[]{:S(2)}) %collective-permute-start.10) | collective-permute-done | bytes 131104 | tf_op jit(solution)/shard_map/ppermute | solution.py:307
  57.9 1.1 %pad_maximum_fusion.1 = bf16[4,4,32,512]{3,2,1,0:T(8,128)(2,1)S(1)} fusion(bf16[1,4,32,512]{3,2,1,0:T(8,128)(2,1)} %bitcast.29, bf16[1,4,32,512]{3,2,1,0:T(8,128)(2,1)} %bitcast.27, bf16[1,4,32,512]{3,2,1,0:T(8,128)(2,1)} %bitcast.25, bf16[1,4,32,512]{3,2,1,0:T(8,128)(2,1)S(1)} %copy-done.4), kind=kLoop, calls=%fused_computation.10 | loop fusion | flops 786432 | bytes 1048576 | tf_op jit(solution)/shard_map/stack | solution.py:314
  59.2 7.2 %all-to-all-done.pages = bf16[16,144,512]{2,1,0:T(8,128)(2,1)S(1)} async-done(((bf16[16,144,512]{2,1,0:T(8,128)(2,1)}), bf16[16,144,512]{2,1,0:T(8,128)(2,1)S(1)}, u32[]{:S(2)}, u32[]{:S(2)}) %all-to-all-start) | async-done | bytes 2359328 | tf_op jit(solution)/shard_map/all_to_all | solution.py:319
  66.4 4.5 %shard_map.122 = bf16[16,32,512]{2,1,0:T(8,128)(2,1)S(1)} custom-call(s32[19]{0:T(128)S(1)} %pad_add_fusion.1.where, bf16[544,640]{1,0:T(8,128)(2,1)S(1)} %fusion.4.inputs, bf16[16,144,512]{2,1,0:T(8,128)(2,1)S(1)} %all-to-all-done.pages), custom_call_target="tpu_custom_call" | custom-call | flops 2281701376 | bytes 4194304 | tf_op jit(solution)/shard_map/pallas_call | solution.py:285
  70.9 15.1 %all_to_all.10 = bf16[16,32,512]{2,1,0:T(8,128)(2,1)S(1)} all-to-all(bf16[16,32,512]{2,1,0:T(8,128)(2,1)S(1)} %shard_map.122), channel_id=1, replica_groups={{2,13,11,3,12,0,4,7,5,14,10,6,9,8,1,15},{18,29,27,19,28,16,20,23,21,30,..., dimensions={0} | all-to-all | bytes 1048576 | tf_op jit(solution)/shard_map/all_to_all | solution.py:319
  86.0 0.7 shard_map.123
  86.7 2.1 %collective-permute-start.15 = (bf16[16,4,8,128]{3,2,1,0:T(8,128)(2,1)S(1)}, bf16[16,4,8,128]{3,2,1,0:T(8,128)(2,1)S(1)}, u32[]{:S(2)}, u32[]{:S(2)}) collective-permute-start(bf16[16,4,8,128]{3,2,1,0:T(8,128)(2,1)S(1)} %bitcast.73), channel_id=1, source_target_pairs={{0,16},{16,0},{1,17},{17,1},{2,18},{18,2},{3,19},{19,3},{4,20},{20... | collective-permute-start | bytes 393224 | tf_op jit(solution)/shard_map/ppermute | solution.py:325
  88.8 1.0 %collective-permute-done.15 = bf16[16,4,8,128]{3,2,1,0:T(8,128)(2,1)S(1)} collective-permute-done((bf16[16,4,8,128]{3,2,1,0:T(8,128)(2,1)S(1)}, bf16[16,4,8,128]{3,2,1,0:T(8,128)(2,1)S(1)}, u32[]{:S(2)}, u32[]{:S(2)}) %collective-permute-start.15) | collective-permute-done | bytes 131104 | tf_op jit(solution)/shard_map/ppermute | solution.py:325
  89.8 0.7 maximum_select_fusion
  (67 shorter events, 7.1 us)
Async XLA Ops:
  0.0 22.2 %copy-start = (bf16[2,1,4,576]{3,2,1,0:T(4,128)(2,1)S(1)}, bf16[2,1,4,576]{3,2,1,0:T(4,128)(2,1)}, u32[]{:S(2)}) copy-start(bf16[2,1,4,576]{3,2,1,0:T(4,128)(2,1)} %param.19) | copy-start | bytes 27652
  3.3 11.1 %copy-start.10 = (s32[1,1,16]{2,1,0:T(1,128)S(1)}, s32[1,1,16]{2,1,0:T(1,128)}, u32[]{:S(2)}) copy-start(s32[1,1,16]{2,1,0:T(1,128)} %param.17) | copy-start | bytes 196
  3.3 11.7 %copy-start.5 = (bf16[2,1,4,128,192]{3,4,2,1,0:T(8,128)(2,1)S(1)}, bf16[2,1,4,128,192]{3,4,2,1,0:T(8,128)(2,1)}, u32[]{:S(2)}) copy-start(bf16[2,1,4,128,192]{3,4,2,1,0:T(8,128)(2,1)} %param.12) | copy-start | bytes 1179652
  3.4 12.0 %copy-start.14 = (s32[16]{0:T(128)S(1)}, s32[16]{0:T(128)}, u32[]{:S(2)}) copy-start(s32[16]{0:T(128)} %constant.39.clone) | copy-start | bytes 196
  3.4 63.0 %all-to-all-start = ((bf16[16,144,512]{2,1,0:T(8,128)(2,1)}), bf16[16,144,512]{2,1,0:T(8,128)(2,1)S(1)}, u32[]{:S(2)}, u32[]{:S(2)}) async-start(bf16[16,144,512]{2,1,0:T(8,128)(2,1)} %shard_map.121), calls=%async_computation | async-start | bytes 4718592 | tf_op jit(solution)/shard_map/all_to_all | solution.py:319
  14.5 7.2 %copy-start.13 = (s32[16]{0:T(128)S(1)}, s32[16]{0:T(128)}, u32[]{:S(2)}) copy-start(s32[16]{0:T(128)} %constant.56) | copy-start | bytes 196
  14.5 14.6 %collective-permute-start.13 = (s32[16]{0:T(128)S(1)}, s32[16]{0:T(128)S(1)}, u32[]{:S(2)}, u32[]{:S(2)}) collective-permute-start(s32[16]{0:T(128)S(1)} %bitcast.85), channel_id=1, source_target_pairs={{0,16},{16,0},{1,17},{17,1},{2,18},{18,2},{3,19},{19,3},{4,20},{20... | collective-permute-start | bytes 200 | tf_op jit(solution)/shard_map/ppermute | solution.py:325
  15.0 18.7 %collective-permute-start.6 = (bf16[2,8,128,256]{3,2,1,0:T(8,128)(2,1)}, bf16[2,8,128,256]{3,2,1,0:T(8,128)(2,1)}, u32[]{:S(2)}, u32[]{:S(2)}) collective-permute-start(bf16[2,8,128,256]{3,2,1,0:T(8,128)(2,1)} %own.2), channel_id=1, source_target_pairs={{0,16},{16,0},{1,17},{17,1},{2,18},{18,2},{3,19},{19,3},{4,20},{20... | collective-permute-start | bytes 3145736 | tf_op jit(solution)/shard_map/ppermute | solution.py:325
  16.1 8.5 %collective-permute-start.1 = (bf16[4,32,128]{2,1,0:T(8,128)(2,1)S(1)}, bf16[4,32,128]{2,1,0:T(8,128)(2,1)S(1)}, u32[]{:S(2)}, u32[]{:S(2)}) collective-permute-start(bf16[4,32,128]{2,1,0:T(8,128)(2,1)S(1)} %get-tuple-element.26), channel_id=1, source_target_pairs={{0,2},{1,3},{2,0},{3,1},{4,6},{5,7},{6,4},{7,5},{8,10},{9,11},{10,... | collective-permute-start | bytes 98312 | tf_op jit(solution)/shard_map/ppermute | solution.py:307
  18.9 7.0 %collective-permute-start = (bf16[4,32,128]{2,1,0:T(8,128)(2,1)S(1)}, bf16[4,32,128]{2,1,0:T(8,128)(2,1)S(1)}, u32[]{:S(2)}, u32[]{:S(2)}) collective-permute-start(bf16[4,32,128]{2,1,0:T(8,128)(2,1)S(1)} %get-tuple-element.27), channel_id=1, source_target_pairs={{0,1},{1,2},{2,3},{3,0},{4,5},{5,6},{6,7},{7,4},{8,9},{9,10},{10,1... | collective-permute-start | bytes 98312 | tf_op jit(solution)/shard_map/ppermute | solution.py:307
  19.2 6.6 %collective-permute-start.2 = (bf16[4,32,128]{2,1,0:T(8,128)(2,1)S(1)}, bf16[4,32,128]{2,1,0:T(8,128)(2,1)S(1)}, u32[]{:S(2)}, u32[]{:S(2)}) collective-permute-start(bf16[4,32,128]{2,1,0:T(8,128)(2,1)S(1)} %get-tuple-element.28), channel_id=1, source_target_pairs={{0,3},{1,0},{2,1},{3,2},{4,7},{5,4},{6,5},{7,6},{8,11},{9,8},{10,9... | collective-permute-start | bytes 98312 | tf_op jit(solution)/shard_map/ppermute | solution.py:307
  24.6 28.9 %collective-permute-start.14 = (bf16[2,8,256,128]{3,2,1,0:T(8,128)(2,1)}, bf16[2,8,256,128]{3,2,1,0:T(8,128)(2,1)}, u32[]{:S(2)}, u32[]{:S(2)}) collective-permute-start(bf16[2,8,256,128]{3,2,1,0:T(8,128)(2,1)} %own.3), channel_id=1, source_target_pairs={{0,16},{16,0},{1,17},{17,1},{2,18},{18,2},{3,19},{19,3},{4,20},{20... | collective-permute-start | bytes 3145736 | tf_op jit(solution)/shard_map/ppermute | solution.py:325
  25.9 4.4 %collective-permute-start.5 = (bf16[4,32,128]{2,1,0:T(8,128)(2,1)S(1)}, bf16[4,32,128]{2,1,0:T(8,128)(2,1)S(1)}, u32[]{:S(2)}, u32[]{:S(2)}) collective-permute-start(bf16[4,32,128]{2,1,0:T(8,128)(2,1)S(1)} %get-tuple-element.22), channel_id=1, source_target_pairs={{0,12},{1,13},{2,14},{3,15},{4,0},{5,1},{6,2},{7,3},{8,4},{9,5},{1... | collective-permute-start | bytes 98312 | tf_op jit(solution)/shard_map/ppermute | solution.py:307
  28.7 4.6 %collective-permute-start.4 = (bf16[4,32,128]{2,1,0:T(8,128)(2,1)S(1)}, bf16[4,32,128]{2,1,0:T(8,128)(2,1)S(1)}, u32[]{:S(2)}, u32[]{:S(2)}) collective-permute-start(bf16[4,32,128]{2,1,0:T(8,128)(2,1)S(1)} %get-tuple-element.23), channel_id=1, source_target_pairs={{0,8},{1,9},{2,10},{3,11},{4,12},{5,13},{6,14},{7,15},{8,0},{9,1},... | collective-permute-start | bytes 98312 | tf_op jit(solution)/shard_map/ppermute | solution.py:307
  29.1 7.1 %copy-start.12 = (s32[16]{0:T(128)}, s32[16]{0:T(128)S(1)}, u32[]{:S(2)}) copy-start(s32[16]{0:T(128)S(1)} %collective-permute-done.13) | copy-start | bytes 196
  29.1 4.6 %collective-permute-start.3 = (bf16[4,32,128]{2,1,0:T(8,128)(2,1)S(1)}, bf16[4,32,128]{2,1,0:T(8,128)(2,1)S(1)}, u32[]{:S(2)}, u32[]{:S(2)}) collective-permute-start(bf16[4,32,128]{2,1,0:T(8,128)(2,1)S(1)} %get-tuple-element.24), channel_id=1, source_target_pairs={{0,4},{1,5},{2,6},{3,7},{4,8},{5,9},{6,10},{7,11},{8,12},{9,13},{1... | collective-permute-start | bytes 98312 | tf_op jit(solution)/shard_map/ppermute | solution.py:307
  33.7 6.0 %copy-start.9 = (s32[2,16]{1,0:T(2,128)S(1)}, s32[2,16]{1,0:T(2,128)}, u32[]{:S(2)}) copy-start(s32[2,16]{1,0:T(2,128)} %rev.3) | copy-start | bytes 388
  33.7 6.0 %copy-start.11 = (s32[1,1,16]{2,1,0:T(1,128)S(1)}, s32[1,1,16]{2,1,0:T(1,128)}, u32[]{:S(2)}) copy-start(s32[1,1,16]{2,1,0:T(1,128)} %param.17) | copy-start | bytes 196
  33.7 6.0 %copy-start.15 = (s32[2]{0:T(128)S(1)}, s32[2]{0:T(128)}, u32[]{:S(2)}) copy-start(s32[2]{0:T(128)} %iota_multiply_fusion) | copy-start | bytes 28
  36.2 17.3 %copy-start.3 = (bf16[2,8,256,128]{3,2,1,0:T(8,128)(2,1)S(1)}, bf16[2,8,256,128]{3,2,1,0:T(8,128)(2,1)}, u32[]{:S(2)}) copy-start(bf16[2,8,256,128]{3,2,1,0:T(8,128)(2,1)} %own.3) | copy-start | bytes 3145732
  37.0 8.1 %collective-permute-start.8 = (bf16[4,32,512]{2,1,0:T(8,128)(2,1)}, bf16[4,32,512]{2,1,0:T(8,128)(2,1)}, u32[]{:S(2)}, u32[]{:S(2)}) collective-permute-start(bf16[4,32,512]{2,1,0:T(8,128)(2,1)} %get-tuple-element.18), channel_id=1, source_target_pairs={{0,2},{1,3},{2,0},{3,1},{4,6},{5,7},{6,4},{7,5},{8,10},{9,11},{10,... | collective-permute-start | bytes 393224 | tf_op jit(solution)/shard_map/ppermute | solution.py:307
  37.0 9.3 %collective-permute-start.7 = (bf16[4,32,512]{2,1,0:T(8,128)(2,1)}, bf16[4,32,512]{2,1,0:T(8,128)(2,1)}, u32[]{:S(2)}, u32[]{:S(2)}) collective-permute-start(bf16[4,32,512]{2,1,0:T(8,128)(2,1)} %get-tuple-element.19), channel_id=1, source_target_pairs={{0,1},{1,2},{2,3},{3,0},{4,5},{5,6},{6,7},{7,4},{8,9},{9,10},{10,1... | collective-permute-start | bytes 393224 | tf_op jit(solution)/shard_map/ppermute | solution.py:307
  37.3 9.0 %collective-permute-start.9 = (bf16[4,32,512]{2,1,0:T(8,128)(2,1)}, bf16[4,32,512]{2,1,0:T(8,128)(2,1)}, u32[]{:S(2)}, u32[]{:S(2)}) collective-permute-start(bf16[4,32,512]{2,1,0:T(8,128)(2,1)} %get-tuple-element.20), channel_id=1, source_target_pairs={{0,3},{1,0},{2,1},{3,2},{4,7},{5,4},{6,5},{7,6},{8,11},{9,8},{10,9... | collective-permute-start | bytes 393224 | tf_op jit(solution)/shard_map/ppermute | solution.py:307
  45.1 5.2 %copy-start.6 = (s32[16,128]{1,0:T(8,128)S(1)}, s32[16,128]{1,0:T(8,128)}, u32[]{:S(2)}) copy-start(s32[16,128]{1,0:T(8,128)} %add.47) | copy-start | bytes 24580
  48.3 7.8 %collective-permute-start.12 = (bf16[4,32,512]{2,1,0:T(8,128)(2,1)}, bf16[4,32,512]{2,1,0:T(8,128)(2,1)}, u32[]{:S(2)}, u32[]{:S(2)}) collective-permute-start(bf16[4,32,512]{2,1,0:T(8,128)(2,1)} %get-tuple-element.14), channel_id=1, source_target_pairs={{0,12},{1,13},{2,14},{3,15},{4,0},{5,1},{6,2},{7,3},{8,4},{9,5},{1... | collective-permute-start | bytes 393224 | tf_op jit(solution)/shard_map/ppermute | solution.py:307
  48.6 7.5 %collective-permute-start.11 = (bf16[4,32,512]{2,1,0:T(8,128)(2,1)}, bf16[4,32,512]{2,1,0:T(8,128)(2,1)}, u32[]{:S(2)}, u32[]{:S(2)}) collective-permute-start(bf16[4,32,512]{2,1,0:T(8,128)(2,1)} %get-tuple-element.15), channel_id=1, source_target_pairs={{0,8},{1,9},{2,10},{3,11},{4,12},{5,13},{6,14},{7,15},{8,0},{9,1},... | collective-permute-start | bytes 393224 | tf_op jit(solution)/shard_map/ppermute | solution.py:307
  49.6 8.3 %collective-permute-start.10 = (bf16[4,32,512]{2,1,0:T(8,128)(2,1)}, bf16[4,32,512]{2,1,0:T(8,128)(2,1)}, u32[]{:S(2)}, u32[]{:S(2)}) collective-permute-start(bf16[4,32,512]{2,1,0:T(8,128)(2,1)} %get-tuple-element.16), channel_id=1, source_target_pairs={{0,4},{1,5},{2,6},{3,7},{4,8},{5,9},{6,10},{7,11},{8,12},{9,13},{1... | collective-permute-start | bytes 393224 | tf_op jit(solution)/shard_map/ppermute | solution.py:307
  53.5 4.4 %copy-start.4 = (bf16[1,4,32,512]{3,2,1,0:T(8,128)(2,1)S(1)}, bf16[1,4,32,512]{3,2,1,0:T(8,128)(2,1)}, u32[]{:S(2)}) copy-start(bf16[1,4,32,512]{3,2,1,0:T(8,128)(2,1)} %get-tuple-element.13) | copy-start | bytes 393220
  53.5 5.5 %copy-start.7 = (bf16[4,576]{1,0:T(4,128)(2,1)S(1)}, bf16[4,576]{1,0:T(4,128)(2,1)}, u32[]{:S(2)}) copy-start(bf16[4,576]{1,0:T(4,128)(2,1)} %dynamic-slice_bitcast_fusion) | copy-start | bytes 13828
  53.5 5.5 %copy-start.8 = (bf16[16,128]{1,0:T(8,128)(2,1)S(1)}, bf16[16,128]{1,0:T(8,128)(2,1)}, u32[]{:S(2)}) copy-start(bf16[16,128]{1,0:T(8,128)(2,1)} %gather_fusion) | copy-start | bytes 12292
  66.4 19.6 %copy-start.2 = (bf16[5,512,256]{2,1,0:T(8,128)(2,1)S(1)}, bf16[5,512,256]{2,1,0:T(8,128)(2,1)}, u32[]{:S(2)}) copy-start(bf16[5,512,256]{2,1,0:T(8,128)(2,1)} %copy-done.1) | copy-start | bytes 3932164
  86.7 3.1 %collective-permute-start.15 = (bf16[16,4,8,128]{3,2,1,0:T(8,128)(2,1)S(1)}, bf16[16,4,8,128]{3,2,1,0:T(8,128)(2,1)S(1)}, u32[]{:S(2)}, u32[]{:S(2)}) collective-permute-start(bf16[16,4,8,128]{3,2,1,0:T(8,128)(2,1)S(1)} %bitcast.73), channel_id=1, source_target_pairs={{0,16},{16,0},{1,17},{17,1},{2,18},{18,2},{3,19},{19,3},{4,20},{20... | collective-permute-start | bytes 393224 | tf_op jit(solution)/shard_map/ppermute | solution.py:325
  (1 other events, 1.1 us)
